TPU v7x, 32 devices: a whole 2x2x4 slice. The times are simulated.
32 devices in a mesh: blk: 8 (over z, x), rep: 4 (over y, core).
Axes of the slice: x: 2, y: 2, z: 4, core: 2. Of those that a mesh axis runs over, the one named last changes fastest.
Arguments:
- features: bfloat16 [8192, 256], P('blk'), may hold values from -6 to 6
- degree: int32 [8192], P('blk'), may hold values from 1 to 8
- order: int32 [8, 1024], P('blk'), may hold values from 0 to 1023, each once within a row
- tile_rows: int32 [8, 4, 48], P('blk', 'rep'), may hold values from 0 to 7
- tile_cols: int32 [8, 4, 48], P('blk', 'rep'), may hold values from 0 to 23
- tile_count: int32 [8, 4], P('blk', 'rep'), may hold values from 1 to 48, as said below
- tile_values: bfloat16 [8, 4, 48, 128, 128], P('blk', 'rep'), may hold values from -0.14941406 to 0.14941406
- w_self: bfloat16 [256, 256], replicated, may hold values from -0.375 to 0.375
- w_neigh: bfloat16 [256, 256], replicated, may hold values from -0.375 to 0.375
- out_grad: bfloat16 [8192, 256], P('blk'), may hold values from -6 to 6
Outputs:
- output: bfloat16 [8192, 256], P('blk')
- grad_features: bfloat16 [8192, 256], P('blk')
- grad_self: float32 [256, 256], replicated
- grad_neigh: float32 [256, 256], replicated
Inputs may be any that keep to these rules, and one draw needn't show every extreme that they name: `tile_count`: some group of some block has all 48 slots live in every draw.
All inputs are finite; a program needn't handle non-finite values.
Results may differ from a plain program's by a relative error of at most 0.0095.
Values may be sent and summed in bfloat16 or wider, within the bound.
No kernel may reach another device: no remote copies, remote signals or barrier semaphores. Data moves between devices by JAX's collectives and lax.ppermute only.
A program may use at most 64 MiB of HBM per device.

v0:
```python
import jax
import jax.numpy as jnp
from jax import lax
from jax.sharding import PartitionSpec as P


def padded(x, sides, width):
    for axis, dim in sides:
        peers, length = (lax.axis_size(axis), x.shape[dim])
        up = [(i, (i + 1) % peers) for i in range(peers)]
        down = [(j, i) for i, j in up]
        last = lax.slice_in_dim(x, length - width, length, axis=dim)
        leading = lax.slice_in_dim(x, 0, width, axis=dim)
        before = lax.ppermute(last, axis, up)
        after = lax.ppermute(leading, axis, down)
        x = jnp.concatenate([before, x, after], axis=dim)
    return x


def from_behind(value, axis, steps):
    count = lax.axis_size(axis)
    pairs = [(source, (source + steps) % count) for source in range(count)]
    return lax.ppermute(value, axis, pairs)


def silu_pair(h):
    sig = jax.nn.sigmoid(h)
    return (h * sig, sig * (1.0 + h * (1.0 - sig)))


def dense_rows(x_rows, agg_rows, g_rows, scale_rows, w_self, w_neigh):
    agg_b = (agg_rows * scale_rows[:, None]).astype(jnp.bfloat16)
    h = jnp.dot(x_rows, w_self, preferred_element_type=jnp.float32) + jnp.dot(
        agg_b, w_neigh, preferred_element_type=jnp.float32
    )
    act, slope = silu_pair(h)
    gp = (g_rows.astype(jnp.float32) * slope).astype(jnp.bfloat16)
    term_self = jnp.einsum("nf,ng->fg", x_rows, gp, preferred_element_type=jnp.float32)
    term_neigh = jnp.einsum("nf,ng->fg", agg_b, gp, preferred_element_type=jnp.float32)
    s_rows = (
        jnp.einsum("ng,fg->nf", gp, w_neigh, preferred_element_type=jnp.float32)
        * scale_rows[:, None]
    ).astype(jnp.bfloat16)
    dself = jnp.einsum("ng,fg->nf", gp, w_self, preferred_element_type=jnp.float32)
    return (act.astype(jnp.bfloat16), s_rows, dself, term_self, term_neigh)


def shards(
    features,
    degree,
    order,
    tile_rows,
    tile_cols,
    tile_count,
    tile_values,
    w_self,
    w_neigh,
    out_grad,
):
    rows_blk, width = features.shape
    row_tiles = rows_blk // 128
    order_v = order[0]
    inverse = jnp.argsort(order_v)
    feats = features[order_v]
    grads = out_grad[order_v]
    scale = 1.0 / degree[order_v].astype(jnp.float32)
    rows_i = tile_rows[0, 0]
    cols_i = tile_cols[0, 0]
    values = tile_values[0, 0]
    slots = rows_i.shape[0]
    live = (jnp.arange(slots, dtype=jnp.int32) < tile_count[0, 0]).astype(jnp.float32)
    share = rows_blk // lax.axis_size("rep")
    start = lax.axis_index("rep") * share
    window = padded(feats, (("blk", 0),), rows_blk)
    pick = window.reshape(3 * row_tiles, 128, width)[cols_i]
    prod = jnp.einsum("tab,tbf->taf", values, pick, preferred_element_type=jnp.float32)
    partial_value = (
        jnp.zeros((row_tiles, 128, width), jnp.float32).at[rows_i].add(prod * live[:, None, None])
    )
    partial_value = partial_value.reshape(rows_blk, width)
    agg_full = lax.psum(partial_value, "rep")
    out_perm, sback, dself, term_self, term_neigh = dense_rows(
        feats, agg_full, grads, scale, w_self, w_neigh
    )
    grad_self, grad_neigh = lax.psum((term_self, term_neigh), "blk")
    dself_rows = lax.dynamic_slice_in_dim(dself, start, share, 0)
    back_pick = sback.reshape(row_tiles, 128, width)[rows_i]
    back = jnp.einsum("tab,taf->tbf", values, back_pick, preferred_element_type=jnp.float32)
    pieces = (
        jnp.zeros((3 * row_tiles, 128, width), jnp.float32)
        .at[cols_i]
        .add(back * live[:, None, None])
    )
    pieces = pieces.reshape(3, rows_blk, width)
    from_upper = from_behind(pieces[0].astype(jnp.bfloat16), "blk", -1).astype(jnp.float32)
    from_lower = from_behind(pieces[2].astype(jnp.bfloat16), "blk", 1).astype(jnp.float32)
    returned = pieces[1] + from_upper + from_lower
    returned_rows = lax.psum_scatter(
        returned.astype(jnp.bfloat16), "rep", scatter_dimension=0, tiled=True
    ).astype(jnp.float32)
    grad_rows = (dself_rows + returned_rows).astype(jnp.bfloat16)
    grad_perm = lax.all_gather(grad_rows, "rep", axis=0, tiled=True)
    return (out_perm[inverse], grad_perm[inverse], grad_self, grad_neigh)


def solution(mesh):
    return jax.shard_map(
        shards,
        mesh=mesh,
        in_specs=(
            P("blk", None),
            P("blk"),
            P("blk", None),
            P("blk", "rep", None),
            P("blk", "rep", None),
            P("blk", "rep"),
            P("blk", "rep", None, None, None),
            P(),
            P(),
            P("blk", None),
        ),
        out_specs=(P("blk", None), P("blk", None), P(), P()),
        check_vma=False,
    )
```

profile of v0, /device:TPU:0, one launch (start us, length us, event | category | flops | bytes accessed | tf_op | source)
XLA Modules:
  0.0 274.6 jit_solution(13237964644846056235)
XLA Ops:
  8.1 4.6 %gather_fusion = bf16[1024,256]{1,0:T(8,128)(2,1)S(1)} fusion(bf16[1024,256]{1,0:T(8,128)(2,1)} %param.10, s32[1024]{0:T(1024)S(1)} %broadcast_clamp_fusion), kind=kCustom, calls=%fused_computation | custom fusion | bytes 1052672 | tf_op jit(solution)/shard_map/gather | solution.py:64
  12.6 3.0 %collective-permute-start = (bf16[1024,256]{1,0:T(8,128)(2,1)S(1)}, bf16[1024,256]{1,0:T(8,128)(2,1)S(1)}, u32[]{:S(2)}, u32[]{:S(2)}) collective-permute-start(bf16[1024,256]{1,0:T(8,128)(2,1)S(1)} %gather_fusion), channel_id=1, source_target_pairs={{0,4},{4,8},{8,12},{12,16},{16,20},{20,24},{24,28},{28,0},{1,5},{5... | collective-permute-start | bytes 1572872 | tf_op jit(solution)/shard_map/ppermute | solution.py:14
  15.6 3.1 %collective-permute-start.1 = (bf16[1024,256]{1,0:T(8,128)(2,1)S(1)}, bf16[1024,256]{1,0:T(8,128)(2,1)S(1)}, u32[]{:S(2)}, u32[]{:S(2)}) collective-permute-start(bf16[1024,256]{1,0:T(8,128)(2,1)S(1)} %gather_fusion), channel_id=1, source_target_pairs={{4,0},{8,4},{12,8},{16,12},{20,16},{24,20},{28,24},{0,28},{5,1},{9... | collective-permute-start | bytes 1572872 | tf_op jit(solution)/shard_map/ppermute | solution.py:15
  19.5 18.6 %collective-permute-done = bf16[1024,256]{1,0:T(8,128)(2,1)S(1)} collective-permute-done((bf16[1024,256]{1,0:T(8,128)(2,1)S(1)}, bf16[1024,256]{1,0:T(8,128)(2,1)S(1)}, u32[]{:S(2)}, u32[]{:S(2)}) %collective-permute-start) | collective-permute-done | bytes 524320 | tf_op jit(solution)/shard_map/ppermute | solution.py:14
  41.4 2.6 gather_fusion.1
  44.0 5.9 %multiply_bitcast_fusion.1 = f32[48,128,256]{1,2,0:T(8,128)} fusion(f32[48]{0:T(128)S(1)} %compare_convert_fusion, bf16[48,128,256]{2,1,0:T(8,128)(2,1)} %gather_fusion.1, bf16[1,1,48,128,128]{4,3,2,1,0:T(8,128)(2,1)S(1)} %copy-done), kind=kOutput, calls=%fused_computation.10 | convolution fusion | flops 404226048 | bytes 11010240 | tf_op jit(solution)/shard_map/tab,tbf->taf/dot_general | solution.py:76
  49.9 6.6 %copy.17 = f32[48,128,256]{2,1,0:T(8,128)} copy(f32[48,128,256]{1,2,0:T(8,128)} %multiply_bitcast_fusion.1) | data formatting | bytes 12582912 | tf_op jit(solution)/shard_map/mul | solution.py:78
  56.5 9.4 %scatter_fusion = f32[8,128,256]{2,1,0:T(8,128)S(1)} fusion(f32[8,128,256]{2,1,0:T(8,128)S(1)} %broadcast_in_dim.6, s32[48]{0:T(128)S(1)} %fusion.6, f32[48,128,256]{2,1,0:T(8,128)} %copy.17), kind=kCustom, calls=%fused_computation.7 | custom fusion | flops 1572864 | bytes 18874560 | tf_op jit(solution)/shard_map/scatter-add | solution.py:78
  67.0 4.5 %gather_fusion.2 = s32[1024]{0:T(1024)S(1)} fusion(s32[1024]{0:T(1024)S(1)} %copy-done.1, s32[1024]{0:T(1024)S(1)} %broadcast_clamp_fusion), kind=kCustom, calls=%fused_computation.2 | custom fusion | bytes 12288 | tf_op jit(solution)/shard_map/gather | solution.py:66
  71.6 5.0 %gather_fusion.4 = bf16[1024,256]{1,0:T(8,128)(2,1)} fusion(bf16[1024,256]{1,0:T(8,128)(2,1)S(1)} %copy-done.3, s32[1024]{0:T(1024)S(1)} %broadcast_clamp_fusion), kind=kCustom, calls=%fused_computation.4 | custom fusion | bytes 1052672 | tf_op jit(solution)/shard_map/gather | solution.py:65
  77.9 25.3 %all-reduce.4.cloned.1.call-done = f32[1024,256]{1,0:T(8,128)} async-done(((f32[1024,256]{1,0:T(8,128)}), f32[1024,256]{1,0:T(8,128)}) %all-reduce.4.cloned.1.call-update) | async-done | bytes 1048592 | tf_op jit(solution)/shard_map/psum | solution.py:81
  105.9 2.5 gather_fusion.5
  108.4 5.9 %multiply_bitcast_fusion = f32[48,128,256]{1,2,0:T(8,128)} fusion(f32[48]{0:T(128)S(1)} %compare_convert_fusion, bf16[48,128,256]{2,1,0:T(8,128)(2,1)} %gather_fusion.5, bf16[1,1,48,128,128]{4,3,2,1,0:T(8,128)(2,1)S(1)} %copy-done), kind=kOutput, calls=%fused_computation.9 | convolution fusion | flops 404226048 | bytes 11010240 | tf_op jit(solution)/shard_map/tab,taf->tbf/dot_general | solution.py:88
  114.3 6.6 %copy.19 = f32[48,128,256]{2,1,0:T(8,128)} copy(f32[48,128,256]{1,2,0:T(8,128)} %multiply_bitcast_fusion) | data formatting | bytes 12582912 | tf_op jit(solution)/shard_map/mul | solution.py:92
  123.0 14.5 %scatter_fusion.1 = f32[24,128,256]{2,1,0:T(8,128)} fusion(f32[24,128,256]{2,1,0:T(8,128)} %broadcast_in_dim.8, s32[48]{0:T(128)S(1)} %fusion.7, f32[48,128,256]{2,1,0:T(8,128)} %copy.19), kind=kCustom, calls=%fused_computation.8 | custom fusion | flops 1572864 | bytes 18874560 | tf_op jit(solution)/shard_map/scatter-add | solution.py:92
  139.6 4.3 %collective-permute-start.2 = (bf16[1024,256]{1,0:T(8,128)(2,1)S(1)}, bf16[1024,256]{1,0:T(8,128)(2,1)S(1)}, u32[]{:S(2)}, u32[]{:S(2)}) collective-permute-start(bf16[1024,256]{1,0:T(8,128)(2,1)S(1)} %bitcast.50), channel_id=1, source_target_pairs={{0,28},{4,0},{8,4},{12,8},{16,12},{20,16},{24,20},{28,24},{1,29},{... | collective-permute-start | bytes 1572872 | tf_op jit(solution)/shard_map/ppermute | solution.py:23
  145.3 19.1 %collective-permute-done.2 = bf16[1024,256]{1,0:T(8,128)(2,1)S(1)} collective-permute-done((bf16[1024,256]{1,0:T(8,128)(2,1)S(1)}, bf16[1024,256]{1,0:T(8,128)(2,1)S(1)}, u32[]{:S(2)}, u32[]{:S(2)}) %collective-permute-start.2) | collective-permute-done | bytes 524320 | tf_op jit(solution)/shard_map/ppermute | solution.py:23
  165.6 4.4 %sort.17 = (s32[1024]{0:T(1024)}, s32[1024]{0:T(1024)S(1)}) sort(s32[1024]{0:T(1024)S(1)} %bitcast.51, s32[1024]{0:T(1024)S(1)} %iota.10), dimensions={0}, to_apply=%region_2.3 | sort | flops 10240 | bytes 16384 | tf_op jit(solution)/shard_map/jit(argsort)/sort | solution.py:63
  171.0 2.5 fusion.8
  174.9 5.0 %gather_fusion.3 = bf16[1024,256]{1,0:T(8,128)(2,1)} fusion(bf16[1024,256]{1,0:T(8,128)(2,1)S(1)} %get-tuple-element.11, s32[1024]{0:T(1024)S(1)} %fusion.5), kind=kCustom, calls=%fused_computation.3 | custom fusion | bytes 1052672 | tf_op jit(solution)/shard_map/gather | solution.py:103
  179.8 8.2 %reduce-scatter.2.cloned.1.call-done = bf16[256,256]{1,0:T(8,128)(2,1)} async-done(((bf16[1024,256]{1,0:T(8,128)(2,1)}), bf16[256,256]{1,0:T(8,128)(2,1)}) %reduce-scatter.2.cloned.1.call-update) | async-done | bytes 131088 | tf_op jit(solution)/shard_map/reduce_scatter | solution.py:98
  189.1 6.8 %all_gather.3 = bf16[1024,256]{1,0:T(8,128)(2,1)S(1)} all-gather(bf16[256,256]{1,0:T(8,128)(2,1)S(1)} %add_convert_fusion), channel_id=1, replica_groups=mesh['blk'=8,'rep'=4] {'rep'}, dimensions={0}, use_global_device_ids=true | all-gather | bytes 655360 | tf_op jit(solution)/shard_map/all_gather | solution.py:102
  195.9 5.0 %gather_fusion.6 = bf16[1024,256]{1,0:T(8,128)(2,1)} fusion(bf16[1024,256]{1,0:T(8,128)(2,1)S(1)} %all_gather.3, s32[1024]{0:T(1024)S(1)} %fusion.5), kind=kCustom, calls=%fused_computation.6 | custom fusion | bytes 1052672 | tf_op jit(solution)/shard_map/gather | solution.py:103
  200.9 63.9 %all-reduce.6.cloned.1.call-done = (f32[256,256]{1,0:T(8,128)}, f32[256,256]{1,0:T(8,128)}) async-done(((f32[256,256]{1,0:T(8,128)}, f32[256,256]{1,0:T(8,128)}), (f32[256,256]{1,0:T(8,128)}, f32[256,256]{1,0:T(8,128)})) %all-reduce.6.cloned.1.call-update) | async-done | bytes 524304 | tf_op jit(solution)/shard_map/psum | solution.py:85
  (58 shorter events, 22.9 us)
Async XLA Ops:
  7.2 36.8 %copy-start = (bf16[1,1,48,128,128]{4,3,2,1,0:T(8,128)(2,1)S(1)}, bf16[1,1,48,128,128]{4,3,2,1,0:T(8,128)(2,1)}, u32[]{:S(2)}) copy-start(bf16[1,1,48,128,128]{4,3,2,1,0:T(8,128)(2,1)} %param.16) | copy-start | bytes 4718596
  7.2 12.2 %copy-start.10 = (s32[1,1,48]{2,1,0:T(1,128)S(1)}, s32[1,1,48]{2,1,0:T(1,128)}, u32[]{:S(2)}) copy-start(s32[1,1,48]{2,1,0:T(1,128)} %param.14) | copy-start | bytes 580
  7.2 12.3 %copy-start.11 = (s32[1,1,48]{2,1,0:T(1,128)S(1)}, s32[1,1,48]{2,1,0:T(1,128)}, u32[]{:S(2)}) copy-start(s32[1,1,48]{2,1,0:T(1,128)} %param.13) | copy-start | bytes 580
  7.2 96.0 %all-reduce.4.cloned.1.call-start = ((), (), s32[]{:S(2)}) async-start(), calls=%async_computation.1 | async-start | bytes 2097152 | tf_op jit(solution)/shard_map/psum | solution.py:81
  12.6 25.4 %copy-start.4 = (bf16[1024,256]{1,0:T(8,128)(2,1)}, bf16[1024,256]{1,0:T(8,128)(2,1)S(1)}, u32[]{:S(2)}) copy-start(bf16[1024,256]{1,0:T(8,128)(2,1)S(1)} %gather_fusion) | copy-start | bytes 1572868
  12.6 25.4 %collective-permute-start = (bf16[1024,256]{1,0:T(8,128)(2,1)S(1)}, bf16[1024,256]{1,0:T(8,128)(2,1)S(1)}, u32[]{:S(2)}, u32[]{:S(2)}) collective-permute-start(bf16[1024,256]{1,0:T(8,128)(2,1)S(1)} %gather_fusion), channel_id=1, source_target_pairs={{0,4},{4,8},{8,12},{12,16},{16,20},{20,24},{24,28},{28,0},{1,5},{5... | collective-permute-start | bytes 1572872 | tf_op jit(solution)/shard_map/ppermute | solution.py:14
  15.6 24.6 %collective-permute-start.1 = (bf16[1024,256]{1,0:T(8,128)(2,1)S(1)}, bf16[1024,256]{1,0:T(8,128)(2,1)S(1)}, u32[]{:S(2)}, u32[]{:S(2)}) collective-permute-start(bf16[1024,256]{1,0:T(8,128)(2,1)S(1)} %gather_fusion), channel_id=1, source_target_pairs={{4,0},{8,4},{12,8},{16,12},{20,16},{24,20},{28,24},{0,28},{5,1},{9... | collective-permute-start | bytes 1572872 | tf_op jit(solution)/shard_map/ppermute | solution.py:15
  65.9 1.0 copy-start.2
  66.0 1.1 copy-start.1
  66.0 5.6 %copy-start.3 = (bf16[1024,256]{1,0:T(8,128)(2,1)S(1)}, bf16[1024,256]{1,0:T(8,128)(2,1)}, u32[]{:S(2)}) copy-start(bf16[1024,256]{1,0:T(8,128)(2,1)} %param.19) | copy-start | bytes 1572868
  66.9 121.1 %reduce-scatter.2.cloned.1.call-start = ((), (), s32[]{:S(2)}) async-start(), calls=%async_computation.2 | async-start | bytes 655360 | tf_op jit(solution)/shard_map/reduce_scatter | solution.py:98
  71.6 5.0 %copy-start.5 = (bf16[1024,256]{1,0:T(8,128)(2,1)S(1)}, bf16[1024,256]{1,0:T(8,128)(2,1)}, u32[]{:S(2)}) copy-start(bf16[1024,256]{1,0:T(8,128)(2,1)} %copy-done.4) | copy-start | bytes 1572868
  71.6 5.0 %copy-start.7 = (bf16[256,256]{1,0:T(8,128)(2,1)S(1)}, bf16[256,256]{1,0:T(8,128)(2,1)}, u32[]{:S(2)}) copy-start(bf16[256,256]{1,0:T(8,128)(2,1)} %param.17) | copy-start | bytes 393220
  71.6 31.6 %copy-start.8 = (bf16[256,256]{1,0:T(8,128)(2,1)S(1)}, bf16[256,256]{1,0:T(8,128)(2,1)}, u32[]{:S(2)}) copy-start(bf16[256,256]{1,0:T(8,128)(2,1)} %param.18) | copy-start | bytes 393220
  139.6 26.0 %copy-start.9 = (s32[1,1024]{1,0:T(1,128)S(1)}, s32[1,1024]{1,0:T(1,128)}, u32[]{:S(2)}) copy-start(s32[1,1024]{1,0:T(1,128)} %param.12) | copy-start | bytes 12292
  139.6 30.4 %copy-start.6 = (bf16[1024,256]{1,0:T(8,128)(2,1)S(1)}, bf16[1024,256]{1,0:T(8,128)(2,1)}, u32[]{:S(2)}) copy-start(bf16[1024,256]{1,0:T(8,128)(2,1)} %copy-done.4) | copy-start | bytes 1572868
  139.6 24.8 %collective-permute-start.2 = (bf16[1024,256]{1,0:T(8,128)(2,1)S(1)}, bf16[1024,256]{1,0:T(8,128)(2,1)S(1)}, u32[]{:S(2)}, u32[]{:S(2)}) collective-permute-start(bf16[1024,256]{1,0:T(8,128)(2,1)S(1)} %bitcast.50), channel_id=1, source_target_pairs={{0,28},{4,0},{8,4},{12,8},{16,12},{20,16},{24,20},{28,24},{1,29},{... | collective-permute-start | bytes 1572872 | tf_op jit(solution)/shard_map/ppermute | solution.py:23
  144.0 20.4 %collective-permute-start.3 = (bf16[1024,256]{1,0:T(8,128)(2,1)S(1)}, bf16[1024,256]{1,0:T(8,128)(2,1)S(1)}, u32[]{:S(2)}, u32[]{:S(2)}) collective-permute-start(bf16[1024,256]{1,0:T(8,128)(2,1)S(1)} %bitcast.49), channel_id=1, source_target_pairs={{0,4},{4,8},{8,12},{12,16},{16,20},{20,24},{24,28},{28,0},{1,5},{5... | collective-permute-start | bytes 1572872 | tf_op jit(solution)/shard_map/ppermute | solution.py:23
  165.4 99.4 %all-reduce.6.cloned.1.call-start = ((), (), s32[]{:S(2)}) async-start(), calls=%async_computation.3 | async-start | bytes 1048576 | tf_op jit(solution)/shard_map/psum | solution.py:85
Sparse Core Ops, SparseCore 0:
  67.1 36.0 all-reduce.3
  165.5 22.5 reduce-scatter.1
  192.1 72.6 all-reduce.5
where the time goes:
time: 275 us
  waiting for transfers between devices  137 us (50%)
  local copies, waits for them, and re-layouts  50.1 us (18%)
  other arithmetic  34.3 us (12%)
  matrix products  20.7 us (8%)
  between operations  14.7 us (5%)
  starting transfers between devices  10.7 us (4%)
  blocking collectives  6.77 us (2%)
    psum x1, waiting for transfers between devices, shards(): grad_self, grad_neigh = lax.psum((term_self, term_neigh), 'blk')  63.9 us
    psum x1, waiting for transfers between devices, shards(): agg_full = lax.psum(partial_value, 'rep')  25.3 us
    ppermute x2, waiting for transfers between devices, from_behind(): return lax.ppermute(value, axis, pairs)  19.1 us
    ppermute x1, waiting for transfers between devices, padded(): before = lax.ppermute(last, axis, up)  18.6 us
    scatter-add x1, other arithmetic, shards(): pieces = jnp.zeros((3 * row_tiles, 128, width), jnp.float32).at[cols_i].a...  14.5 us
    gather x2, local copies, waits for them, and re-layouts, shards(): return (out_perm[inverse], grad_perm[inverse], grad_self, grad_neigh)  9.95 us
    scatter-add x1, other arithmetic, shards(): jnp.zeros((row_tiles, 128, width), jnp.float32).at[rows_i]  9.41 us
    reduce_scatter x1, waiting for transfers between devices, shards(): lax.psum_scatter(returned.astype(jnp.bfloat16), 'rep', scatter_dimension=...  8.22 us
  transfers between devices with their start and end apart: 7, of which 6 were waited for; matrix products, arithmetic and copies ran while one was open for 12% of the time, Pallas kernels for 0%

commit v1 on v0

v1 whole, which is shorter than its diff:
```python
import jax
import jax.numpy as jnp
from jax import lax
from jax.experimental import pallas as pl
from jax.experimental.pallas import tpu as pltpu
from jax.sharding import PartitionSpec as P

BF = jnp.bfloat16
F32 = jnp.float32
T = 128


def mm(a, b):
    return jnp.dot(a, b, preferred_element_type=F32)


def mm_nt(a, b):
    return lax.dot_general(a, b, (((1,), (1,)), ((), ())), preferred_element_type=F32)


def mm_tn(a, b):
    return lax.dot_general(a, b, (((0,), (0,)), ((), ())), preferred_element_type=F32)


def core_of():
    return lax.rem(lax.axis_index("rep"), 2)


def y_of():
    return lax.div(lax.axis_index("rep"), 2)


def onehot_rows(order_row, count):
    column = jnp.transpose(jnp.broadcast_to(order_row, (T, T)))
    lane = lax.broadcasted_iota(jnp.int32, (T, T), 1).astype(F32)
    cuts = [
        jnp.where(column == lane + float(j * T), 1.0, 0.0).astype(BF) for j in range(count // T)
    ]
    return jnp.concatenate(cuts, axis=1)


def onehot_inverse(order_row, first, rows):
    wide = (rows, order_row.shape[1])
    at = lax.broadcasted_iota(jnp.int32, wide, 0) + first
    return jnp.where(jnp.broadcast_to(order_row, wide) == at, 1.0, 0.0).astype(BF)


def half_lanes(index):
    return pl.ds(pl.multiple_of(index * T, T), T)


def reorder_kernel(order_ref, x_ref, out_ref):
    c = core_of()
    rows = out_ref.shape[0]
    x = x_ref[:, half_lanes(c)]
    for i in range(rows // T):
        hot = onehot_rows(order_ref[i : i + 1, :].astype(F32), rows)
        out_ref[i * T : (i + 1) * T, :] = mm(hot, x).astype(BF)


def prepare_kernel(order_ref, degree_ref, x_ref, g_ref, w_ref, xh_ref, gh_ref, hs_ref, sc_ref, sr_ref):
    c = core_of()
    rows = x_ref.shape[0]
    tiles = rows // T // 2
    deg = jnp.broadcast_to(degree_ref[...].astype(F32), (8, rows)).astype(BF)
    for i in range(tiles):
        hot = onehot_rows(order_ref[pl.ds(c * tiles + i, 1), :].astype(F32), rows)
        here = slice(i * T, (i + 1) * T)
        xt = mm(hot, x_ref[...]).astype(BF)
        xh_ref[here, :] = xt
        gh_ref[here, :] = mm(hot, g_ref[...]).astype(BF)
        hs_ref[here, :] = mm(xt, w_ref[...])
        scale = 1.0 / mm_nt(deg, hot)
        sr_ref[:, here] = scale
        sc_ref[here, :] = jnp.transpose(jnp.broadcast_to(scale[0:1, :], (T, T)))


def gather_kernel(
    ra_ref, ca_ref, na_ref, rb_ref, cb_ref, nb_ref,
    prev_ref, own_ref, next_ref, va_ref, vb_ref,
    here_ref, other_ref, win, acc,
):
    c = core_of()
    rows = own_ref.shape[0]
    tiles = rows // T
    half = rows // 2
    win[0:rows, :] = prev_ref[...]
    win[rows : 2 * rows, :] = own_ref[...]
    win[2 * rows : 3 * rows, :] = next_ref[...]
    acc[...] = jnp.zeros_like(acc)
    slots = va_ref.shape[0]
    for t in range(slots):
        for r_ref, c_ref, n_ref, v_ref in (
            (ra_ref, ca_ref, na_ref, va_ref),
            (rb_ref, cb_ref, nb_ref, vb_ref),
        ):
            r = jnp.where(t < n_ref[0], r_ref[t], tiles)
            prod = mm(v_ref[t], win[pl.ds(pl.multiple_of(c_ref[t] * T, T), T), :])
            acc[r] += prod
    for i in range(tiles // 2):
        here_ref[i * T : (i + 1) * T, :] = acc[c * (tiles // 2) + i].astype(BF)
        other_ref[i * T : (i + 1) * T, :] = acc[(1 - c) * (tiles // 2) + i].astype(BF)


def dense_kernel(
    own_ref, core_ref, y_ref, diag_ref, hs_ref, gh_ref, sc_ref, sr_ref, wn_ref,
    act_ref, gp_ref, agg_ref, keep_ref, send_ref,
):
    c = core_of()
    scale = sc_ref[...]
    agg_ref[:, half_lanes(c)] = (
        (own_ref[...].astype(F32) + y_ref[...].astype(F32)) * scale
    ).astype(BF)
    agg_ref[:, half_lanes(1 - c)] = (
        (core_ref[...].astype(F32) + diag_ref[...].astype(F32)) * scale
    ).astype(BF)
    h = hs_ref[...] + mm(agg_ref[...], wn_ref[...])
    sig = jax.nn.sigmoid(h)
    act_ref[...] = (h * sig).astype(BF)
    gp = (gh_ref[...].astype(F32) * (sig * (1.0 + h * (1.0 - sig)))).astype(BF)
    gp_ref[...] = gp
    row = sr_ref[0:1, :]
    keep_ref[...] = (mm_nt(wn_ref[pl.ds(pl.multiple_of(c * T, T), T), :], gp) * row).astype(BF)
    send_ref[...] = (mm_nt(wn_ref[pl.ds(pl.multiple_of((1 - c) * T, T), T), :], gp) * row).astype(BF)


def terms_kernel(xh_ref, agg_ref, gp_ref, ws_ref, keep_ref, send_ref, mine_ref, theirs_ref):
    c, y = core_of(), y_of()
    gp = gp_ref[...]
    keep_ref[...] = mm_nt(ws_ref[pl.ds(pl.multiple_of(c * T, T), T), :], gp)
    send_ref[...] = mm_nt(ws_ref[pl.ds(pl.multiple_of((1 - c) * T, T), T), :], gp)
    mine_ref[...] = jnp.zeros_like(mine_ref)

    def term(lhs_ref):
        mine_ref[...] = mm_tn(lhs_ref[:, half_lanes(c)], gp)
        theirs_ref[...] = mm_tn(lhs_ref[:, half_lanes(1 - c)], gp)

    @pl.when(y == 0)
    def _():
        term(xh_ref)

    @pl.when(y != 0)
    def _():
        term(agg_ref)


def scatter_kernel(
    ra_ref, ca_ref, na_ref, rb_ref, cb_ref, nb_ref,
    mine_ref, theirs_ref, va_ref, vb_ref,
    own_ref, ownx_ref, dn_ref, dnx_ref, up_ref, upx_ref, src, acc,
):
    c, y = core_of(), y_of()
    half = mine_ref.shape[1]
    tiles = 2 * half // T
    ht = tiles // 2
    for i in range(ht):
        cut = slice(i * T, (i + 1) * T)
        src[c * ht + i] = mine_ref[:, cut]
        src[(1 - c) * ht + i] = theirs_ref[:, cut]
    acc[...] = jnp.zeros_like(acc)
    slots = va_ref.shape[0]
    for t in range(slots):
        for r_ref, c_ref, n_ref, v_ref in (
            (ra_ref, ca_ref, na_ref, va_ref),
            (rb_ref, cb_ref, nb_ref, vb_ref),
        ):
            col = jnp.where(t < n_ref[0], c_ref[t], 3 * tiles)
            acc[col] += mm(src[r_ref[t]], v_ref[t])
    for i in range(ht):
        same, cross = y * ht + i, (1 - y) * ht + i
        own_ref[i] = acc[tiles + same]
        ownx_ref[i] = acc[tiles + cross].astype(BF)
        dn_ref[i] = acc[same].astype(BF)
        dnx_ref[i] = acc[cross].astype(BF)
        up_ref[i] = acc[2 * tiles + same].astype(BF)
        upx_ref[i] = acc[2 * tiles + cross].astype(BF)


def total_kernel(own_ref, y_ref, a_ref, b_ref, d_ref, e_ref, keep_ref, recv_ref, out_ref):
    c, y = core_of(), y_of()
    local = jnp.broadcast_to(c == y, keep_ref.shape)
    dself = jnp.where(local, keep_ref[...], recv_ref[...])
    for i in range(own_ref.shape[0]):
        total = own_ref[i] + dself[:, i * T : (i + 1) * T] + y_ref[i].astype(F32)
        total = total + a_ref[i].astype(F32) + b_ref[i].astype(F32)
        total = total + d_ref[i].astype(F32) + e_ref[i].astype(F32)
        out_ref[i] = total.astype(BF)


def restore_kernel(order_ref, own_ref, core_ref, y_ref, diag_ref, out_ref, full):
    c, y = core_of(), y_of()
    rows = out_ref.shape[0]
    ht = own_ref.shape[0]
    for i in range(ht):
        for ref, fh, rh in (
            (own_ref, c, y),
            (core_ref, 1 - c, y),
            (y_ref, c, 1 - y),
            (diag_ref, 1 - c, 1 - y),
        ):
            at = pl.ds(pl.multiple_of((rh * ht + i) * T, T), T)
            full[pl.ds(pl.multiple_of(fh * T, T), T), at] = ref[i]
    for j in range(rows // 256):
        hot = onehot_inverse(order_ref[...], j * 256, 256)
        out_ref[j * 256 : (j + 1) * 256, :] = mm_nt(hot, full[...]).astype(BF)


def output_kernel(order_ref, own_ref, core_ref, out_ref, full):
    c = core_of()
    half = own_ref.shape[0]
    rows = 2 * half
    full[pl.ds(pl.multiple_of(c * half, half), half), :] = own_ref[...]
    full[pl.ds(pl.multiple_of((1 - c) * half, half), half), :] = core_ref[...]
    for j in range(rows // 256):
        hot = onehot_inverse(order_ref[...], j * 256, 256)
        out_ref[j * 256 : (j + 1) * 256, :] = mm(hot, full[...]).astype(BF)


def call(kernel, outs, ins, smem=0, scratch=(), name=None, flops=0, moved=0):
    specs = [pl.BlockSpec(memory_space=pltpu.SMEM)] * smem
    specs += [pl.BlockSpec(memory_space=pltpu.VMEM)] * (len(ins) - smem)
    shapes = [jax.ShapeDtypeStruct(s, d) for s, d in outs]
    out_specs = [pl.BlockSpec(memory_space=pltpu.VMEM)] * len(outs)
    single = len(outs) == 1
    return pl.pallas_call(
        kernel,
        out_shape=shapes[0] if single else shapes,
        in_specs=specs,
        out_specs=out_specs[0] if single else out_specs,
        scratch_shapes=list(scratch),
        name=name,
        cost_estimate=pl.CostEstimate(flops=flops, bytes_accessed=moved, transcendentals=0),
    )(*ins)


def shards(
    features, degree, order, tile_rows, tile_cols, tile_count, tile_values, w_self, w_neigh, out_grad
):
    rows, width = features.shape
    half = rows // 2
    tiles = rows // T
    ht = tiles // 2
    blocks = lax.axis_size("blk")
    reps = lax.axis_size("rep")
    assert reps == 4 and width == 2 * T

    def hop(x, blk_step, rep_mask):
        pairs = [
            (b * reps + r, ((b + blk_step) % blocks) * reps + (r ^ rep_mask))
            for b in range(blocks)
            for r in range(reps)
        ]
        return lax.ppermute(x, ("blk", "rep"), pairs)

    def swap_core(x):
        return lax.ppermute(x, "rep", [(r, r ^ 1) for r in range(reps)])

    def swap_y(x):
        return lax.ppermute(x, "rep", [(r, r ^ 2) for r in range(reps)])

    def swap_diag(x):
        return lax.ppermute(x, "rep", [(r, r ^ 3) for r in range(reps)])

    order8 = order.reshape(tiles, T)
    deg = degree.reshape(1, rows)
    ra, ca, na = tile_rows[0, 0], tile_cols[0, 0], tile_count[0]
    va = tile_values[0, 0]

    feats_c = call(reorder_kernel, [((rows, T), BF)], [order8, features], name="reorder")
    prev = hop(feats_c, 1, 0)
    nxt = hop(feats_c, -1, 0)
    vb = swap_core(va)
    rb, cb, nb = swap_core(ra), swap_core(ca), swap_core(na)
    xh, gh, hs, sc, sr = call(
        prepare_kernel,
        [((half, width), BF), ((half, width), BF), ((half, width), F32), ((half, T), F32), ((8, half), F32)],
        [order8, deg, features, out_grad, w_self],
        name="prepare",
    )
    index = [ra, ca, na, rb, cb, nb]
    here, other = call(
        gather_kernel,
        [((half, T), BF), ((half, T), BF)],
        index + [prev, feats_c, nxt, va, vb],
        smem=6,
        scratch=[pltpu.VMEM((3 * rows, T), BF), pltpu.VMEM((tiles + 1, T, T), F32)],
        name="gather",
    )
    from_y = swap_y(here)
    from_diag = swap_diag(other)
    from_core = swap_core(other)
    act, gp, agg, s_keep, s_send = call(
        dense_kernel,
        [((half, width), BF), ((half, width), BF), ((half, width), BF), ((T, half), BF), ((T, half), BF)],
        [here, from_core, from_y, from_diag, hs, gh, sc, sr, w_neigh],
        name="dense",
    )
    s_other = swap_core(s_send)
    d_keep, d_send, g_mine, g_theirs = call(
        terms_kernel,
        [((T, half), F32), ((T, half), F32), ((T, width), F32), ((T, width), F32)],
        [xh, agg, gp, w_self],
        name="terms",
    )
    piece = (ht, T, T)
    own, ownx, dn, dnx, up, upx = call(
        scatter_kernel,
        [(piece, F32)] + [(piece, BF)] * 5,
        index + [s_keep, s_other, va, vb],
        smem=6,
        scratch=[pltpu.VMEM((tiles, T, T), BF), pltpu.VMEM((3 * tiles + 1, T, T), F32)],
        name="scatter",
    )
    r_a = hop(dn, -1, 0)
    r_b = hop(dnx, -1, 2)
    r_d = hop(up, 1, 0)
    r_e = hop(upx, 1, 2)
    r_y = swap_y(ownx)
    d_recv = swap_core(d_send)
    act_other = swap_core(act)
    output = call(
        output_kernel,
        [((rows, width), BF)],
        [order, act, act_other],
        scratch=[pltpu.VMEM((rows, width), BF)],
        name="output",
    )
    grad_piece = call(
        total_kernel, [(piece, BF)], [own, r_y, r_a, r_b, r_d, r_e, d_keep, d_recv], name="total"
    )
    g = g_mine + swap_core(g_theirs)
    step = 1
    while step < blocks:
        g = g + lax.ppermute(g, "blk", [(b, b ^ step) for b in range(blocks)])
        step *= 2
    g = g.astype(BF)
    p_y = swap_y(grad_piece)
    p_core = swap_core(grad_piece)
    p_diag = swap_core(p_y)
    grad_features = call(
        restore_kernel,
        [((rows, width), BF)],
        [order, grad_piece, p_core, p_y, p_diag],
        scratch=[pltpu.VMEM((width, rows), BF)],
        name="restore",
    )
    weights = lax.all_gather(g, "rep", axis=0, tiled=True).astype(F32)
    return output, grad_features, weights[:width], weights[width:]


def solution(mesh):
    return jax.shard_map(
        shards,
        mesh=mesh,
        in_specs=(
            P("blk", None),
            P("blk"),
            P("blk", None),
            P("blk", "rep", None),
            P("blk", "rep", None),
            P("blk", "rep"),
            P("blk", "rep", None, None, None),
            P(),
            P(),
            P("blk", None),
        ),
        out_specs=(P("blk", None), P("blk", None), P(), P()),
        check_vma=False,
    )
```

time: 275 us -> 87.4 us (0.32)
  waiting for transfers between devices: 137 us -> 18.5 us
  local copies, waits for them, and re-layouts: 50.1 us -> 6.16 us
  other arithmetic: 34.3 us -> 0.07 us
  Pallas kernels: 0 us -> 28.8 us
  matrix products: 20.7 us -> 0 us
  starting transfers between devices: 10.7 us -> 26.4 us
  between operations: 14.7 us -> 1.45 us
    psum x2 -> x0, waiting for transfers between devices: 89.2 us -> none  [the longest x1 63.9 us: shards(): grad_self, grad_neigh = lax.psum((term_self, term_neigh), 'blk')]
    gather x7 -> x0, local copies, waits for them, and re-layouts: 29.1 us -> none  [the longest x2 9.95 us: shards(): return (out_perm[inverse], grad_perm[inverse], grad_self, grad_neigh)]
    pallas_call x0 -> x9, Pallas kernels: none -> 28.8 us  [call(): pl.pallas_call(kernel, out_shape=shapes[0] if single else shapes, in_spec...]
    scatter-add x2 -> x0, other arithmetic: 23.9 us -> none  [the longest x1 14.5 us: shards(): pieces = jnp.zeros((3 * row_tiles, 128, width), jnp.float32).at[cols_i].a...]
    ppermute x4 -> x24, waiting for transfers between devices: 39.9 us -> 18.5 us  [the longest x6 9.8 us: hop(): return lax.ppermute(x, ('blk', 'rep'), pairs)]
    dot_general x8 -> x0, matrix products: 20.7 us -> none  [the longest x1 5.92 us: shards(): jnp.einsum('tab,tbf->taf', values, pick, preferred_element_type=jnp.float32)]
    ppermute x4 -> x24, starting transfers between devices: 10.4 us -> 26.4 us  [the longest x6 11.4 us: hop(): return lax.ppermute(x, ('blk', 'rep'), pairs)]
    mul x2 -> x0, local copies, waits for them, and re-layouts: 13.1 us -> none  [the longest x1 6.58 us: shards(): back * live[:, None, None]]
  transfers between devices with their start and end apart: 7 -> 24, of which waited for: 6 -> 8; matrix products, arithmetic and copies ran while one was open for 12% -> 1% of each run, Pallas kernels for 0% -> 21%
where the time goes in v1:
time: 87.4 us; the launch traced here: 87.1 us
  Pallas kernels  28.8 us (33%)
  starting transfers between devices  26.4 us (30%)
  waiting for transfers between devices  18.5 us (21%)
  local copies, waits for them, and re-layouts  6.16 us (7%)
  blocking collectives  5.79 us (7%)
  between operations  1.45 us (2%)
    pallas_call x9, Pallas kernels, call(): pl.pallas_call(kernel, out_shape=shapes[0] if single else shapes, in_spec...  28.8 us
    ppermute x6, starting transfers between devices, hop(): return lax.ppermute(x, ('blk', 'rep'), pairs)  11.4 us
    ppermute x6, waiting for transfers between devices, hop(): return lax.ppermute(x, ('blk', 'rep'), pairs)  9.8 us
    ppermute x3, starting transfers between devices, shards(): g = g + lax.ppermute(g, 'blk', [(b, b ^ step) for b in range(blocks)])  7.47 us
    all_gather x1, blocking collectives, shards(): weights = lax.all_gather(g, 'rep', axis=0, tiled=True).astype(F32)  5.79 us
    ppermute x3, waiting for transfers between devices, shards(): g = g + lax.ppermute(g, 'blk', [(b, b ^ step) for b in range(blocks)])  5.55 us
    unnamed x42, local copies, waits for them, and re-layouts  5.33 us
    ppermute x3, starting transfers between devices, swap_y(): return lax.ppermute(x, 'rep', [(r, r ^ 2) for r in range(reps)])  4.23 us
  transfers between devices with their start and end apart: 24, of which 8 were waited for; matrix products, arithmetic and copies ran while one was open for 1% of the time, Pallas kernels for 21%

profile of v1, /device:TPU:0, one launch (start us, length us, event | category | flops | bytes accessed | tf_op | source)
XLA Modules:
  0.0 87.1 jit_solution(17555826588388518526)
XLA Ops:
  1.1 2.7 %reorder.1.own_ref = bf16[1024,128]{1,0:T(8,128)(2,1)} custom-call(s32[8,128]{1,0:T(8,128)} %bitcast.11, bf16[1024,256]{1,0:T(8,128)(2,1)} %x_ref.3), custom_call_target="tpu_custom_call" | custom-call | tf_op jit(solution)/shard_map/reorder/pallas_call | solution.py:225
  3.8 5.5 %collective-permute-start.4 = (bf16[1024,128]{1,0:T(8,128)(2,1)}, bf16[1024,128]{1,0:T(8,128)(2,1)S(1)}, u32[]{:S(2)}, u32[]{:S(2)}) collective-permute-start(bf16[1024,128]{1,0:T(8,128)(2,1)} %reorder.1.own_ref), channel_id=1, source_target_pairs={{0,28},{1,29},{2,30},{3,31},{4,0},{5,1},{6,2},{7,3},{8,4},{9,5},{1... | collective-permute-start | bytes 786440 | tf_op jit(solution)/shard_map/ppermute | solution.py:253
  12.1 3.8 %collective-permute-done.4.next_ref = bf16[1024,128]{1,0:T(8,128)(2,1)S(1)} collective-permute-done((bf16[1024,128]{1,0:T(8,128)(2,1)}, bf16[1024,128]{1,0:T(8,128)(2,1)S(1)}, u32[]{:S(2)}, u32[]{:S(2)}) %collective-permute-start.4) | collective-permute-done | bytes 262176 | tf_op jit(solution)/shard_map/ppermute | solution.py:253
  15.9 4.8 %collective-permute-done.3.prev_ref = bf16[1024,128]{1,0:T(8,128)(2,1)S(1)} collective-permute-done((bf16[1024,128]{1,0:T(8,128)(2,1)}, bf16[1024,128]{1,0:T(8,128)(2,1)S(1)}, u32[]{:S(2)}, u32[]{:S(2)}) %collective-permute-start.3) | collective-permute-done | bytes 262176 | tf_op jit(solution)/shard_map/ppermute | solution.py:253
  22.0 4.7 %gather.1 = (bf16[512,128]{1,0:T(8,128)(2,1)}, bf16[512,128]{1,0:T(8,128)(2,1)}) custom-call(s32[48]{0:T(128)} %bitcast.15, s32[48]{0:T(128)} %bitcast.18, s32[1]{0:T(128)} %bitcast.6.na_ref, s32[48]{0:T(128)} %copy-done.19, s32[48]{0:T(128)} %copy-done.20, s32[1]{0:T(128)} %collective-permute-done.2.nb_ref, bf16[1024,128]{1,0:T(8,128)(2,1)} %copy-done.2, ...), custom_call_target="tpu_custom_call" | custom-call | tf_op jit(solution)/shard_map/gather/pallas_call | solution.py:225
  26.7 1.5 %collective-permute-start.7 = (bf16[512,128]{1,0:T(8,128)(2,1)}, bf16[512,128]{1,0:T(8,128)(2,1)S(1)}, u32[]{:S(2)}, u32[]{:S(2)}) collective-permute-start(bf16[512,128]{1,0:T(8,128)(2,1)} %get-tuple-element.26.own_ref), channel_id=1, source_target_pairs={{0,2},{1,3},{2,0},{3,1},{4,6},{5,7},{6,4},{7,5},{8,10},{9,11},{10,... | collective-permute-start | bytes 393224 | tf_op jit(solution)/shard_map/ppermute | solution.py:259
  28.8 3.5 %prepare.1 = (bf16[512,256]{1,0:T(8,128)(2,1)}, bf16[512,256]{1,0:T(8,128)(2,1)}, f32[512,256]{1,0:T(8,128)}, f32[512,128]{1,0:T(8,128)}, f32[8,512]{1,0:T(8,128)}) custom-call(s32[8,128]{1,0:T(8,128)} %bitcast.12, s32[1,1024]{1,0:T(1,128)} %bitcast.13, bf16[1024,256]{1,0:T(8,128)(2,1)} %x_ref.3, bf16[1024,256]{1,0:T(8,128)(2,1)} %g_ref.1, ...), custom_call_target="tpu_custom_call" | custom-call | tf_op jit(solution)/shard_map/prepare/pallas_call | solution.py:225
  32.3 1.8 %collective-permute-done.8.diag_ref = bf16[512,128]{1,0:T(8,128)(2,1)S(1)} collective-permute-done((bf16[512,128]{1,0:T(8,128)(2,1)}, bf16[512,128]{1,0:T(8,128)(2,1)S(1)}, u32[]{:S(2)}, u32[]{:S(2)}) %collective-permute-start.8) | collective-permute-done | bytes 131104 | tf_op jit(solution)/shard_map/ppermute | solution.py:262
  34.9 2.9 %dense.1 = (bf16[512,256]{1,0:T(8,128)(2,1)}, bf16[512,256]{1,0:T(8,128)(2,1)}, bf16[512,256]{1,0:T(8,128)(2,1)}, bf16[128,512]{1,0:T(8,128)(2,1)}, bf16[128,512]{1,0:T(8,128)(2,1)}) custom-call(bf16[512,128]{1,0:T(8,128)(2,1)} %get-tuple-element.26.own_ref, bf16[512,128]{1,0:T(8,128)(2,1)} %copy-done.17, bf16[512,128]{1,0:T(8,128)(2,1)} %copy-done.14, ...), custom_call_target="tpu_custom_call" | custom-call | tf_op jit(solution)/shard_map/dense/pallas_call | solution.py:225
  38.0 2.6 %terms.1 = (f32[128,512]{1,0:T(8,128)}, f32[128,512]{1,0:T(8,128)}, f32[128,256]{1,0:T(8,128)}, f32[128,256]{1,0:T(8,128)}) custom-call(bf16[512,256]{1,0:T(8,128)(2,1)} %get-tuple-element.41.xh_ref, bf16[512,256]{1,0:T(8,128)(2,1)} %get-tuple-element.42.agg_ref, bf16[512,256]{1,0:T(8,128)(2,1)} %get-tuple-element.43.gp_ref, bf16[256,256]{1,0:T(8,128)(2,1)} %ws_ref.1), custom_call_target="tpu_custom_call" | custom-call | tf_op jit(solution)/shard_map/terms/pallas_call | solution.py:225
  41.8 4.9 %scatter.1 = (f32[4,128,128]{2,1,0:T(8,128)}, bf16[4,128,128]{2,1,0:T(8,128)(2,1)}, bf16[4,128,128]{2,1,0:T(8,128)(2,1)}, bf16[4,128,128]{2,1,0:T(8,128)(2,1)}, ...) custom-call(s32[48]{0:T(128)} %bitcast.16, s32[48]{0:T(128)} %bitcast.19, s32[1]{0:T(128)} %bitcast.7.na_ref, ...), custom_call_target="tpu_custom_call" | custom-call | tf_op jit(solution)/shard_map/scatter/pallas_call | solution.py:225
  46.7 1.5 %collective-permute-start.11 = (bf16[4,128,128]{2,1,0:T(8,128)(2,1)}, bf16[4,128,128]{2,1,0:T(8,128)(2,1)S(1)}, u32[]{:S(2)}, u32[]{:S(2)}) collective-permute-start(bf16[4,128,128]{2,1,0:T(8,128)(2,1)} %get-tuple-element.36), channel_id=1, source_target_pairs={{0,2},{1,3},{2,0},{3,1},{4,6},{5,7},{6,4},{7,5},{8,10},{9,11},{10,... | collective-permute-start | bytes 393224 | tf_op jit(solution)/shard_map/ppermute | solution.py:259
  48.2 1.7 %collective-permute-start.21 = (f32[128,256]{1,0:T(8,128)S(1)}, f32[128,256]{1,0:T(8,128)S(1)}, u32[]{:S(2)}, u32[]{:S(2)}) collective-permute-start(f32[128,256]{1,0:T(8,128)S(1)} %add.12), channel_id=1, source_target_pairs={{0,4},{4,0},{8,12},{12,8},{16,20},{20,16},{24,28},{28,24},{1,5},{5... | collective-permute-start | bytes 393224 | tf_op jit(solution)/shard_map/ppermute | solution.py:334
  49.9 2.4 %collective-permute-start.12 = (bf16[4,128,128]{2,1,0:T(8,128)(2,1)}, bf16[4,128,128]{2,1,0:T(8,128)(2,1)S(1)}, u32[]{:S(2)}, u32[]{:S(2)}) collective-permute-start(bf16[4,128,128]{2,1,0:T(8,128)(2,1)} %get-tuple-element.37), channel_id=1, source_target_pairs={{0,28},{1,29},{2,30},{3,31},{4,0},{5,1},{6,2},{7,3},{8,4},{9,5},{1... | collective-permute-start | bytes 393224 | tf_op jit(solution)/shard_map/ppermute | solution.py:253
  52.3 1.4 %collective-permute-start.13 = (bf16[4,128,128]{2,1,0:T(8,128)(2,1)}, bf16[4,128,128]{2,1,0:T(8,128)(2,1)S(1)}, u32[]{:S(2)}, u32[]{:S(2)}) collective-permute-start(bf16[4,128,128]{2,1,0:T(8,128)(2,1)} %get-tuple-element.38), channel_id=1, source_target_pairs={{0,30},{1,31},{2,28},{3,29},{4,2},{5,3},{6,0},{7,1},{8,6},{9,7},{1... | collective-permute-start | bytes 393224 | tf_op jit(solution)/shard_map/ppermute | solution.py:253
  54.3 1.5 %collective-permute-start.15 = (bf16[4,128,128]{2,1,0:T(8,128)(2,1)}, bf16[4,128,128]{2,1,0:T(8,128)(2,1)S(1)}, u32[]{:S(2)}, u32[]{:S(2)}) collective-permute-start(bf16[4,128,128]{2,1,0:T(8,128)(2,1)} %get-tuple-element.40), channel_id=1, source_target_pairs={{0,6},{1,7},{2,4},{3,5},{4,10},{5,11},{6,8},{7,9},{8,14},{9,15},{1... | collective-permute-start | bytes 393224 | tf_op jit(solution)/shard_map/ppermute | solution.py:253
  55.8 3.7 %collective-permute-done.21 = f32[128,256]{1,0:T(8,128)S(1)} collective-permute-done((f32[128,256]{1,0:T(8,128)S(1)}, f32[128,256]{1,0:T(8,128)S(1)}, u32[]{:S(2)}, u32[]{:S(2)}) %collective-permute-start.21) | collective-permute-done | bytes 131104 | tf_op jit(solution)/shard_map/ppermute | solution.py:334
  59.5 4.2 %collective-permute-start.22 = (f32[128,256]{1,0:T(8,128)S(1)}, f32[128,256]{1,0:T(8,128)S(1)}, u32[]{:S(2)}, u32[]{:S(2)}) collective-permute-start(f32[128,256]{1,0:T(8,128)S(1)} %add.13), channel_id=1, source_target_pairs={{0,8},{4,12},{8,0},{12,4},{16,24},{20,28},{24,16},{28,20},{1,9},{5... | collective-permute-start | bytes 393224 | tf_op jit(solution)/shard_map/ppermute | solution.py:334
  65.6 2.2 %total.1.own_ref = bf16[4,128,128]{2,1,0:T(8,128)(2,1)} custom-call(f32[4,128,128]{2,1,0:T(8,128)} %get-tuple-element.35.own_ref, bf16[4,128,128]{2,1,0:T(8,128)(2,1)} %copy-done.6, bf16[4,128,128]{2,1,0:T(8,128)(2,1)} %copy-done.7, bf16[4,128,128]{2,1,0:T(8,128)(2,1)} %copy-done.8, bf16[4,128,128]{2,1,0:T(8,128)(2,1)} %copy-done.9, ...), custom_call_target="tpu_custom_call" | custom-call | tf_op jit(solution)/shard_map/total/pallas_call | solution.py:225
  69.1 1.6 %collective-permute-start.23 = (f32[128,256]{1,0:T(8,128)S(1)}, f32[128,256]{1,0:T(8,128)S(1)}, u32[]{:S(2)}, u32[]{:S(2)}) collective-permute-start(f32[128,256]{1,0:T(8,128)S(1)} %add.14), channel_id=1, source_target_pairs={{0,16},{4,20},{8,24},{12,28},{16,0},{20,4},{24,8},{28,12},{1,17},{... | collective-permute-start | bytes 393224 | tf_op jit(solution)/shard_map/ppermute | solution.py:334
  71.4 2.6 %output.1 = bf16[1024,256]{1,0:T(8,128)(2,1)} custom-call(s32[1,1024]{1,0:T(1,128)} %order_ref.3, bf16[512,256]{1,0:T(8,128)(2,1)} %get-tuple-element.32.own_ref, bf16[512,256]{1,0:T(8,128)(2,1)} %copy-done.5), custom_call_target="tpu_custom_call" | custom-call | tf_op jit(solution)/shard_map/output/pallas_call | solution.py:225
  74.5 1.9 %collective-permute-done.23 = f32[128,256]{1,0:T(8,128)S(1)} collective-permute-done((f32[128,256]{1,0:T(8,128)S(1)}, f32[128,256]{1,0:T(8,128)S(1)}, u32[]{:S(2)}, u32[]{:S(2)}) %collective-permute-start.23) | collective-permute-done | bytes 131104 | tf_op jit(solution)/shard_map/ppermute | solution.py:334
  76.4 5.8 %all_gather.3 = bf16[512,256]{1,0:T(8,128)(2,1)S(1)} all-gather(bf16[128,256]{1,0:T(8,128)(2,1)S(1)} %add_convert_fusion), channel_id=1, replica_groups=mesh['blk'=8,'rep'=4] {'rep'}, dimensions={0}, use_global_device_ids=true | all-gather | bytes 327680 | tf_op jit(solution)/shard_map/all_gather | solution.py:347
  84.3 2.8 %restore.1 = bf16[1024,256]{1,0:T(8,128)(2,1)} custom-call(s32[1,1024]{1,0:T(1,128)} %order_ref.3, bf16[4,128,128]{2,1,0:T(8,128)(2,1)} %total.1.own_ref, bf16[4,128,128]{2,1,0:T(8,128)(2,1)} %copy-done.16, bf16[4,128,128]{2,1,0:T(8,128)(2,1)} %copy-done.13, bf16[4,128,128]{2,1,0:T(8,128)(2,1)} %copy-done.18), custom_call_target="tpu_custom_call" | custom-call | tf_op jit(solution)/shard_map/restore/pallas_call | solution.py:225
  (81 shorter events, 13.8 us)
Async XLA Ops:
  0.6 20.1 %collective-permute-start.5 = (bf16[48,128,128]{2,1,0:T(8,128)(2,1)}, bf16[48,128,128]{2,1,0:T(8,128)(2,1)S(1)}, u32[]{:S(2)}, u32[]{:S(2)}) collective-permute-start(bf16[48,128,128]{2,1,0:T(8,128)(2,1)} %bitcast.8), channel_id=1, source_target_pairs={{0,1},{1,0},{2,3},{3,2},{4,5},{5,4},{6,7},{7,6},{8,9},{9,8},{10,11... | collective-permute-start | bytes 4718600 | tf_op jit(solution)/shard_map/ppermute | solution.py:256
  3.8 12.1 %collective-permute-start.4 = (bf16[1024,128]{1,0:T(8,128)(2,1)}, bf16[1024,128]{1,0:T(8,128)(2,1)S(1)}, u32[]{:S(2)}, u32[]{:S(2)}) collective-permute-start(bf16[1024,128]{1,0:T(8,128)(2,1)} %reorder.1.own_ref), channel_id=1, source_target_pairs={{0,28},{1,29},{2,30},{3,31},{4,0},{5,1},{6,2},{7,3},{8,4},{9,5},{1... | collective-permute-start | bytes 786440 | tf_op jit(solution)/shard_map/ppermute | solution.py:253
  9.4 11.3 %collective-permute-start.3 = (bf16[1024,128]{1,0:T(8,128)(2,1)}, bf16[1024,128]{1,0:T(8,128)(2,1)S(1)}, u32[]{:S(2)}, u32[]{:S(2)}) collective-permute-start(bf16[1024,128]{1,0:T(8,128)(2,1)} %reorder.1.own_ref), channel_id=1, source_target_pairs={{0,4},{1,5},{2,6},{3,7},{4,8},{5,9},{6,10},{7,11},{8,12},{9,13},{1... | collective-permute-start | bytes 786440 | tf_op jit(solution)/shard_map/ppermute | solution.py:253
  9.4 2.4 %collective-permute-start = (s32[48]{0:T(128)}, s32[48]{0:T(128)S(1)}, u32[]{:S(2)}, u32[]{:S(2)}) collective-permute-start(s32[48]{0:T(128)} %bitcast.14), channel_id=1, source_target_pairs={{0,1},{1,0},{2,3},{3,2},{4,5},{5,4},{6,7},{7,6},{8,9},{9,8},{10,11... | collective-permute-start | bytes 584 | tf_op jit(solution)/shard_map/ppermute | solution.py:256
  9.6 1.3 %collective-permute-start.2 = (s32[1]{0:T(128)}, s32[1]{0:T(128)}, u32[]{:S(2)}, u32[]{:S(2)}) collective-permute-start(s32[1]{0:T(128)} %bitcast.2), channel_id=1, source_target_pairs={{0,1},{1,0},{2,3},{3,2},{4,5},{5,4},{6,7},{7,6},{8,9},{9,8},{10,11... | collective-permute-start | bytes 20 | tf_op jit(solution)/shard_map/ppermute | solution.py:256
  10.8 1.3 %collective-permute-start.1 = (s32[48]{0:T(128)}, s32[48]{0:T(128)S(1)}, u32[]{:S(2)}, u32[]{:S(2)}) collective-permute-start(s32[48]{0:T(128)} %bitcast.17), channel_id=1, source_target_pairs={{0,1},{1,0},{2,3},{3,2},{4,5},{5,4},{6,7},{7,6},{8,9},{9,8},{10,11... | collective-permute-start | bytes 584 | tf_op jit(solution)/shard_map/ppermute | solution.py:256
  26.7 5.7 %collective-permute-start.7 = (bf16[512,128]{1,0:T(8,128)(2,1)}, bf16[512,128]{1,0:T(8,128)(2,1)S(1)}, u32[]{:S(2)}, u32[]{:S(2)}) collective-permute-start(bf16[512,128]{1,0:T(8,128)(2,1)} %get-tuple-element.26.own_ref), channel_id=1, source_target_pairs={{0,2},{1,3},{2,0},{3,1},{4,6},{5,7},{6,4},{7,5},{8,10},{9,11},{10,... | collective-permute-start | bytes 393224 | tf_op jit(solution)/shard_map/ppermute | solution.py:259
  28.2 6.0 %collective-permute-start.8 = (bf16[512,128]{1,0:T(8,128)(2,1)}, bf16[512,128]{1,0:T(8,128)(2,1)S(1)}, u32[]{:S(2)}, u32[]{:S(2)}) collective-permute-start(bf16[512,128]{1,0:T(8,128)(2,1)} %get-tuple-element.27), channel_id=1, source_target_pairs={{0,3},{1,2},{2,1},{3,0},{4,7},{5,6},{6,5},{7,4},{8,11},{9,10},{10,... | collective-permute-start | bytes 393224 | tf_op jit(solution)/shard_map/ppermute | solution.py:262
  28.2 6.0 %collective-permute-start.6 = (bf16[512,128]{1,0:T(8,128)(2,1)}, bf16[512,128]{1,0:T(8,128)(2,1)S(1)}, u32[]{:S(2)}, u32[]{:S(2)}) collective-permute-start(bf16[512,128]{1,0:T(8,128)(2,1)} %get-tuple-element.27), channel_id=1, source_target_pairs={{0,1},{1,0},{2,3},{3,2},{4,5},{5,4},{6,7},{7,6},{8,9},{9,8},{10,11... | collective-permute-start | bytes 393224 | tf_op jit(solution)/shard_map/ppermute | solution.py:256
  37.7 3.4 %collective-permute-start.10 = (bf16[128,512]{1,0:T(8,128)(2,1)}, bf16[128,512]{1,0:T(8,128)(2,1)S(1)}, u32[]{:S(2)}, u32[]{:S(2)}) collective-permute-start(bf16[128,512]{1,0:T(8,128)(2,1)} %get-tuple-element.34), channel_id=1, source_target_pairs={{0,1},{1,0},{2,3},{3,2},{4,5},{5,4},{6,7},{7,6},{8,9},{9,8},{10,11... | collective-permute-start | bytes 393224 | tf_op jit(solution)/shard_map/ppermute | solution.py:256
  40.6 13.1 %collective-permute-start.16 = (f32[128,512]{1,0:T(8,128)}, f32[128,512]{1,0:T(8,128)S(1)}, u32[]{:S(2)}, u32[]{:S(2)}) collective-permute-start(f32[128,512]{1,0:T(8,128)} %get-tuple-element.45), channel_id=1, source_target_pairs={{0,1},{1,0},{2,3},{3,2},{4,5},{5,4},{6,7},{7,6},{8,9},{9,8},{10,11... | collective-permute-start | bytes 786440 | tf_op jit(solution)/shard_map/ppermute | solution.py:256
  40.8 7.3 %collective-permute-start.20 = (f32[128,256]{1,0:T(8,128)}, f32[128,256]{1,0:T(8,128)S(1)}, u32[]{:S(2)}, u32[]{:S(2)}) collective-permute-start(f32[128,256]{1,0:T(8,128)} %get-tuple-element.47), channel_id=1, source_target_pairs={{0,1},{1,0},{2,3},{3,2},{4,5},{5,4},{6,7},{7,6},{8,9},{9,8},{10,11... | collective-permute-start | bytes 393224 | tf_op jit(solution)/shard_map/ppermute | solution.py:256
  46.7 7.6 %collective-permute-start.11 = (bf16[4,128,128]{2,1,0:T(8,128)(2,1)}, bf16[4,128,128]{2,1,0:T(8,128)(2,1)S(1)}, u32[]{:S(2)}, u32[]{:S(2)}) collective-permute-start(bf16[4,128,128]{2,1,0:T(8,128)(2,1)} %get-tuple-element.36), channel_id=1, source_target_pairs={{0,2},{1,3},{2,0},{3,1},{4,6},{5,7},{6,4},{7,5},{8,10},{9,11},{10,... | collective-permute-start | bytes 393224 | tf_op jit(solution)/shard_map/ppermute | solution.py:259
  48.2 11.2 %collective-permute-start.21 = (f32[128,256]{1,0:T(8,128)S(1)}, f32[128,256]{1,0:T(8,128)S(1)}, u32[]{:S(2)}, u32[]{:S(2)}) collective-permute-start(f32[128,256]{1,0:T(8,128)S(1)} %add.12), channel_id=1, source_target_pairs={{0,4},{4,0},{8,12},{12,8},{16,20},{20,16},{24,28},{28,24},{1,5},{5... | collective-permute-start | bytes 393224 | tf_op jit(solution)/shard_map/ppermute | solution.py:334
  49.9 9.6 %collective-permute-start.12 = (bf16[4,128,128]{2,1,0:T(8,128)(2,1)}, bf16[4,128,128]{2,1,0:T(8,128)(2,1)S(1)}, u32[]{:S(2)}, u32[]{:S(2)}) collective-permute-start(bf16[4,128,128]{2,1,0:T(8,128)(2,1)} %get-tuple-element.37), channel_id=1, source_target_pairs={{0,28},{1,29},{2,30},{3,31},{4,0},{5,1},{6,2},{7,3},{8,4},{9,5},{1... | collective-permute-start | bytes 393224 | tf_op jit(solution)/shard_map/ppermute | solution.py:253
  52.3 12.5 %collective-permute-start.13 = (bf16[4,128,128]{2,1,0:T(8,128)(2,1)}, bf16[4,128,128]{2,1,0:T(8,128)(2,1)S(1)}, u32[]{:S(2)}, u32[]{:S(2)}) collective-permute-start(bf16[4,128,128]{2,1,0:T(8,128)(2,1)} %get-tuple-element.38), channel_id=1, source_target_pairs={{0,30},{1,31},{2,28},{3,29},{4,2},{5,3},{6,0},{7,1},{8,6},{9,7},{1... | collective-permute-start | bytes 393224 | tf_op jit(solution)/shard_map/ppermute | solution.py:253
  53.8 11.1 %collective-permute-start.14 = (bf16[4,128,128]{2,1,0:T(8,128)(2,1)}, bf16[4,128,128]{2,1,0:T(8,128)(2,1)S(1)}, u32[]{:S(2)}, u32[]{:S(2)}) collective-permute-start(bf16[4,128,128]{2,1,0:T(8,128)(2,1)} %get-tuple-element.39), channel_id=1, source_target_pairs={{0,4},{1,5},{2,6},{3,7},{4,8},{5,9},{6,10},{7,11},{8,12},{9,13},{1... | collective-permute-start | bytes 393224 | tf_op jit(solution)/shard_map/ppermute | solution.py:253
  54.3 10.6 %collective-permute-start.15 = (bf16[4,128,128]{2,1,0:T(8,128)(2,1)}, bf16[4,128,128]{2,1,0:T(8,128)(2,1)S(1)}, u32[]{:S(2)}, u32[]{:S(2)}) collective-permute-start(bf16[4,128,128]{2,1,0:T(8,128)(2,1)} %get-tuple-element.40), channel_id=1, source_target_pairs={{0,6},{1,7},{2,4},{3,5},{4,10},{5,11},{6,8},{7,9},{8,14},{9,15},{1... | collective-permute-start | bytes 393224 | tf_op jit(solution)/shard_map/ppermute | solution.py:253
  59.4 11.2 %collective-permute-start.9 = (bf16[512,256]{1,0:T(8,128)(2,1)S(1)}, bf16[512,256]{1,0:T(8,128)(2,1)S(1)}, u32[]{:S(2)}, u32[]{:S(2)}) collective-permute-start(bf16[512,256]{1,0:T(8,128)(2,1)S(1)} %copy-done.3), channel_id=1, source_target_pairs={{0,1},{1,0},{2,3},{3,2},{4,5},{5,4},{6,7},{7,6},{8,9},{9,8},{10,11... | collective-permute-start | bytes 786440 | tf_op jit(solution)/shard_map/ppermute | solution.py:256
  59.5 9.5 %collective-permute-start.22 = (f32[128,256]{1,0:T(8,128)S(1)}, f32[128,256]{1,0:T(8,128)S(1)}, u32[]{:S(2)}, u32[]{:S(2)}) collective-permute-start(f32[128,256]{1,0:T(8,128)S(1)} %add.13), channel_id=1, source_target_pairs={{0,8},{4,12},{8,0},{12,4},{16,24},{20,28},{24,16},{28,20},{1,9},{5... | collective-permute-start | bytes 393224 | tf_op jit(solution)/shard_map/ppermute | solution.py:334
  67.8 6.2 %collective-permute-start.18 = (bf16[4,128,128]{2,1,0:T(8,128)(2,1)}, bf16[4,128,128]{2,1,0:T(8,128)(2,1)S(1)}, u32[]{:S(2)}, u32[]{:S(2)}) collective-permute-start(bf16[4,128,128]{2,1,0:T(8,128)(2,1)} %total.1.own_ref), channel_id=1, source_target_pairs={{0,2},{1,3},{2,0},{3,1},{4,6},{5,7},{6,4},{7,5},{8,10},{9,11},{10,... | collective-permute-start | bytes 393224 | tf_op jit(solution)/shard_map/ppermute | solution.py:259
  69.1 7.3 %collective-permute-start.23 = (f32[128,256]{1,0:T(8,128)S(1)}, f32[128,256]{1,0:T(8,128)S(1)}, u32[]{:S(2)}, u32[]{:S(2)}) collective-permute-start(f32[128,256]{1,0:T(8,128)S(1)} %add.14), channel_id=1, source_target_pairs={{0,16},{4,20},{8,24},{12,28},{16,0},{20,4},{24,8},{28,12},{1,17},{... | collective-permute-start | bytes 393224 | tf_op jit(solution)/shard_map/ppermute | solution.py:334
  73.9 9.0 %collective-permute-start.17 = (bf16[4,128,128]{2,1,0:T(8,128)(2,1)}, bf16[4,128,128]{2,1,0:T(8,128)(2,1)S(1)}, u32[]{:S(2)}, u32[]{:S(2)}) collective-permute-start(bf16[4,128,128]{2,1,0:T(8,128)(2,1)} %total.1.own_ref), channel_id=1, source_target_pairs={{0,1},{1,0},{2,3},{3,2},{4,5},{5,4},{6,7},{7,6},{8,9},{9,8},{10,11... | collective-permute-start | bytes 393224 | tf_op jit(solution)/shard_map/ppermute | solution.py:256
  74.0 9.0 %collective-permute-start.19 = (bf16[4,128,128]{2,1,0:T(8,128)(2,1)S(1)}, bf16[4,128,128]{2,1,0:T(8,128)(2,1)S(1)}, u32[]{:S(2)}, u32[]{:S(2)}) collective-permute-start(bf16[4,128,128]{2,1,0:T(8,128)(2,1)S(1)} %collective-permute-done.18.y_ref), channel_id=1, source_target_pairs={{0,1},{1,0},{2,3},{3,2},{4,5},{5,4},{6,7},{7,6},{8,9},{9,8},{10,11... | collective-permute-start | bytes 393224 | tf_op jit(solution)/shard_map/ppermute | solution.py:256
  (21 other events, 92.5 us)

commit v2 on v1

--- a/solution.py
+++ b/solution.py
@@ -8,6 +8,7 @@
 BF = jnp.bfloat16
 F32 = jnp.float32
 T = 128
+VMEM = 16 * 2**20
 
 
 def mm(a, b):
@@ -229,6 +230,7 @@
         out_specs=out_specs[0] if single else out_specs,
         scratch_shapes=list(scratch),
         name=name,
+        compiler_params=pltpu.CompilerParams(vmem_limit_bytes=VMEM),
         cost_estimate=pl.CostEstimate(flops=flops, bytes_accessed=moved, transcendentals=0),
     )(*ins)
 

time: 87.4 us -> 74.2 us (0.85)
  Pallas kernels: 28.8 us -> 12.2 us
  starting transfers between devices: 26.4 us -> 28.5 us
  waiting for transfers between devices: 18.5 us -> 20.6 us
    pallas_call x9, Pallas kernels: 28.8 us -> 12.2 us  [call(): pl.pallas_call(kernel, out_shape=shapes[0] if single else shapes, in_spec...]
    ppermute x3, waiting for transfers between devices: 0.05 us -> 1.76 us  [swap_y(): return lax.ppermute(x, 'rep', [(r, r ^ 2) for r in range(reps)])]
    ppermute x3, starting transfers between devices: 7.47 us -> 9.12 us  [shards(): g = g + lax.ppermute(g, 'blk', [(b, b ^ step) for b in range(blocks)])]
    unnamed x42 -> x28, local copies, waits for them, and re-layouts: 5.33 us -> 4.49 us
  transfers between devices with their start and end apart: 24 -> 24, of which waited for: 8 -> 9; matrix products, arithmetic and copies ran while one was open for 1% -> 1% of each run, Pallas kernels for 21% -> 10%
where the time goes in v2:
time: 74.2 us; the launch traced here: 73.9 us
  starting transfers between devices  28.5 us (38%)
  waiting for transfers between devices  20.6 us (28%)
  Pallas kernels  12.2 us (16%)
  blocking collectives  5.79 us (8%)
  local copies, waits for them, and re-layouts  5.32 us (7%)
  between operations  1.46 us (2%)
    pallas_call x9, Pallas kernels, call(): pl.pallas_call(kernel, out_shape=shapes[0] if single else shapes, in_spec...  12.2 us
    ppermute x6, starting transfers between devices, hop(): return lax.ppermute(x, ('blk', 'rep'), pairs)  11.4 us
    ppermute x6, waiting for transfers between devices, hop(): return lax.ppermute(x, ('blk', 'rep'), pairs)  9.73 us
    ppermute x3, starting transfers between devices, shards(): g = g + lax.ppermute(g, 'blk', [(b, b ^ step) for b in range(blocks)])  9.12 us
    ppermute x3, waiting for transfers between devices, shards(): g = g + lax.ppermute(g, 'blk', [(b, b ^ step) for b in range(blocks)])  5.94 us
    all_gather x1, blocking collectives, shards(): weights = lax.all_gather(g, 'rep', axis=0, tiled=True).astype(F32)  5.79 us
    ppermute x3, starting transfers between devices, swap_y(): return lax.ppermute(x, 'rep', [(r, r ^ 2) for r in range(reps)])  4.56 us
    unnamed x28, local copies, waits for them, and re-layouts  4.49 us
  transfers between devices with their start and end apart: 24, of which 9 were waited for; matrix products, arithmetic and copies ran while one was open for 1% of the time, Pallas kernels for 10%

profile of v2, /device:TPU:0, one launch (start us, length us, event | category | flops | bytes accessed | tf_op | source)
XLA Modules:
  0.0 73.9 jit_solution(8971432598988684029)
XLA Ops:
  3.8 5.6 %collective-permute-start.4 = (bf16[1024,128]{1,0:T(8,128)(2,1)S(1)}, bf16[1024,128]{1,0:T(8,128)(2,1)S(1)}, u32[]{:S(2)}, u32[]{:S(2)}) collective-permute-start(bf16[1024,128]{1,0:T(8,128)(2,1)S(1)} %reorder.1.own_ref), channel_id=1, source_target_pairs={{0,28},{1,29},{2,30},{3,31},{4,0},{5,1},{6,2},{7,3},{8,4},{9,5},{1... | collective-permute-start | bytes 786440 | tf_op jit(solution)/shard_map/ppermute | solution.py:255
  12.1 3.5 %collective-permute-done.4.next_ref = bf16[1024,128]{1,0:T(8,128)(2,1)S(1)} collective-permute-done((bf16[1024,128]{1,0:T(8,128)(2,1)S(1)}, bf16[1024,128]{1,0:T(8,128)(2,1)S(1)}, u32[]{:S(2)}, u32[]{:S(2)}) %collective-permute-start.4) | collective-permute-done | bytes 262176 | tf_op jit(solution)/shard_map/ppermute | solution.py:255
  15.6 4.9 %collective-permute-done.3.prev_ref = bf16[1024,128]{1,0:T(8,128)(2,1)S(1)} collective-permute-done((bf16[1024,128]{1,0:T(8,128)(2,1)S(1)}, bf16[1024,128]{1,0:T(8,128)(2,1)S(1)}, u32[]{:S(2)}, u32[]{:S(2)}) %collective-permute-start.3) | collective-permute-done | bytes 262176 | tf_op jit(solution)/shard_map/ppermute | solution.py:255
  20.5 1.4 %copy-done = bf16[1,1,48,128,128]{4,3,2,1,0:T(8,128)(2,1)S(1)} copy-done((bf16[1,1,48,128,128]{4,3,2,1,0:T(8,128)(2,1)S(1)}, bf16[1,1,48,128,128]{4,3,2,1,0:T(8,128)(2,1)}, u32[]{:S(2)}) %copy-start) | copy-done | bytes 1572888
  23.3 2.6 %gather.1 = (bf16[512,128]{1,0:T(8,128)(2,1)S(1)}, bf16[512,128]{1,0:T(8,128)(2,1)S(1)}) custom-call(s32[48]{0:T(128)S(1)} %bitcast.15, s32[48]{0:T(128)S(1)} %bitcast.18, s32[1]{0:T(128)} %bitcast.6.na_ref, s32[48]{0:T(128)S(1)} %collective-permute-done.rb_ref, s32[48]{0:T(128)S(1)} %collective-permute-done.1.cb_ref, s32[1]{0:T(128)} %collective-permute-done.2.nb_ref, ...), custom_call_target="tpu_custom_call" | custom-call | tf_op jit(solution)/shard_map/gather/pallas_call | solution.py:226
  25.9 1.6 %collective-permute-start.7 = (bf16[512,128]{1,0:T(8,128)(2,1)S(1)}, bf16[512,128]{1,0:T(8,128)(2,1)S(1)}, u32[]{:S(2)}, u32[]{:S(2)}) collective-permute-start(bf16[512,128]{1,0:T(8,128)(2,1)S(1)} %get-tuple-element.26.own_ref), channel_id=1, source_target_pairs={{0,2},{1,3},{2,0},{3,1},{4,6},{5,7},{6,4},{7,5},{8,10},{9,11},{10,... | collective-permute-start | bytes 393224 | tf_op jit(solution)/shard_map/ppermute | solution.py:261
  28.1 1.5 %prepare.1 = (bf16[512,256]{1,0:T(8,128)(2,1)S(1)}, bf16[512,256]{1,0:T(8,128)(2,1)S(1)}, f32[512,256]{1,0:T(8,128)S(1)}, f32[512,128]{1,0:T(8,128)S(1)}, f32[8,512]{1,0:T(8,128)S(1)}) custom-call(s32[8,128]{1,0:T(8,128)S(1)} %bitcast.12, s32[1,1024]{1,0:T(1,128)S(1)} %bitcast.13, bf16[1024,256]{1,0:T(8,128)(2,1)S(1)} %copy-done.3, ...), custom_call_target="tpu_custom_call" | custom-call | tf_op jit(solution)/shard_map/prepare/pallas_call | solution.py:226
  29.6 1.8 %collective-permute-done.7.y_ref = bf16[512,128]{1,0:T(8,128)(2,1)S(1)} collective-permute-done((bf16[512,128]{1,0:T(8,128)(2,1)S(1)}, bf16[512,128]{1,0:T(8,128)(2,1)S(1)}, u32[]{:S(2)}, u32[]{:S(2)}) %collective-permute-start.7) | collective-permute-done | bytes 131104 | tf_op jit(solution)/shard_map/ppermute | solution.py:261
  31.4 1.9 %collective-permute-done.8.diag_ref = bf16[512,128]{1,0:T(8,128)(2,1)S(1)} collective-permute-done((bf16[512,128]{1,0:T(8,128)(2,1)S(1)}, bf16[512,128]{1,0:T(8,128)(2,1)S(1)}, u32[]{:S(2)}, u32[]{:S(2)}) %collective-permute-start.8) | collective-permute-done | bytes 131104 | tf_op jit(solution)/shard_map/ppermute | solution.py:264
  35.5 2.6 %scatter.1 = (f32[4,128,128]{2,1,0:T(8,128)S(1)}, bf16[4,128,128]{2,1,0:T(8,128)(2,1)S(1)}, bf16[4,128,128]{2,1,0:T(8,128)(2,1)S(1)}, bf16[4,128,128]{2,1,0:T(8,...) custom-call(s32[48]{0:T(128)S(1)} %bitcast.16, s32[48]{0:T(128)S(1)} %bitcast.19, ...), custom_call_target="tpu_custom_call" | custom-call | tf_op jit(solution)/shard_map/scatter/pallas_call | solution.py:226
  38.1 1.5 %collective-permute-start.11 = (bf16[4,128,128]{2,1,0:T(8,128)(2,1)S(1)}, bf16[4,128,128]{2,1,0:T(8,128)(2,1)S(1)}, u32[]{:S(2)}, u32[]{:S(2)}) collective-permute-start(bf16[4,128,128]{2,1,0:T(8,128)(2,1)S(1)} %get-tuple-element.36), channel_id=1, source_target_pairs={{0,2},{1,3},{2,0},{3,1},{4,6},{5,7},{6,4},{7,5},{8,10},{9,11},{10,... | collective-permute-start | bytes 393224 | tf_op jit(solution)/shard_map/ppermute | solution.py:261
  39.6 1.7 %collective-permute-start.21 = (f32[128,256]{1,0:T(8,128)S(1)}, f32[128,256]{1,0:T(8,128)S(1)}, u32[]{:S(2)}, u32[]{:S(2)}) collective-permute-start(f32[128,256]{1,0:T(8,128)S(1)} %add.12), channel_id=1, source_target_pairs={{0,4},{4,0},{8,12},{12,8},{16,20},{20,16},{24,28},{28,24},{1,5},{5... | collective-permute-start | bytes 393224 | tf_op jit(solution)/shard_map/ppermute | solution.py:336
  41.3 2.3 %collective-permute-start.12 = (bf16[4,128,128]{2,1,0:T(8,128)(2,1)S(1)}, bf16[4,128,128]{2,1,0:T(8,128)(2,1)S(1)}, u32[]{:S(2)}, u32[]{:S(2)}) collective-permute-start(bf16[4,128,128]{2,1,0:T(8,128)(2,1)S(1)} %get-tuple-element.37), channel_id=1, source_target_pairs={{0,28},{1,29},{2,30},{3,31},{4,0},{5,1},{6,2},{7,3},{8,4},{9,5},{1... | collective-permute-start | bytes 393224 | tf_op jit(solution)/shard_map/ppermute | solution.py:255
  43.6 1.6 %collective-permute-start.13 = (bf16[4,128,128]{2,1,0:T(8,128)(2,1)S(1)}, bf16[4,128,128]{2,1,0:T(8,128)(2,1)S(1)}, u32[]{:S(2)}, u32[]{:S(2)}) collective-permute-start(bf16[4,128,128]{2,1,0:T(8,128)(2,1)S(1)} %get-tuple-element.38), channel_id=1, source_target_pairs={{0,30},{1,31},{2,28},{3,29},{4,2},{5,3},{6,0},{7,1},{8,6},{9,7},{1... | collective-permute-start | bytes 393224 | tf_op jit(solution)/shard_map/ppermute | solution.py:255
  45.6 1.5 %collective-permute-start.15 = (bf16[4,128,128]{2,1,0:T(8,128)(2,1)S(1)}, bf16[4,128,128]{2,1,0:T(8,128)(2,1)S(1)}, u32[]{:S(2)}, u32[]{:S(2)}) collective-permute-start(bf16[4,128,128]{2,1,0:T(8,128)(2,1)S(1)} %get-tuple-element.40), channel_id=1, source_target_pairs={{0,6},{1,7},{2,4},{3,5},{4,10},{5,11},{6,8},{7,9},{8,14},{9,15},{1... | collective-permute-start | bytes 393224 | tf_op jit(solution)/shard_map/ppermute | solution.py:255
  47.2 3.6 %collective-permute-done.21 = f32[128,256]{1,0:T(8,128)S(1)} collective-permute-done((f32[128,256]{1,0:T(8,128)S(1)}, f32[128,256]{1,0:T(8,128)S(1)}, u32[]{:S(2)}, u32[]{:S(2)}) %collective-permute-start.21) | collective-permute-done | bytes 131104 | tf_op jit(solution)/shard_map/ppermute | solution.py:336
  50.9 4.1 %collective-permute-start.22 = (f32[128,256]{1,0:T(8,128)S(1)}, f32[128,256]{1,0:T(8,128)S(1)}, u32[]{:S(2)}, u32[]{:S(2)}) collective-permute-start(f32[128,256]{1,0:T(8,128)S(1)} %add.13), channel_id=1, source_target_pairs={{0,8},{4,12},{8,0},{12,4},{16,24},{20,28},{24,16},{28,20},{1,9},{5... | collective-permute-start | bytes 393224 | tf_op jit(solution)/shard_map/ppermute | solution.py:336
  55.0 1.3 %collective-permute-done.13.b_ref = bf16[4,128,128]{2,1,0:T(8,128)(2,1)S(1)} collective-permute-done((bf16[4,128,128]{2,1,0:T(8,128)(2,1)S(1)}, bf16[4,128,128]{2,1,0:T(8,128)(2,1)S(1)}, u32[]{:S(2)}, u32[]{:S(2)}) %collective-permute-start.13) | collective-permute-done | bytes 131104 | tf_op jit(solution)/shard_map/ppermute | solution.py:255
  56.4 1.5 %collective-permute-start.18 = (bf16[4,128,128]{2,1,0:T(8,128)(2,1)S(1)}, bf16[4,128,128]{2,1,0:T(8,128)(2,1)S(1)}, u32[]{:S(2)}, u32[]{:S(2)}) collective-permute-start(bf16[4,128,128]{2,1,0:T(8,128)(2,1)S(1)} %total.1.own_ref), channel_id=1, source_target_pairs={{0,2},{1,3},{2,0},{3,1},{4,6},{5,7},{6,4},{7,5},{8,10},{9,11},{10,... | collective-permute-start | bytes 393224 | tf_op jit(solution)/shard_map/ppermute | solution.py:261
  57.9 3.3 %collective-permute-start.23 = (f32[128,256]{1,0:T(8,128)S(1)}, f32[128,256]{1,0:T(8,128)S(1)}, u32[]{:S(2)}, u32[]{:S(2)}) collective-permute-start(f32[128,256]{1,0:T(8,128)S(1)} %add.14), channel_id=1, source_target_pairs={{0,16},{4,20},{8,24},{12,28},{16,0},{20,4},{24,8},{28,12},{1,17},{... | collective-permute-start | bytes 393224 | tf_op jit(solution)/shard_map/ppermute | solution.py:336
  61.3 1.5 %output.1 = bf16[1024,256]{1,0:T(8,128)(2,1)} custom-call(s32[1,1024]{1,0:T(1,128)S(1)} %copy-done.8, bf16[512,256]{1,0:T(8,128)(2,1)S(1)} %get-tuple-element.32.own_ref, bf16[512,256]{1,0:T(8,128)(2,1)S(1)} %collective-permute-done.9.core_ref), custom_call_target="tpu_custom_call" | custom-call | tf_op jit(solution)/shard_map/output/pallas_call | solution.py:226
  63.3 2.3 %collective-permute-done.23 = f32[128,256]{1,0:T(8,128)S(1)} collective-permute-done((f32[128,256]{1,0:T(8,128)S(1)}, f32[128,256]{1,0:T(8,128)S(1)}, u32[]{:S(2)}, u32[]{:S(2)}) %collective-permute-start.23) | collective-permute-done | bytes 131104 | tf_op jit(solution)/shard_map/ppermute | solution.py:336
  65.6 5.8 %all_gather.3 = bf16[512,256]{1,0:T(8,128)(2,1)S(1)} all-gather(bf16[128,256]{1,0:T(8,128)(2,1)S(1)} %add_convert_fusion), channel_id=1, replica_groups=mesh['blk'=8,'rep'=4] {'rep'}, dimensions={0}, use_global_device_ids=true | all-gather | bytes 327680 | tf_op jit(solution)/shard_map/all_gather | solution.py:349
  72.2 1.7 %restore.1 = bf16[1024,256]{1,0:T(8,128)(2,1)} custom-call(s32[1,1024]{1,0:T(1,128)S(1)} %copy-done.8, bf16[4,128,128]{2,1,0:T(8,128)(2,1)S(1)} %total.1.own_ref, bf16[4,128,128]{2,1,0:T(8,128)(2,1)S(1)} %collective-permute-done.17.core_ref, bf16[4,128,128]{2,1,0:T(8,128)(2,1)S(1)} %collective-permute-done.18.y_ref, ...), custom_call_target="tpu_custom_call" | custom-call | tf_op jit(solution)/shard_map/restore/pallas_call | solution.py:226
  (67 shorter events, 11.4 us)
Async XLA Ops:
  0.6 19.9 %collective-permute-start.5 = (bf16[48,128,128]{2,1,0:T(8,128)(2,1)}, bf16[48,128,128]{2,1,0:T(8,128)(2,1)S(1)}, u32[]{:S(2)}, u32[]{:S(2)}) collective-permute-start(bf16[48,128,128]{2,1,0:T(8,128)(2,1)} %bitcast.8), channel_id=1, source_target_pairs={{0,1},{1,0},{2,3},{3,2},{4,5},{5,4},{6,7},{7,6},{8,9},{9,8},{10,11... | collective-permute-start | bytes 4718600 | tf_op jit(solution)/shard_map/ppermute | solution.py:258
  3.8 11.8 %collective-permute-start.4 = (bf16[1024,128]{1,0:T(8,128)(2,1)S(1)}, bf16[1024,128]{1,0:T(8,128)(2,1)S(1)}, u32[]{:S(2)}, u32[]{:S(2)}) collective-permute-start(bf16[1024,128]{1,0:T(8,128)(2,1)S(1)} %reorder.1.own_ref), channel_id=1, source_target_pairs={{0,28},{1,29},{2,30},{3,31},{4,0},{5,1},{6,2},{7,3},{8,4},{9,5},{1... | collective-permute-start | bytes 786440 | tf_op jit(solution)/shard_map/ppermute | solution.py:255
  9.4 11.1 %collective-permute-start.3 = (bf16[1024,128]{1,0:T(8,128)(2,1)S(1)}, bf16[1024,128]{1,0:T(8,128)(2,1)S(1)}, u32[]{:S(2)}, u32[]{:S(2)}) collective-permute-start(bf16[1024,128]{1,0:T(8,128)(2,1)S(1)} %reorder.1.own_ref), channel_id=1, source_target_pairs={{0,4},{1,5},{2,6},{3,7},{4,8},{5,9},{6,10},{7,11},{8,12},{9,13},{1... | collective-permute-start | bytes 786440 | tf_op jit(solution)/shard_map/ppermute | solution.py:255
  9.4 2.4 %collective-permute-start = (s32[48]{0:T(128)}, s32[48]{0:T(128)S(1)}, u32[]{:S(2)}, u32[]{:S(2)}) collective-permute-start(s32[48]{0:T(128)} %bitcast.14), channel_id=1, source_target_pairs={{0,1},{1,0},{2,3},{3,2},{4,5},{5,4},{6,7},{7,6},{8,9},{9,8},{10,11... | collective-permute-start | bytes 584 | tf_op jit(solution)/shard_map/ppermute | solution.py:258
  9.6 1.3 %collective-permute-start.2 = (s32[1]{0:T(128)}, s32[1]{0:T(128)}, u32[]{:S(2)}, u32[]{:S(2)}) collective-permute-start(s32[1]{0:T(128)} %bitcast.2), channel_id=1, source_target_pairs={{0,1},{1,0},{2,3},{3,2},{4,5},{5,4},{6,7},{7,6},{8,9},{9,8},{10,11... | collective-permute-start | bytes 20 | tf_op jit(solution)/shard_map/ppermute | solution.py:258
  10.8 1.3 %collective-permute-start.1 = (s32[48]{0:T(128)}, s32[48]{0:T(128)S(1)}, u32[]{:S(2)}, u32[]{:S(2)}) collective-permute-start(s32[48]{0:T(128)} %bitcast.17), channel_id=1, source_target_pairs={{0,1},{1,0},{2,3},{3,2},{4,5},{5,4},{6,7},{7,6},{8,9},{9,8},{10,11... | collective-permute-start | bytes 584 | tf_op jit(solution)/shard_map/ppermute | solution.py:258
  25.9 5.5 %collective-permute-start.7 = (bf16[512,128]{1,0:T(8,128)(2,1)S(1)}, bf16[512,128]{1,0:T(8,128)(2,1)S(1)}, u32[]{:S(2)}, u32[]{:S(2)}) collective-permute-start(bf16[512,128]{1,0:T(8,128)(2,1)S(1)} %get-tuple-element.26.own_ref), channel_id=1, source_target_pairs={{0,2},{1,3},{2,0},{3,1},{4,6},{5,7},{6,4},{7,5},{8,10},{9,11},{10,... | collective-permute-start | bytes 393224 | tf_op jit(solution)/shard_map/ppermute | solution.py:261
  27.5 5.8 %collective-permute-start.8 = (bf16[512,128]{1,0:T(8,128)(2,1)S(1)}, bf16[512,128]{1,0:T(8,128)(2,1)S(1)}, u32[]{:S(2)}, u32[]{:S(2)}) collective-permute-start(bf16[512,128]{1,0:T(8,128)(2,1)S(1)} %get-tuple-element.27), channel_id=1, source_target_pairs={{0,3},{1,2},{2,1},{3,0},{4,7},{5,6},{6,5},{7,4},{8,11},{9,10},{10,... | collective-permute-start | bytes 393224 | tf_op jit(solution)/shard_map/ppermute | solution.py:264
  27.5 5.8 %collective-permute-start.6 = (bf16[512,128]{1,0:T(8,128)(2,1)S(1)}, bf16[512,128]{1,0:T(8,128)(2,1)S(1)}, u32[]{:S(2)}, u32[]{:S(2)}) collective-permute-start(bf16[512,128]{1,0:T(8,128)(2,1)S(1)} %get-tuple-element.27), channel_id=1, source_target_pairs={{0,1},{1,0},{2,3},{3,2},{4,5},{5,4},{6,7},{7,6},{8,9},{9,8},{10,11... | collective-permute-start | bytes 393224 | tf_op jit(solution)/shard_map/ppermute | solution.py:258
  33.9 1.5 %collective-permute-start.10 = (bf16[128,512]{1,0:T(8,128)(2,1)S(1)}, bf16[128,512]{1,0:T(8,128)(2,1)S(1)}, u32[]{:S(2)}, u32[]{:S(2)}) collective-permute-start(bf16[128,512]{1,0:T(8,128)(2,1)S(1)} %get-tuple-element.34), channel_id=1, source_target_pairs={{0,1},{1,0},{2,3},{3,2},{4,5},{5,4},{6,7},{7,6},{8,9},{9,8},{10,11... | collective-permute-start | bytes 393224 | tf_op jit(solution)/shard_map/ppermute | solution.py:258
  34.9 10.3 %collective-permute-start.16 = (f32[128,512]{1,0:T(8,128)S(1)}, f32[128,512]{1,0:T(8,128)S(1)}, u32[]{:S(2)}, u32[]{:S(2)}) collective-permute-start(f32[128,512]{1,0:T(8,128)S(1)} %get-tuple-element.45), channel_id=1, source_target_pairs={{0,1},{1,0},{2,3},{3,2},{4,5},{5,4},{6,7},{7,6},{8,9},{9,8},{10,11... | collective-permute-start | bytes 786440 | tf_op jit(solution)/shard_map/ppermute | solution.py:258
  35.2 4.5 %collective-permute-start.20 = (f32[128,256]{1,0:T(8,128)S(1)}, f32[128,256]{1,0:T(8,128)S(1)}, u32[]{:S(2)}, u32[]{:S(2)}) collective-permute-start(f32[128,256]{1,0:T(8,128)S(1)} %get-tuple-element.47), channel_id=1, source_target_pairs={{0,1},{1,0},{2,3},{3,2},{4,5},{5,4},{6,7},{7,6},{8,9},{9,8},{10,11... | collective-permute-start | bytes 393224 | tf_op jit(solution)/shard_map/ppermute | solution.py:258
  38.1 7.5 %collective-permute-start.11 = (bf16[4,128,128]{2,1,0:T(8,128)(2,1)S(1)}, bf16[4,128,128]{2,1,0:T(8,128)(2,1)S(1)}, u32[]{:S(2)}, u32[]{:S(2)}) collective-permute-start(bf16[4,128,128]{2,1,0:T(8,128)(2,1)S(1)} %get-tuple-element.36), channel_id=1, source_target_pairs={{0,2},{1,3},{2,0},{3,1},{4,6},{5,7},{6,4},{7,5},{8,10},{9,11},{10,... | collective-permute-start | bytes 393224 | tf_op jit(solution)/shard_map/ppermute | solution.py:261
  39.6 11.2 %collective-permute-start.21 = (f32[128,256]{1,0:T(8,128)S(1)}, f32[128,256]{1,0:T(8,128)S(1)}, u32[]{:S(2)}, u32[]{:S(2)}) collective-permute-start(f32[128,256]{1,0:T(8,128)S(1)} %add.12), channel_id=1, source_target_pairs={{0,4},{4,0},{8,12},{12,8},{16,20},{20,16},{24,28},{28,24},{1,5},{5... | collective-permute-start | bytes 393224 | tf_op jit(solution)/shard_map/ppermute | solution.py:336
  41.3 9.5 %collective-permute-start.12 = (bf16[4,128,128]{2,1,0:T(8,128)(2,1)S(1)}, bf16[4,128,128]{2,1,0:T(8,128)(2,1)S(1)}, u32[]{:S(2)}, u32[]{:S(2)}) collective-permute-start(bf16[4,128,128]{2,1,0:T(8,128)(2,1)S(1)} %get-tuple-element.37), channel_id=1, source_target_pairs={{0,28},{1,29},{2,30},{3,31},{4,0},{5,1},{6,2},{7,3},{8,4},{9,5},{1... | collective-permute-start | bytes 393224 | tf_op jit(solution)/shard_map/ppermute | solution.py:255
  43.6 12.6 %collective-permute-start.13 = (bf16[4,128,128]{2,1,0:T(8,128)(2,1)S(1)}, bf16[4,128,128]{2,1,0:T(8,128)(2,1)S(1)}, u32[]{:S(2)}, u32[]{:S(2)}) collective-permute-start(bf16[4,128,128]{2,1,0:T(8,128)(2,1)S(1)} %get-tuple-element.38), channel_id=1, source_target_pairs={{0,30},{1,31},{2,28},{3,29},{4,2},{5,3},{6,0},{7,1},{8,6},{9,7},{1... | collective-permute-start | bytes 393224 | tf_op jit(solution)/shard_map/ppermute | solution.py:255
  45.2 11.1 %collective-permute-start.14 = (bf16[4,128,128]{2,1,0:T(8,128)(2,1)S(1)}, bf16[4,128,128]{2,1,0:T(8,128)(2,1)S(1)}, u32[]{:S(2)}, u32[]{:S(2)}) collective-permute-start(bf16[4,128,128]{2,1,0:T(8,128)(2,1)S(1)} %get-tuple-element.39), channel_id=1, source_target_pairs={{0,4},{1,5},{2,6},{3,7},{4,8},{5,9},{6,10},{7,11},{8,12},{9,13},{1... | collective-permute-start | bytes 393224 | tf_op jit(solution)/shard_map/ppermute | solution.py:255
  45.6 10.7 %collective-permute-start.15 = (bf16[4,128,128]{2,1,0:T(8,128)(2,1)S(1)}, bf16[4,128,128]{2,1,0:T(8,128)(2,1)S(1)}, u32[]{:S(2)}, u32[]{:S(2)}) collective-permute-start(bf16[4,128,128]{2,1,0:T(8,128)(2,1)S(1)} %get-tuple-element.40), channel_id=1, source_target_pairs={{0,6},{1,7},{2,4},{3,5},{4,10},{5,11},{6,8},{7,9},{8,14},{9,15},{1... | collective-permute-start | bytes 393224 | tf_op jit(solution)/shard_map/ppermute | solution.py:255
  50.8 10.4 %collective-permute-start.9 = (bf16[512,256]{1,0:T(8,128)(2,1)S(1)}, bf16[512,256]{1,0:T(8,128)(2,1)S(1)}, u32[]{:S(2)}, u32[]{:S(2)}) collective-permute-start(bf16[512,256]{1,0:T(8,128)(2,1)S(1)} %get-tuple-element.32.own_ref), channel_id=1, source_target_pairs={{0,1},{1,0},{2,3},{3,2},{4,5},{5,4},{6,7},{7,6},{8,9},{9,8},{10,11... | collective-permute-start | bytes 786440 | tf_op jit(solution)/shard_map/ppermute | solution.py:258
  50.9 7.0 %collective-permute-start.22 = (f32[128,256]{1,0:T(8,128)S(1)}, f32[128,256]{1,0:T(8,128)S(1)}, u32[]{:S(2)}, u32[]{:S(2)}) collective-permute-start(f32[128,256]{1,0:T(8,128)S(1)} %add.13), channel_id=1, source_target_pairs={{0,8},{4,12},{8,0},{12,4},{16,24},{20,28},{24,16},{28,20},{1,9},{5... | collective-permute-start | bytes 393224 | tf_op jit(solution)/shard_map/ppermute | solution.py:336
  56.4 6.4 %collective-permute-start.18 = (bf16[4,128,128]{2,1,0:T(8,128)(2,1)S(1)}, bf16[4,128,128]{2,1,0:T(8,128)(2,1)S(1)}, u32[]{:S(2)}, u32[]{:S(2)}) collective-permute-start(bf16[4,128,128]{2,1,0:T(8,128)(2,1)S(1)} %total.1.own_ref), channel_id=1, source_target_pairs={{0,2},{1,3},{2,0},{3,1},{4,6},{5,7},{6,4},{7,5},{8,10},{9,11},{10,... | collective-permute-start | bytes 393224 | tf_op jit(solution)/shard_map/ppermute | solution.py:261
  57.9 7.7 %collective-permute-start.23 = (f32[128,256]{1,0:T(8,128)S(1)}, f32[128,256]{1,0:T(8,128)S(1)}, u32[]{:S(2)}, u32[]{:S(2)}) collective-permute-start(f32[128,256]{1,0:T(8,128)S(1)} %add.14), channel_id=1, source_target_pairs={{0,16},{4,20},{8,24},{12,28},{16,0},{20,4},{24,8},{28,12},{1,17},{... | collective-permute-start | bytes 393224 | tf_op jit(solution)/shard_map/ppermute | solution.py:336
  62.8 9.4 %collective-permute-start.17 = (bf16[4,128,128]{2,1,0:T(8,128)(2,1)S(1)}, bf16[4,128,128]{2,1,0:T(8,128)(2,1)S(1)}, u32[]{:S(2)}, u32[]{:S(2)}) collective-permute-start(bf16[4,128,128]{2,1,0:T(8,128)(2,1)S(1)} %total.1.own_ref), channel_id=1, source_target_pairs={{0,1},{1,0},{2,3},{3,2},{4,5},{5,4},{6,7},{7,6},{8,9},{9,8},{10,11... | collective-permute-start | bytes 393224 | tf_op jit(solution)/shard_map/ppermute | solution.py:258
  62.8 9.4 %collective-permute-start.19 = (bf16[4,128,128]{2,1,0:T(8,128)(2,1)S(1)}, bf16[4,128,128]{2,1,0:T(8,128)(2,1)S(1)}, u32[]{:S(2)}, u32[]{:S(2)}) collective-permute-start(bf16[4,128,128]{2,1,0:T(8,128)(2,1)S(1)} %collective-permute-done.18.y_ref), channel_id=1, source_target_pairs={{0,1},{1,0},{2,3},{3,2},{4,5},{5,4},{6,7},{7,6},{8,9},{9,8},{10,11... | collective-permute-start | bytes 393224 | tf_op jit(solution)/shard_map/ppermute | solution.py:258
  (14 other events, 56.4 us)

commit v3 on v2

v3 whole, which is shorter than its diff:
```python
import jax
import jax.numpy as jnp
from jax import lax
from jax.experimental import pallas as pl
from jax.experimental.pallas import tpu as pltpu
from jax.sharding import PartitionSpec as P

BF = jnp.bfloat16
F32 = jnp.float32
T = 128
VMEM = 16 * 2**20


def mm(a, b):
    return jnp.dot(a, b, preferred_element_type=F32)


def mm_nt(a, b):
    return lax.dot_general(a, b, (((1,), (1,)), ((), ())), preferred_element_type=F32)


def mm_tn(a, b):
    return lax.dot_general(a, b, (((0,), (0,)), ((), ())), preferred_element_type=F32)


def core_of():
    return lax.rem(lax.axis_index("rep"), 2)


def y_of():
    return lax.div(lax.axis_index("rep"), 2)


def order_column(order_row):
    return jnp.transpose(jnp.broadcast_to(order_row, (T, T)))


def onehot_rows(column, count):
    lane = lax.broadcasted_iota(jnp.int32, (T, T), 1).astype(F32)
    cuts = [
        jnp.where(column == lane + float(j * T), 1.0, 0.0).astype(BF) for j in range(count // T)
    ]
    return jnp.concatenate(cuts, axis=1)


def onehot_inverse(order_row, first, rows):
    wide = (rows, order_row.shape[1])
    at = lax.broadcasted_iota(jnp.int32, wide, 0) + first
    return jnp.where(jnp.broadcast_to(order_row, wide) == at, 1.0, 0.0).astype(BF)


def half_lanes(index):
    return pl.ds(pl.multiple_of(index * T, T), T)


def reorder_kernel(order_hbm, x_hbm, rows_hbm, cols_hbm, count_ref, out_ref, idx_ref, order, x, rows, cols, sems):
    c = core_of()
    total = out_ref.shape[0]
    copies = [
        pltpu.make_async_copy(src, dst, sems.at[i])
        for i, (src, dst) in enumerate(
            (
                (order_hbm, order),
                (x_hbm.at[:, half_lanes(c)], x),
                (rows_hbm, rows),
                (cols_hbm, cols),
            )
        )
    ]
    for copy in copies:
        copy.start()
    copies[0].wait()
    columns = [order_column(order[i : i + 1, :].astype(F32)) for i in range(total // T)]
    copies[1].wait()
    for i in range(total // T):
        out_ref[i * T : (i + 1) * T, :] = mm(onehot_rows(columns[i], total), x[...]).astype(BF)
    for copy in copies[2:]:
        copy.wait()
    slots = rows.shape[1]
    idx_ref[...] = jnp.zeros_like(idx_ref)
    idx_ref[0:1, 0:slots] = rows[...]
    idx_ref[1:2, 0:slots] = cols[...]
    idx_ref[2:3, :] = jnp.full((1, T), count_ref[0, 0], jnp.int32)


def pair_slots(mine, theirs, slots, row_tiles, pairs, out_ref, pending):
    dead = row_tiles
    nothing = 2 * slots
    beyond = 3 * row_tiles

    def clear(i, _):
        out_ref[0, i] = dead
        out_ref[1, i] = nothing
        out_ref[2, i] = nothing
        out_ref[3, i] = beyond
        out_ref[4, i] = beyond
        return 0

    lax.fori_loop(0, pairs, clear, 0)
    for r in range(row_tiles + 1):
        pending[0, r] = -1
        pending[1, r] = beyond

    def emit(n, r, a, b, col_a, col_b):
        out_ref[0, n] = r
        out_ref[1, n] = a
        out_ref[2, n] = b
        out_ref[3, n] = col_a
        out_ref[4, n] = col_b

    n = jnp.int32(0)
    for base, idx in ((0, mine), (slots, theirs)):
        count = idx[2, 0]

        def place(s, n, base=base, idx=idx, count=count):
            live = s < count
            r = jnp.where(live, idx[0, s], dead)
            col = jnp.where(live, idx[1, s], beyond)
            first = pending[0, r]
            whole = first >= 0

            @pl.when(whole)
            def _():
                emit(n, r, first, base + s, pending[1, r], col)
                pending[0, r] = -1

            @pl.when(jnp.logical_not(whole))
            def _():
                pending[0, r] = base + s
                pending[1, r] = col

            return n + whole.astype(jnp.int32)

        n = lax.fori_loop(0, slots, place, n)

    def rest(r, n):
        first = pending[0, r]
        left = first >= 0

        @pl.when(left)
        def _():
            emit(n, r, first, nothing, pending[1, r], beyond)

        return n + left.astype(jnp.int32)

    lax.fori_loop(0, row_tiles, rest, n)


def prepare_kernel(
    mine, theirs, va_any, vb_any, order_ref, degree_ref, x_ref, g_ref, w_ref,
    xh_ref, gh_ref, hs_ref, sc_ref, sr_ref, tiles_ref, pairs_ref, pending, sems,
):
    c = core_of()
    rows = x_ref.shape[0]
    slots = va_any.shape[0]
    copies = [
        pltpu.make_async_copy(va_any, tiles_ref.at[0:slots], sems.at[0]),
        pltpu.make_async_copy(vb_any, tiles_ref.at[slots : 2 * slots], sems.at[1]),
    ]
    for copy in copies:
        copy.start()
    tiles_ref[2 * slots] = jnp.zeros((T, T), BF)
    pair_slots(mine, theirs, slots, rows // T, slots + rows // T // 2, pairs_ref, pending)
    tiles = rows // T // 2
    deg = jnp.broadcast_to(degree_ref[...].astype(F32), (8, rows)).astype(BF)
    for i in range(tiles):
        column = order_column(order_ref[pl.ds(c * tiles + i, 1), :].astype(F32))
        hot = onehot_rows(column, rows)
        here = slice(i * T, (i + 1) * T)
        xt = mm(hot, x_ref[...]).astype(BF)
        xh_ref[here, :] = xt
        gh_ref[here, :] = mm(hot, g_ref[...]).astype(BF)
        hs_ref[here, :] = mm(xt, w_ref[...])
        scale = 1.0 / mm_nt(deg, hot)
        sr_ref[:, here] = scale
        sc_ref[here, :] = jnp.transpose(jnp.broadcast_to(scale[0:1, :], (T, T)))
    for copy in copies:
        copy.wait()


def gather_kernel(pairs_ref, prev_ref, own_ref, next_ref, tiles_ref, here_ref, other_ref, win, acc):
    c = core_of()
    rows = own_ref.shape[0]
    tiles = rows // T
    win[0:rows, :] = prev_ref[...]
    win[rows : 2 * rows, :] = own_ref[...]
    win[2 * rows : 3 * rows, :] = next_ref[...]
    win[3 * rows : 3 * rows + T, :] = jnp.zeros((T, T), BF)
    acc[...] = jnp.zeros_like(acc)

    def window(col):
        return win[pl.ds(pl.multiple_of(col * T, T), T), :]

    for p in range((tiles_ref.shape[0] - 1 + tiles) // 2):
        left = jnp.concatenate([tiles_ref[pairs_ref[1, p]], tiles_ref[pairs_ref[2, p]]], axis=1)
        right = jnp.concatenate([window(pairs_ref[3, p]), window(pairs_ref[4, p])], axis=0)
        acc[pairs_ref[0, p]] += mm(left, right)
    for i in range(tiles // 2):
        here_ref[i * T : (i + 1) * T, :] = acc[c * (tiles // 2) + i].astype(BF)
        other_ref[i * T : (i + 1) * T, :] = acc[(1 - c) * (tiles // 2) + i].astype(BF)


def dense_kernel(
    own_ref, core_ref, y_ref, diag_ref, hs_ref, gh_ref, sc_ref, sr_ref, wn_ref,
    act_ref, gp_ref, agg_ref, keep_ref, send_ref,
):
    c = core_of()
    scale = sc_ref[...]
    agg_ref[:, half_lanes(c)] = (
        (own_ref[...].astype(F32) + y_ref[...].astype(F32)) * scale
    ).astype(BF)
    agg_ref[:, half_lanes(1 - c)] = (
        (core_ref[...].astype(F32) + diag_ref[...].astype(F32)) * scale
    ).astype(BF)
    h = hs_ref[...] + mm(agg_ref[...], wn_ref[...])
    sig = jax.nn.sigmoid(h)
    act_ref[...] = (h * sig).astype(BF)
    gp = (gh_ref[...].astype(F32) * (sig * (1.0 + h * (1.0 - sig)))).astype(BF)
    gp_ref[...] = gp
    row = sr_ref[0:1, :]
    keep_ref[...] = (mm_nt(wn_ref[pl.ds(pl.multiple_of(c * T, T), T), :], gp) * row).astype(BF)
    send_ref[...] = (mm_nt(wn_ref[pl.ds(pl.multiple_of((1 - c) * T, T), T), :], gp) * row).astype(BF)


def terms_kernel(xh_ref, agg_ref, gp_ref, ws_ref, keep_ref, send_ref, mine_ref, theirs_ref):
    c, y = core_of(), y_of()
    gp = gp_ref[...]
    keep_ref[...] = mm_nt(ws_ref[pl.ds(pl.multiple_of(c * T, T), T), :], gp)
    send_ref[...] = mm_nt(ws_ref[pl.ds(pl.multiple_of((1 - c) * T, T), T), :], gp)

    def term(lhs_ref):
        mine_ref[...] = mm_tn(lhs_ref[:, half_lanes(c)], gp).astype(BF)
        theirs_ref[...] = mm_tn(lhs_ref[:, half_lanes(1 - c)], gp).astype(BF)

    @pl.when(y == 0)
    def _():
        term(xh_ref)

    @pl.when(y != 0)
    def _():
        term(agg_ref)


def scatter_kernel(
    pairs_ref, mine_ref, theirs_ref, tiles_ref,
    down_ref, own_ref, up_ref, src, acc,
):
    c = core_of()
    half = mine_ref.shape[1]
    tiles = 2 * half // T
    ht = tiles // 2
    for i in range(ht):
        cut = slice(i * T, (i + 1) * T)
        src[c * ht + i] = mine_ref[:, cut]
        src[(1 - c) * ht + i] = theirs_ref[:, cut]
    src[tiles] = jnp.zeros((T, T), BF)
    acc[...] = jnp.zeros_like(acc)
    for p in range((tiles_ref.shape[0] - 1 + tiles) // 2):
        right = jnp.concatenate([tiles_ref[pairs_ref[1, p]], tiles_ref[pairs_ref[2, p]]], axis=1)
        prod = mm(src[pairs_ref[0, p]], right)
        acc[pairs_ref[3, p]] += prod[:, :T]
        acc[pairs_ref[4, p]] += prod[:, T:]
    for i in range(tiles):
        down_ref[i] = acc[i].astype(BF)
        own_ref[i] = acc[tiles + i]
        up_ref[i] = acc[2 * tiles + i].astype(BF)


def chip_kernel(own_ref, a_ref, b_ref, g0_ref, g1_ref, g2_ref, g3_ref, out_ref):
    tiles = own_ref.shape[0]
    out_ref[0:tiles] = (own_ref[...] + (a_ref[...].astype(F32) + b_ref[...].astype(F32))).astype(BF)
    near = g0_ref[...].astype(F32) + g1_ref[...].astype(F32)
    weights = (near + (g2_ref[...].astype(F32) + g3_ref[...].astype(F32))).astype(BF)
    out_ref[tiles] = weights[:, :T]
    out_ref[tiles + 1] = weights[:, T:]


def total_kernel(mine_ref, theirs_ref, keep_ref, recv_ref, out_ref):
    c, y = core_of(), y_of()
    tiles = mine_ref.shape[0] - 2
    ht = tiles // 2
    for i in range(ht):
        cut = slice(i * T, (i + 1) * T)
        for first, ref in ((c * ht, keep_ref), ((1 - c) * ht, recv_ref)):
            both = mine_ref[first + i].astype(F32) + theirs_ref[first + i].astype(F32)
            out_ref[first + i] = (ref[:, cut] + both).astype(BF)
    for i in range(2):
        out_ref[tiles + 2 * y + i] = mine_ref[tiles + i]
        out_ref[tiles + 2 * (1 - y) + i] = theirs_ref[tiles + i]


def restore_kernel(order_ref, own_ref, core_ref, out_ref, self_ref, neigh_ref, full):
    c = core_of()
    rows = out_ref.shape[0]
    for side, ref in ((c, own_ref), (1 - c, core_ref)):
        at = pl.ds(pl.multiple_of(side * T, T), T)
        for i in range(2):
            cut = slice(i * T, (i + 1) * T)
            self_ref[at, cut] = ref[rows // T + i].astype(F32)
            neigh_ref[at, cut] = ref[rows // T + 2 + i].astype(F32)
    for i in range(rows // T):
        cut = slice(i * T, (i + 1) * T)
        full[pl.ds(pl.multiple_of(c * T, T), T), cut] = own_ref[i]
        full[pl.ds(pl.multiple_of((1 - c) * T, T), T), cut] = core_ref[i]
    for j in range(rows // 256):
        hot = onehot_inverse(order_ref[...], j * 256, 256)
        out_ref[j * 256 : (j + 1) * 256, :] = mm_nt(hot, full[...]).astype(BF)


def output_kernel(order_ref, own_ref, core_ref, out_ref, full):
    c = core_of()
    half = own_ref.shape[0]
    rows = 2 * half
    full[pl.ds(pl.multiple_of(c * half, half), half), :] = own_ref[...]
    full[pl.ds(pl.multiple_of((1 - c) * half, half), half), :] = core_ref[...]
    for j in range(rows // 256):
        hot = onehot_inverse(order_ref[...], j * 256, 256)
        out_ref[j * 256 : (j + 1) * 256, :] = mm(hot, full[...]).astype(BF)


def call(kernel, outs, ins, spaces=None, scratch=(), name=None, out_spaces=None):
    spaces = dict(spaces or {})
    out_spaces = dict(out_spaces or {})
    specs = [pl.BlockSpec(memory_space=spaces.get(i, pltpu.VMEM)) for i in range(len(ins))]
    shapes = [jax.ShapeDtypeStruct(s, d) for s, d in outs]
    out_specs = [pl.BlockSpec(memory_space=out_spaces.get(i, pltpu.VMEM)) for i in range(len(outs))]
    single = len(outs) == 1
    return pl.pallas_call(
        kernel,
        out_shape=shapes[0] if single else shapes,
        in_specs=specs,
        out_specs=out_specs[0] if single else out_specs,
        scratch_shapes=list(scratch),
        name=name,
        compiler_params=pltpu.CompilerParams(vmem_limit_bytes=VMEM),
        cost_estimate=pl.CostEstimate(flops=0, bytes_accessed=0, transcendentals=0),
    )(*ins)


def shards(
    features, degree, order, tile_rows, tile_cols, tile_count, tile_values, w_self, w_neigh, out_grad
):
    rows, width = features.shape
    half = rows // 2
    tiles = rows // T
    ht = tiles // 2
    blocks = lax.axis_size("blk")
    reps = lax.axis_size("rep")
    assert reps == 4 and width == 2 * T

    def hop(x, blk_step, rep_mask):
        pairs = [
            (b * reps + r, ((b + blk_step) % blocks) * reps + (r ^ rep_mask))
            for b in range(blocks)
            for r in range(reps)
        ]
        return lax.ppermute(x, ("blk", "rep"), pairs)

    def swap_core(x):
        return lax.ppermute(x, "rep", [(r, r ^ 1) for r in range(reps)])

    def swap_y(x):
        return lax.ppermute(x, "rep", [(r, r ^ 2) for r in range(reps)])

    def swap_diag(x):
        return lax.ppermute(x, "rep", [(r, r ^ 3) for r in range(reps)])

    def stay(x):
        return pltpu.with_memory_space_constraint(x, pltpu.MemorySpace.HBM)

    order8 = stay(order.reshape(tiles, T))
    deg = stay(degree.reshape(1, rows))
    features, out_grad = stay(features), stay(out_grad)
    va = tile_values[0, 0]
    slots = va.shape[0]
    hbm = pltpu.MemorySpace.HBM
    smem = pltpu.SMEM
    dma = pltpu.SemaphoreType.DMA

    feats_c, mine = call(
        reorder_kernel,
        [((rows, T), BF), ((8, T), jnp.int32)],
        [order8, features, stay(tile_rows[0]), stay(tile_cols[0]), tile_count],
        spaces={0: hbm, 1: hbm, 2: hbm, 3: hbm, 4: smem},
        scratch=[
            pltpu.VMEM((tiles, T), jnp.int32),
            pltpu.VMEM((rows, T), BF),
            pltpu.VMEM((1, slots), jnp.int32),
            pltpu.VMEM((1, slots), jnp.int32),
            dma((4,)),
        ],
        name="reorder",
    )
    prev = hop(feats_c, 1, 0)
    nxt = hop(feats_c, -1, 0)
    theirs = swap_core(mine)
    va, _ = lax.optimization_barrier((va, feats_c))
    vb = swap_core(va)
    va = stay(va)
    xh, gh, hs, sc, sr, both, pairs = call(
        prepare_kernel,
        [
            ((half, width), BF),
            ((half, width), BF),
            ((half, width), F32),
            ((half, T), F32),
            ((8, half), F32),
            ((2 * slots + 1, T, T), BF),
            ((8, T), jnp.int32),
        ],
        [mine, theirs, va, vb, order8, deg, features, out_grad, stay(w_self)],
        spaces={0: smem, 1: smem, 2: pl.ANY, 3: pl.ANY},
        out_spaces={6: smem},
        scratch=[pltpu.SMEM((2, 16), jnp.int32), dma((2,))],
        name="prepare",
    )
    here, other = call(
        gather_kernel,
        [((half, T), BF), ((half, T), BF)],
        [pairs, prev, feats_c, nxt, both],
        spaces={0: smem},
        scratch=[pltpu.VMEM((3 * rows + T, T), BF), pltpu.VMEM((tiles + 1, T, T), F32)],
        name="gather",
    )
    from_y = swap_y(here)
    from_diag = swap_diag(other)
    from_core = swap_core(other)
    act, gp, agg, s_keep, s_send = call(
        dense_kernel,
        [((half, width), BF), ((half, width), BF), ((half, width), BF), ((T, half), BF), ((T, half), BF)],
        [here, from_core, from_y, from_diag, hs, gh, sc, sr, w_neigh],
        name="dense",
    )
    s_other = swap_core(s_send)
    d_keep, d_send, g_mine, g_theirs = call(
        terms_kernel,
        [((T, half), F32), ((T, half), F32), ((T, width), BF), ((T, width), BF)],
        [xh, agg, gp, w_self],
        name="terms",
    )
    terms_in = [g_mine, swap_core(g_theirs)]
    if (blocks.bit_length() - 1) % 2:
        for x, mask in ((g_mine, 0), (g_theirs, 1)):
            pairs_of = [(b * reps + r, (b ^ 1) * reps + (r ^ mask)) for b in range(blocks) for r in range(reps)]
            terms_in.append(lax.ppermute(x, ("blk", "rep"), pairs_of))
    piece = (tiles, T, T)
    down, own, up = call(
        scatter_kernel,
        [(piece, BF), (piece, F32), (piece, BF)],
        [pairs, s_keep, s_other, both],
        spaces={0: smem},
        scratch=[pltpu.VMEM((tiles + 1, T, T), BF), pltpu.VMEM((3 * tiles + 1, T, T), F32)],
        name="scatter",
    )
    from_up = hop(down, -1, 0)
    from_down = hop(up, 1, 0)
    d_recv = swap_core(d_send)
    bits = blocks.bit_length() - 1
    assert blocks == 1 << bits and bits >= 2

    def from_block(x, mask):
        return lax.ppermute(x, "blk", [(b, b ^ mask) for b in range(blocks)])

    def four(p, q, r, s):
        near = p.astype(F32) + q.astype(F32)
        return (near + (r.astype(F32) + s.astype(F32))).astype(BF)

    at = bits % 2
    g = four(*terms_in) if at else (terms_in[0].astype(F32) + terms_in[1].astype(F32)).astype(BF)
    while True:
        parts = [g] + [from_block(g, k << at) for k in (1, 2, 3)]
        at += 2
        if at == bits:
            break
        g = four(*parts)
    chip = call(chip_kernel, [((tiles + 2, T, T), BF)], [own, from_up, from_down] + parts, name="chip")
    chip, act = lax.optimization_barrier((chip, act))
    chip_y = swap_y(chip)
    act_other = swap_core(act)
    output = call(
        output_kernel,
        [((rows, width), BF)],
        [order, act, act_other],
        scratch=[pltpu.VMEM((rows, width), BF)],
        name="output",
    )
    chip_y, output = lax.optimization_barrier((chip_y, output))
    total = call(total_kernel, [((tiles + 4, T, T), BF)], [chip, chip_y, d_keep, d_recv], name="total")
    total_core = swap_core(total)
    grad_features, grad_self, grad_neigh = call(
        restore_kernel,
        [((rows, width), BF), ((width, width), F32), ((width, width), F32)],
        [order, total, total_core],
        scratch=[pltpu.VMEM((width, rows), BF)],
        name="restore",
    )
    return output, grad_features, grad_self, grad_neigh


def solution(mesh):
    return jax.shard_map(
        shards,
        mesh=mesh,
        in_specs=(
            P("blk", None),
            P("blk"),
            P("blk", None),
            P("blk", "rep", None),
            P("blk", "rep", None),
            P("blk", "rep"),
            P("blk", "rep", None, None, None),
            P(),
            P(),
            P("blk", None),
        ),
        out_specs=(P("blk", None), P("blk", None), P(), P()),
        check_vma=False,
    )
```

time: 74.2 us -> 66.5 us (0.90)
  the two profiles are of different devices: /device:TPU:0 before, /device:TPU:11 now
where the time goes in v3:
time: 66.5 us; the launch traced here: 66.3 us
  waiting for transfers between devices  30.5 us (46%)
  starting transfers between devices  18.3 us (28%)
  Pallas kernels  16.1 us (24%)
  between operations  1.38 us (2%)
    pallas_call x10, Pallas kernels, call(): pl.pallas_call(kernel, out_shape=shapes[0] if single else shapes, in_spec...  16.1 us
    ppermute x3, waiting for transfers between devices, from_block(): return lax.ppermute(x, 'blk', [(b, b ^ mask) for b in range(blocks)])  12 us
    ppermute x2, waiting for transfers between devices, swap_y(): return lax.ppermute(x, 'rep', [(r, r ^ 2) for r in range(reps)])  7.43 us
    ppermute x8, starting transfers between devices, swap_core(): return lax.ppermute(x, 'rep', [(r, r ^ 1) for r in range(reps)])  5.12 us
    ppermute x3, starting transfers between devices, from_block(): return lax.ppermute(x, 'blk', [(b, b ^ mask) for b in range(blocks)])  4.46 us
    ppermute x4, waiting for transfers between devices, hop(): return lax.ppermute(x, ('blk', 'rep'), pairs)  4.43 us
    ppermute x4, starting transfers between devices, hop(): return lax.ppermute(x, ('blk', 'rep'), pairs)  3.88 us
    ppermute x8, waiting for transfers between devices, swap_core(): return lax.ppermute(x, 'rep', [(r, r ^ 1) for r in range(reps)])  3.67 us
  transfers between devices with their start and end apart: 20, of which 11 were waited for; matrix products, arithmetic and copies ran while one was open for 0% of the time, Pallas kernels for 15%

profile of v3, /device:TPU:11, one launch (start us, length us, event | category | flops | bytes accessed | tf_op | source)
XLA Modules:
  0.0 66.3 jit_solution(16483506851730831186)
XLA Ops:
  1.3 1.7 %reorder.1 = (bf16[1024,128]{1,0:T(8,128)(2,1)S(1)}, s32[8,128]{1,0:T(8,128)S(1)}) custom-call(s32[8,128]{1,0:T(8,128)} %bitcast.5, bf16[1024,256]{1,0:T(8,128)(2,1)} %x_ref.1, s32[1,48]{1,0:T(1,128)} %bitcast.10, s32[1,48]{1,0:T(1,128)} %bitcast.11, s32[1,1]{1,0:T(1,128)S(6)} %copy.14.count_ref), custom_call_target="tpu_custom_call" | custom-call | tf_op jit(solution)/shard_map/reorder/pallas_call | solution.py:328
  3.7 1.3 %collective-permute-start.2 = (bf16[1024,128]{1,0:T(8,128)(2,1)S(1)}, bf16[1024,128]{1,0:T(8,128)(2,1)S(1)}, u32[]{:S(2)}, u32[]{:S(2)}) collective-permute-start(bf16[1024,128]{1,0:T(8,128)(2,1)S(1)} %get-tuple-element.36.own_ref), channel_id=1, source_target_pairs={{0,4},{1,5},{2,6},{3,7},{4,8},{5,9},{6,10},{7,11},{8,12},{9,13},{1... | collective-permute-start | bytes 786440 | tf_op jit(solution)/shard_map/ppermute | solution.py:357
  5.8 0.9 %collective-permute-done.theirs = s32[8,128]{1,0:T(8,128)S(1)} collective-permute-done((s32[8,128]{1,0:T(8,128)S(1)}, s32[8,128]{1,0:T(8,128)S(1)}, u32[]{:S(2)}, u32[]{:S(2)}) %collective-permute-start) | collective-permute-done | bytes 4128 | tf_op jit(solution)/shard_map/ppermute | solution.py:360
  7.0 5.8 %prepare.1 = (bf16[512,256]{1,0:T(8,128)(2,1)S(1)}, bf16[512,256]{1,0:T(8,128)(2,1)S(1)}, f32[512,256]{1,0:T(8,128)S(1)}, f32[512,128]{1,0:T(8,128)S(1)}, f32[8,...) custom-call(s32[8,128]{1,0:T(8,128)S(1)} %get-tuple-element.35.mine, ...), custom_call_target="tpu_custom_call" | custom-call | tf_op jit(solution)/shard_map/prepare/pallas_call | solution.py:328
  12.8 4.4 %collective-permute-done.2.prev_ref = bf16[1024,128]{1,0:T(8,128)(2,1)S(1)} collective-permute-done((bf16[1024,128]{1,0:T(8,128)(2,1)S(1)}, bf16[1024,128]{1,0:T(8,128)(2,1)S(1)}, u32[]{:S(2)}, u32[]{:S(2)}) %collective-permute-start.2) | collective-permute-done | bytes 262176 | tf_op jit(solution)/shard_map/ppermute | solution.py:357
  17.2 1.9 %gather.1 = (bf16[512,128]{1,0:T(8,128)(2,1)S(1)}, bf16[512,128]{1,0:T(8,128)(2,1)S(1)}) custom-call(s32[8,128]{1,0:T(8,128)S(1)} %get-tuple-element.38.pairs_ref, bf16[1024,128]{1,0:T(8,128)(2,1)S(1)} %collective-permute-done.2.prev_ref, bf16[1024,128]{1,0:T(8,128)(2,1)S(1)} %get-tuple-element.36.own_ref, ...), custom_call_target="tpu_custom_call" | custom-call | tf_op jit(solution)/shard_map/gather/pallas_call | solution.py:328
  20.1 1.3 %collective-permute-start.5 = (bf16[512,128]{1,0:T(8,128)(2,1)S(1)}, bf16[512,128]{1,0:T(8,128)(2,1)S(1)}, u32[]{:S(2)}, u32[]{:S(2)}) collective-permute-start(bf16[512,128]{1,0:T(8,128)(2,1)S(1)} %get-tuple-element.40.own_ref), channel_id=1, source_target_pairs={{0,2},{1,3},{2,0},{3,1},{4,6},{5,7},{6,4},{7,5},{8,10},{9,11},{10,... | collective-permute-start | bytes 393224 | tf_op jit(solution)/shard_map/ppermute | solution.py:363
  21.8 3.4 %collective-permute-done.5.y_ref = bf16[512,128]{1,0:T(8,128)(2,1)S(1)} collective-permute-done((bf16[512,128]{1,0:T(8,128)(2,1)S(1)}, bf16[512,128]{1,0:T(8,128)(2,1)S(1)}, u32[]{:S(2)}, u32[]{:S(2)}) %collective-permute-start.5) | collective-permute-done | bytes 131104 | tf_op jit(solution)/shard_map/ppermute | solution.py:363
  25.2 3.0 %collective-permute-done.6.diag_ref = bf16[512,128]{1,0:T(8,128)(2,1)S(1)} collective-permute-done((bf16[512,128]{1,0:T(8,128)(2,1)S(1)}, bf16[512,128]{1,0:T(8,128)(2,1)S(1)}, u32[]{:S(2)}, u32[]{:S(2)}) %collective-permute-start.6) | collective-permute-done | bytes 131104 | tf_op jit(solution)/shard_map/ppermute | solution.py:366
  30.0 1.1 %collective-permute-start.11 = (bf16[128,256]{1,0:T(8,128)(2,1)S(1)}, bf16[128,256]{1,0:T(8,128)(2,1)S(1)}, u32[]{:S(2)}, u32[]{:S(2)}) collective-permute-start(bf16[128,256]{1,0:T(8,128)(2,1)S(1)} %get-tuple-element.54), channel_id=1, source_target_pairs={{0,4},{1,5},{2,6},{3,7},{4,0},{5,1},{6,2},{7,3},{8,12},{9,13},{10,... | collective-permute-start | bytes 196616 | tf_op jit(solution)/shard_map/ppermute | solution.py:445
  31.9 2.0 %scatter.1 = (bf16[8,128,128]{2,1,0:T(8,128)(2,1)S(1)}, f32[8,128,128]{2,1,0:T(8,128)S(1)}, bf16[8,128,128]{2,1,0:T(8,128)(2,1)S(1)}) custom-call(s32[8,128]{1,0:T(8,128)S(1)} %get-tuple-element.38.pairs_ref, bf16[128,512]{1,0:T(8,128)(2,1)S(1)} %get-tuple-element.46.mine_ref, bf16[128,512]{1,0:T(8,128)(2,1)S(1)} %collective-permute-done.7.theirs_ref, ...), custom_call_target="tpu_custom_call" | custom-call | tf_op jit(solution)/shard_map/scatter/pallas_call | solution.py:328
  33.9 1.2 %collective-permute-start.8 = (bf16[8,128,128]{2,1,0:T(8,128)(2,1)S(1)}, bf16[8,128,128]{2,1,0:T(8,128)(2,1)S(1)}, u32[]{:S(2)}, u32[]{:S(2)}) collective-permute-start(bf16[8,128,128]{2,1,0:T(8,128)(2,1)S(1)} %get-tuple-element.49), channel_id=1, source_target_pairs={{0,28},{1,29},{2,30},{3,31},{4,0},{5,1},{6,2},{7,3},{8,4},{9,5},{1... | collective-permute-start | bytes 786440 | tf_op jit(solution)/shard_map/ppermute | solution.py:357
  35.1 1.2 %collective-permute-start.9 = (bf16[8,128,128]{2,1,0:T(8,128)(2,1)S(1)}, bf16[8,128,128]{2,1,0:T(8,128)(2,1)S(1)}, u32[]{:S(2)}, u32[]{:S(2)}) collective-permute-start(bf16[8,128,128]{2,1,0:T(8,128)(2,1)S(1)} %get-tuple-element.50), channel_id=1, source_target_pairs={{0,4},{1,5},{2,6},{3,7},{4,8},{5,9},{6,10},{7,11},{8,12},{9,13},{1... | collective-permute-start | bytes 786440 | tf_op jit(solution)/shard_map/ppermute | solution.py:357
  36.6 4.0 %collective-permute-start.14 = (bf16[128,256]{1,0:T(8,128)(2,1)S(1)}, bf16[128,256]{1,0:T(8,128)(2,1)S(1)}, u32[]{:S(2)}, u32[]{:S(2)}) collective-permute-start(bf16[128,256]{1,0:T(8,128)(2,1)S(1)} %add_convert_fusion.g0_ref), channel_id=1, source_target_pairs={{0,16},{4,20},{8,24},{12,28},{16,0},{20,4},{24,8},{28,12},{1,17},{... | collective-permute-start | bytes 196616 | tf_op jit(solution)/shard_map/ppermute | solution.py:462
  40.8 3.2 %collective-permute-done.13.g1_ref = bf16[128,256]{1,0:T(8,128)(2,1)S(1)} collective-permute-done((bf16[128,256]{1,0:T(8,128)(2,1)S(1)}, bf16[128,256]{1,0:T(8,128)(2,1)S(1)}, u32[]{:S(2)}, u32[]{:S(2)}) %collective-permute-start.13) | collective-permute-done | bytes 65568 | tf_op jit(solution)/shard_map/ppermute | solution.py:462
  44.0 5.4 %collective-permute-done.14.g2_ref = bf16[128,256]{1,0:T(8,128)(2,1)S(1)} collective-permute-done((bf16[128,256]{1,0:T(8,128)(2,1)S(1)}, bf16[128,256]{1,0:T(8,128)(2,1)S(1)}, u32[]{:S(2)}, u32[]{:S(2)}) %collective-permute-start.14) | collective-permute-done | bytes 65568 | tf_op jit(solution)/shard_map/ppermute | solution.py:462
  49.4 3.4 %collective-permute-done.15.g3_ref = bf16[128,256]{1,0:T(8,128)(2,1)S(1)} collective-permute-done((bf16[128,256]{1,0:T(8,128)(2,1)S(1)}, bf16[128,256]{1,0:T(8,128)(2,1)S(1)}, u32[]{:S(2)}, u32[]{:S(2)}) %collective-permute-start.15) | collective-permute-done | bytes 65568 | tf_op jit(solution)/shard_map/ppermute | solution.py:462
  52.9 1.3 %collective-permute-start.16 = (bf16[10,128,128]{2,1,0:T(8,128)(2,1)S(1)}, bf16[10,128,128]{2,1,0:T(8,128)(2,1)S(1)}, u32[]{:S(2)}, u32[]{:S(2)}) collective-permute-start(bf16[10,128,128]{2,1,0:T(8,128)(2,1)S(1)} %chip.1.mine_ref), channel_id=1, source_target_pairs={{0,2},{1,3},{2,0},{3,1},{4,6},{5,7},{6,4},{7,5},{8,10},{9,11},{10,... | collective-permute-start | bytes 983048 | tf_op jit(solution)/shard_map/ppermute | solution.py:363
  55.0 1.2 %collective-permute-done.17.core_ref = bf16[512,256]{1,0:T(8,128)(2,1)S(1)} collective-permute-done((bf16[512,256]{1,0:T(8,128)(2,1)S(1)}, bf16[512,256]{1,0:T(8,128)(2,1)S(1)}, u32[]{:S(2)}, u32[]{:S(2)}) %collective-permute-start.17) | collective-permute-done | bytes 262176 | tf_op jit(solution)/shard_map/ppermute | solution.py:360
  56.1 1.5 %output.1 = bf16[1024,256]{1,0:T(8,128)(2,1)} custom-call(s32[1,1024]{1,0:T(1,128)S(1)} %copy-done.2, bf16[512,256]{1,0:T(8,128)(2,1)S(1)} %get-tuple-element.58.own_ref, bf16[512,256]{1,0:T(8,128)(2,1)S(1)} %collective-permute-done.17.core_ref), custom_call_target="tpu_custom_call" | custom-call | tf_op jit(solution)/shard_map/output/pallas_call | solution.py:328
  57.7 4.1 %collective-permute-done.16.theirs_ref = bf16[10,128,128]{2,1,0:T(8,128)(2,1)S(1)} collective-permute-done((bf16[10,128,128]{2,1,0:T(8,128)(2,1)S(1)}, bf16[10,128,128]{2,1,0:T(8,128)(2,1)S(1)}, u32[]{:S(2)}, u32[]{:S(2)}) %collective-permute-start.16) | collective-permute-done | bytes 327712 | tf_op jit(solution)/shard_map/ppermute | solution.py:363
  61.9 1.4 %collective-permute-start.19 = (bf16[12,128,128]{2,1,0:T(8,128)(2,1)S(1)}, bf16[12,128,128]{2,1,0:T(8,128)(2,1)S(1)}, u32[]{:S(2)}, u32[]{:S(2)}) collective-permute-start(bf16[12,128,128]{2,1,0:T(8,128)(2,1)S(1)} %total.1.own_ref), channel_id=1, source_target_pairs={{0,1},{1,0},{2,3},{3,2},{4,5},{5,4},{6,7},{7,6},{8,9},{9,8},{10,11... | collective-permute-start | bytes 1179656 | tf_op jit(solution)/shard_map/ppermute | solution.py:360
  63.3 1.3 %collective-permute-done.19.core_ref = bf16[12,128,128]{2,1,0:T(8,128)(2,1)S(1)} collective-permute-done((bf16[12,128,128]{2,1,0:T(8,128)(2,1)S(1)}, bf16[12,128,128]{2,1,0:T(8,128)(2,1)S(1)}, u32[]{:S(2)}, u32[]{:S(2)}) %collective-permute-start.19) | collective-permute-done | bytes 393248 | tf_op jit(solution)/shard_map/ppermute | solution.py:360
  64.6 1.7 %restore.1 = (bf16[1024,256]{1,0:T(8,128)(2,1)}, f32[256,256]{1,0:T(8,128)}, f32[256,256]{1,0:T(8,128)}) custom-call(s32[1,1024]{1,0:T(1,128)S(1)} %copy-done.2, bf16[12,128,128]{2,1,0:T(8,128)(2,1)S(1)} %total.1.own_ref, bf16[12,128,128]{2,1,0:T(8,128)(2,1)S(1)} %collective-permute-done.19.core_ref), custom_call_target="tpu_custom_call" | custom-call | tf_op jit(solution)/shard_map/restore/pallas_call | solution.py:328
  (33 shorter events, 7.3 us)
Async XLA Ops:
  3.0 4.0 %collective-permute-start.1 = (bf16[48,128,128]{2,1,0:T(8,128)(2,1)}, bf16[48,128,128]{2,1,0:T(8,128)(2,1)S(1)}, u32[]{:S(2)}, u32[]{:S(2)}) collective-permute-start(bf16[48,128,128]{2,1,0:T(8,128)(2,1)} %bitcast.7), channel_id=1, source_target_pairs={{0,1},{1,0},{2,3},{3,2},{4,5},{5,4},{6,7},{7,6},{8,9},{9,8},{10,11... | collective-permute-start | bytes 4718600 | tf_op jit(solution)/shard_map/ppermute | solution.py:360
  3.7 13.5 %collective-permute-start.2 = (bf16[1024,128]{1,0:T(8,128)(2,1)S(1)}, bf16[1024,128]{1,0:T(8,128)(2,1)S(1)}, u32[]{:S(2)}, u32[]{:S(2)}) collective-permute-start(bf16[1024,128]{1,0:T(8,128)(2,1)S(1)} %get-tuple-element.36.own_ref), channel_id=1, source_target_pairs={{0,4},{1,5},{2,6},{3,7},{4,8},{5,9},{6,10},{7,11},{8,12},{9,13},{1... | collective-permute-start | bytes 786440 | tf_op jit(solution)/shard_map/ppermute | solution.py:357
  5.0 12.2 %collective-permute-start.3 = (bf16[1024,128]{1,0:T(8,128)(2,1)S(1)}, bf16[1024,128]{1,0:T(8,128)(2,1)S(1)}, u32[]{:S(2)}, u32[]{:S(2)}) collective-permute-start(bf16[1024,128]{1,0:T(8,128)(2,1)S(1)} %get-tuple-element.36.own_ref), channel_id=1, source_target_pairs={{0,28},{1,29},{2,30},{3,31},{4,0},{5,1},{6,2},{7,3},{8,4},{9,5},{1... | collective-permute-start | bytes 786440 | tf_op jit(solution)/shard_map/ppermute | solution.py:357
  5.2 1.6 %collective-permute-start = (s32[8,128]{1,0:T(8,128)S(1)}, s32[8,128]{1,0:T(8,128)S(1)}, u32[]{:S(2)}, u32[]{:S(2)}) collective-permute-start(s32[8,128]{1,0:T(8,128)S(1)} %get-tuple-element.35.mine), channel_id=1, source_target_pairs={{0,1},{1,0},{2,3},{3,2},{4,5},{5,4},{6,7},{7,6},{8,9},{9,8},{10,11... | collective-permute-start | bytes 12296 | tf_op jit(solution)/shard_map/ppermute | solution.py:360
  17.2 10.9 %copy-start.1 = (bf16[256,256]{1,0:T(8,128)(2,1)S(1)}, bf16[256,256]{1,0:T(8,128)(2,1)}, u32[]{:S(2)}) copy-start(bf16[256,256]{1,0:T(8,128)(2,1)} %wn_ref.1) | copy-start | bytes 393220
  19.1 9.9 %copy-start = (bf16[256,256]{1,0:T(8,128)(2,1)S(1)}, bf16[256,256]{1,0:T(8,128)(2,1)}, u32[]{:S(2)}) copy-start(bf16[256,256]{1,0:T(8,128)(2,1)} %ws_ref.1) | copy-start | bytes 393220
  19.1 2.6 %collective-permute-start.4 = (bf16[512,128]{1,0:T(8,128)(2,1)S(1)}, bf16[512,128]{1,0:T(8,128)(2,1)S(1)}, u32[]{:S(2)}, u32[]{:S(2)}) collective-permute-start(bf16[512,128]{1,0:T(8,128)(2,1)S(1)} %get-tuple-element.41), channel_id=1, source_target_pairs={{0,1},{1,0},{2,3},{3,2},{4,5},{5,4},{6,7},{7,6},{8,9},{9,8},{10,11... | collective-permute-start | bytes 393224 | tf_op jit(solution)/shard_map/ppermute | solution.py:360
  20.1 5.1 %collective-permute-start.5 = (bf16[512,128]{1,0:T(8,128)(2,1)S(1)}, bf16[512,128]{1,0:T(8,128)(2,1)S(1)}, u32[]{:S(2)}, u32[]{:S(2)}) collective-permute-start(bf16[512,128]{1,0:T(8,128)(2,1)S(1)} %get-tuple-element.40.own_ref), channel_id=1, source_target_pairs={{0,2},{1,3},{2,0},{3,1},{4,6},{5,7},{6,4},{7,5},{8,10},{9,11},{10,... | collective-permute-start | bytes 393224 | tf_op jit(solution)/shard_map/ppermute | solution.py:363
  21.3 6.8 %collective-permute-start.6 = (bf16[512,128]{1,0:T(8,128)(2,1)S(1)}, bf16[512,128]{1,0:T(8,128)(2,1)S(1)}, u32[]{:S(2)}, u32[]{:S(2)}) collective-permute-start(bf16[512,128]{1,0:T(8,128)(2,1)S(1)} %get-tuple-element.41), channel_id=1, source_target_pairs={{0,3},{1,2},{2,1},{3,0},{4,7},{5,6},{6,5},{7,4},{8,11},{9,10},{10,... | collective-permute-start | bytes 393224 | tf_op jit(solution)/shard_map/ppermute | solution.py:366
  28.8 3.1 %collective-permute-start.7 = (bf16[128,512]{1,0:T(8,128)(2,1)S(1)}, bf16[128,512]{1,0:T(8,128)(2,1)S(1)}, u32[]{:S(2)}, u32[]{:S(2)}) collective-permute-start(bf16[128,512]{1,0:T(8,128)(2,1)S(1)} %get-tuple-element.47), channel_id=1, source_target_pairs={{0,1},{1,0},{2,3},{3,2},{4,5},{5,4},{6,7},{7,6},{8,9},{9,8},{10,11... | collective-permute-start | bytes 393224 | tf_op jit(solution)/shard_map/ppermute | solution.py:360
  29.7 6.6 %collective-permute-start.10 = (bf16[128,256]{1,0:T(8,128)(2,1)S(1)}, bf16[128,256]{1,0:T(8,128)(2,1)S(1)}, u32[]{:S(2)}, u32[]{:S(2)}) collective-permute-start(bf16[128,256]{1,0:T(8,128)(2,1)S(1)} %get-tuple-element.55), channel_id=1, source_target_pairs={{0,1},{1,0},{2,3},{3,2},{4,5},{5,4},{6,7},{7,6},{8,9},{9,8},{10,11... | collective-permute-start | bytes 196616 | tf_op jit(solution)/shard_map/ppermute | solution.py:360
  30.0 6.3 %collective-permute-start.11 = (bf16[128,256]{1,0:T(8,128)(2,1)S(1)}, bf16[128,256]{1,0:T(8,128)(2,1)S(1)}, u32[]{:S(2)}, u32[]{:S(2)}) collective-permute-start(bf16[128,256]{1,0:T(8,128)(2,1)S(1)} %get-tuple-element.54), channel_id=1, source_target_pairs={{0,4},{1,5},{2,6},{3,7},{4,0},{5,1},{6,2},{7,3},{8,12},{9,13},{10,... | collective-permute-start | bytes 196616 | tf_op jit(solution)/shard_map/ppermute | solution.py:445
  31.2 5.1 %collective-permute-start.12 = (bf16[128,256]{1,0:T(8,128)(2,1)S(1)}, bf16[128,256]{1,0:T(8,128)(2,1)S(1)}, u32[]{:S(2)}, u32[]{:S(2)}) collective-permute-start(bf16[128,256]{1,0:T(8,128)(2,1)S(1)} %get-tuple-element.55), channel_id=1, source_target_pairs={{0,5},{1,4},{2,7},{3,6},{4,1},{5,0},{6,3},{7,2},{8,13},{9,12},{10,... | collective-permute-start | bytes 196616 | tf_op jit(solution)/shard_map/ppermute | solution.py:445
  33.9 22.3 %copy-start.2 = (s32[1,1024]{1,0:T(1,128)S(1)}, s32[1,1024]{1,0:T(1,128)}, u32[]{:S(2)}) copy-start(s32[1,1024]{1,0:T(1,128)} %order_ref.3) | copy-start | bytes 12292
  33.9 18.9 %collective-permute-start.8 = (bf16[8,128,128]{2,1,0:T(8,128)(2,1)S(1)}, bf16[8,128,128]{2,1,0:T(8,128)(2,1)S(1)}, u32[]{:S(2)}, u32[]{:S(2)}) collective-permute-start(bf16[8,128,128]{2,1,0:T(8,128)(2,1)S(1)} %get-tuple-element.49), channel_id=1, source_target_pairs={{0,28},{1,29},{2,30},{3,31},{4,0},{5,1},{6,2},{7,3},{8,4},{9,5},{1... | collective-permute-start | bytes 786440 | tf_op jit(solution)/shard_map/ppermute | solution.py:357
  35.1 17.7 %collective-permute-start.9 = (bf16[8,128,128]{2,1,0:T(8,128)(2,1)S(1)}, bf16[8,128,128]{2,1,0:T(8,128)(2,1)S(1)}, u32[]{:S(2)}, u32[]{:S(2)}) collective-permute-start(bf16[8,128,128]{2,1,0:T(8,128)(2,1)S(1)} %get-tuple-element.50), channel_id=1, source_target_pairs={{0,4},{1,5},{2,6},{3,7},{4,8},{5,9},{6,10},{7,11},{8,12},{9,13},{1... | collective-permute-start | bytes 786440 | tf_op jit(solution)/shard_map/ppermute | solution.py:357
  36.3 7.7 %collective-permute-start.13 = (bf16[128,256]{1,0:T(8,128)(2,1)S(1)}, bf16[128,256]{1,0:T(8,128)(2,1)S(1)}, u32[]{:S(2)}, u32[]{:S(2)}) collective-permute-start(bf16[128,256]{1,0:T(8,128)(2,1)S(1)} %add_convert_fusion.g0_ref), channel_id=1, source_target_pairs={{0,8},{4,12},{8,0},{12,4},{16,24},{20,28},{24,16},{28,20},{1,9},{5... | collective-permute-start | bytes 196616 | tf_op jit(solution)/shard_map/ppermute | solution.py:462
  36.6 12.8 %collective-permute-start.14 = (bf16[128,256]{1,0:T(8,128)(2,1)S(1)}, bf16[128,256]{1,0:T(8,128)(2,1)S(1)}, u32[]{:S(2)}, u32[]{:S(2)}) collective-permute-start(bf16[128,256]{1,0:T(8,128)(2,1)S(1)} %add_convert_fusion.g0_ref), channel_id=1, source_target_pairs={{0,16},{4,20},{8,24},{12,28},{16,0},{20,4},{24,8},{28,12},{1,17},{... | collective-permute-start | bytes 196616 | tf_op jit(solution)/shard_map/ppermute | solution.py:462
  40.6 12.2 %collective-permute-start.15 = (bf16[128,256]{1,0:T(8,128)(2,1)S(1)}, bf16[128,256]{1,0:T(8,128)(2,1)S(1)}, u32[]{:S(2)}, u32[]{:S(2)}) collective-permute-start(bf16[128,256]{1,0:T(8,128)(2,1)S(1)} %add_convert_fusion.g0_ref), channel_id=1, source_target_pairs={{0,24},{4,28},{8,16},{12,20},{16,8},{20,12},{24,0},{28,4},{1,25},{... | collective-permute-start | bytes 196616 | tf_op jit(solution)/shard_map/ppermute | solution.py:462
  52.9 8.9 %collective-permute-start.16 = (bf16[10,128,128]{2,1,0:T(8,128)(2,1)S(1)}, bf16[10,128,128]{2,1,0:T(8,128)(2,1)S(1)}, u32[]{:S(2)}, u32[]{:S(2)}) collective-permute-start(bf16[10,128,128]{2,1,0:T(8,128)(2,1)S(1)} %chip.1.mine_ref), channel_id=1, source_target_pairs={{0,2},{1,3},{2,0},{3,1},{4,6},{5,7},{6,4},{7,5},{8,10},{9,11},{10,... | collective-permute-start | bytes 983048 | tf_op jit(solution)/shard_map/ppermute | solution.py:363
  54.2 1.9 %collective-permute-start.17 = (bf16[512,256]{1,0:T(8,128)(2,1)S(1)}, bf16[512,256]{1,0:T(8,128)(2,1)S(1)}, u32[]{:S(2)}, u32[]{:S(2)}) collective-permute-start(bf16[512,256]{1,0:T(8,128)(2,1)S(1)} %get-tuple-element.58.own_ref), channel_id=1, source_target_pairs={{0,1},{1,0},{2,3},{3,2},{4,5},{5,4},{6,7},{7,6},{8,9},{9,8},{10,11... | collective-permute-start | bytes 786440 | tf_op jit(solution)/shard_map/ppermute | solution.py:360
  55.0 6.8 %collective-permute-start.18 = (f32[128,512]{1,0:T(8,128)S(1)}, f32[128,512]{1,0:T(8,128)S(1)}, u32[]{:S(2)}, u32[]{:S(2)}) collective-permute-start(f32[128,512]{1,0:T(8,128)S(1)} %get-tuple-element.62), channel_id=1, source_target_pairs={{0,1},{1,0},{2,3},{3,2},{4,5},{5,4},{6,7},{7,6},{8,9},{9,8},{10,11... | collective-permute-start | bytes 786440 | tf_op jit(solution)/shard_map/ppermute | solution.py:360
  61.9 2.8 %collective-permute-start.19 = (bf16[12,128,128]{2,1,0:T(8,128)(2,1)S(1)}, bf16[12,128,128]{2,1,0:T(8,128)(2,1)S(1)}, u32[]{:S(2)}, u32[]{:S(2)}) collective-permute-start(bf16[12,128,128]{2,1,0:T(8,128)(2,1)S(1)} %total.1.own_ref), channel_id=1, source_target_pairs={{0,1},{1,0},{2,3},{3,2},{4,5},{5,4},{6,7},{7,6},{8,9},{9,8},{10,11... | collective-permute-start | bytes 1179656 | tf_op jit(solution)/shard_map/ppermute | solution.py:360

commit v4 on v3

--- a/solution.py
+++ b/solution.py
@@ -178,13 +178,17 @@
         copy.wait()
 
 
-def gather_kernel(pairs_ref, prev_ref, own_ref, next_ref, tiles_ref, here_ref, other_ref, win, acc):
-    c = core_of()
+def near_part():
+    return 2 - 2 * lax.rem(lax.axis_index("blk"), 2)
+
+
+def gather_kernel(pairs_ref, near_ref, own_ref, far_ref, tiles_ref, here_ref, other_ref, win, acc):
+    c, near = core_of(), near_part()
     rows = own_ref.shape[0]
     tiles = rows // T
-    win[0:rows, :] = prev_ref[...]
+    win[pl.ds(pl.multiple_of(near * rows, rows), rows), :] = near_ref[...]
     win[rows : 2 * rows, :] = own_ref[...]
-    win[2 * rows : 3 * rows, :] = next_ref[...]
+    win[pl.ds(pl.multiple_of((2 - near) * rows, rows), rows), :] = far_ref[...]
     win[3 * rows : 3 * rows + T, :] = jnp.zeros((T, T), BF)
     acc[...] = jnp.zeros_like(acc)
 
@@ -222,15 +226,21 @@
     send_ref[...] = (mm_nt(wn_ref[pl.ds(pl.multiple_of((1 - c) * T, T), T), :], gp) * row).astype(BF)
 
 
-def terms_kernel(xh_ref, agg_ref, gp_ref, ws_ref, keep_ref, send_ref, mine_ref, theirs_ref):
+def terms_kernel(xh_ref, agg_ref, gp_ref, ws_ref, keep_ref, send_ref, *refs):
     c, y = core_of(), y_of()
+    term_refs, full_ref = refs[:4], refs[4]
     gp = gp_ref[...]
     keep_ref[...] = mm_nt(ws_ref[pl.ds(pl.multiple_of(c * T, T), T), :], gp)
     send_ref[...] = mm_nt(ws_ref[pl.ds(pl.multiple_of((1 - c) * T, T), T), :], gp)
 
+    half = T // 2
+    x = lax.rem(lax.axis_index("blk"), 2)
+
     def term(lhs_ref):
-        mine_ref[...] = mm_tn(lhs_ref[:, half_lanes(c)], gp).astype(BF)
-        theirs_ref[...] = mm_tn(lhs_ref[:, half_lanes(1 - c)], gp).astype(BF)
+        for side, (keep, send) in ((c, term_refs[:2]), (1 - c, term_refs[2:])):
+            full_ref[...] = mm_tn(lhs_ref[:, half_lanes(side)], gp)
+            keep[...] = full_ref[pl.ds(pl.multiple_of(x * half, half), half), :].astype(BF)
+            send[...] = full_ref[pl.ds(pl.multiple_of((1 - x) * half, half), half), :].astype(BF)
 
     @pl.when(y == 0)
     def _():
@@ -243,9 +253,9 @@
 
 def scatter_kernel(
     pairs_ref, mine_ref, theirs_ref, tiles_ref,
-    down_ref, own_ref, up_ref, src, acc,
+    near_ref, own_ref, far_ref, src, acc,
 ):
-    c = core_of()
+    c, near = core_of(), near_part()
     half = mine_ref.shape[1]
     tiles = 2 * half // T
     ht = tiles // 2
@@ -261,43 +271,49 @@
         acc[pairs_ref[3, p]] += prod[:, :T]
         acc[pairs_ref[4, p]] += prod[:, T:]
     for i in range(tiles):
-        down_ref[i] = acc[i].astype(BF)
+        near_ref[i] = acc[near * tiles + i].astype(BF)
         own_ref[i] = acc[tiles + i]
-        up_ref[i] = acc[2 * tiles + i].astype(BF)
-
-
-def chip_kernel(own_ref, a_ref, b_ref, g0_ref, g1_ref, g2_ref, g3_ref, out_ref):
+        far_ref[i] = acc[(2 - near) * tiles + i].astype(BF)
+
+
+def chip_kernel(own_ref, a_ref, b_ref, g0_ref, g1_ref, g2_ref, g3_ref, out_ref, weights_ref):
     tiles = own_ref.shape[0]
     out_ref[0:tiles] = (own_ref[...] + (a_ref[...].astype(F32) + b_ref[...].astype(F32))).astype(BF)
     near = g0_ref[...].astype(F32) + g1_ref[...].astype(F32)
     weights = (near + (g2_ref[...].astype(F32) + g3_ref[...].astype(F32))).astype(BF)
-    out_ref[tiles] = weights[:, :T]
-    out_ref[tiles + 1] = weights[:, T:]
-
-
-def total_kernel(mine_ref, theirs_ref, keep_ref, recv_ref, out_ref):
-    c, y = core_of(), y_of()
-    tiles = mine_ref.shape[0] - 2
+    half = T // 2
+    for ref in (weights_ref, out_ref.at[tiles]):
+        ref[:half, :] = weights[:, :T]
+        ref[half:, :] = weights[:, T:]
+
+
+def total_kernel(mine_ref, theirs_ref, keep_ref, recv_ref, near_ref, near_y_ref, out_ref):
+    c, y, x = core_of(), y_of(), lax.rem(lax.axis_index("blk"), 2)
+    tiles = mine_ref.shape[0] - 1
     ht = tiles // 2
     for i in range(ht):
         cut = slice(i * T, (i + 1) * T)
         for first, ref in ((c * ht, keep_ref), ((1 - c) * ht, recv_ref)):
             both = mine_ref[first + i].astype(F32) + theirs_ref[first + i].astype(F32)
             out_ref[first + i] = (ref[:, cut] + both).astype(BF)
-    for i in range(2):
-        out_ref[tiles + 2 * y + i] = mine_ref[tiles + i]
-        out_ref[tiles + 2 * (1 - y) + i] = theirs_ref[tiles + i]
+    out_ref[tiles + 2 * y + x] = mine_ref[tiles]
+    out_ref[tiles + 2 * y + 1 - x] = near_ref[...]
+    out_ref[tiles + 2 * (1 - y) + x] = theirs_ref[tiles]
+    out_ref[tiles + 2 * (1 - y) + 1 - x] = near_y_ref[...]
 
 
 def restore_kernel(order_ref, own_ref, core_ref, out_ref, self_ref, neigh_ref, full):
     c = core_of()
     rows = out_ref.shape[0]
+    half = T // 2
     for side, ref in ((c, own_ref), (1 - c, core_ref)):
-        at = pl.ds(pl.multiple_of(side * T, T), T)
-        for i in range(2):
-            cut = slice(i * T, (i + 1) * T)
-            self_ref[at, cut] = ref[rows // T + i].astype(F32)
-            neigh_ref[at, cut] = ref[rows // T + 2 + i].astype(F32)
+        for x in range(2):
+            at = pl.ds(pl.multiple_of(side * T + x * half, half), half)
+            for i in range(2):
+                cut = slice(i * T, (i + 1) * T)
+                rows_of = slice(i * half, (i + 1) * half)
+                self_ref[at, cut] = ref[rows // T + x, rows_of, :].astype(F32)
+                neigh_ref[at, cut] = ref[rows // T + 2 + x, rows_of, :].astype(F32)
     for i in range(rows // T):
         cut = slice(i * T, (i + 1) * T)
         full[pl.ds(pl.multiple_of(c * T, T), T), cut] = own_ref[i]
@@ -348,13 +364,11 @@
     reps = lax.axis_size("rep")
     assert reps == 4 and width == 2 * T
 
-    def hop(x, blk_step, rep_mask):
-        pairs = [
-            (b * reps + r, ((b + blk_step) % blocks) * reps + (r ^ rep_mask))
-            for b in range(blocks)
-            for r in range(reps)
-        ]
-        return lax.ppermute(x, ("blk", "rep"), pairs)
+    def swap_near(x):
+        return lax.ppermute(x, "blk", [(b, b ^ 1) for b in range(blocks)])
+
+    def swap_far(x):
+        return lax.ppermute(x, "blk", [(b, (b + 2 * (b % 2) - 1) % blocks) for b in range(blocks)])
 
     def swap_core(x):
         return lax.ppermute(x, "rep", [(r, r ^ 1) for r in range(reps)])
@@ -391,8 +405,8 @@
         ],
         name="reorder",
     )
-    prev = hop(feats_c, 1, 0)
-    nxt = hop(feats_c, -1, 0)
+    near = swap_near(feats_c)
+    far = swap_far(feats_c)
     theirs = swap_core(mine)
     va, _ = lax.optimization_barrier((va, feats_c))
     vb = swap_core(va)
@@ -417,7 +431,7 @@
     here, other = call(
         gather_kernel,
         [((half, T), BF), ((half, T), BF)],
-        [pairs, prev, feats_c, nxt, both],
+        [pairs, near, feats_c, far, both],
         spaces={0: smem},
         scratch=[pltpu.VMEM((3 * rows + T, T), BF), pltpu.VMEM((tiles + 1, T, T), F32)],
         name="gather",
@@ -432,19 +446,20 @@
         name="dense",
     )
     s_other = swap_core(s_send)
-    d_keep, d_send, g_mine, g_theirs = call(
+    d_keep, d_send, mine_near, mine_far, theirs_near, theirs_far = call(
         terms_kernel,
-        [((T, half), F32), ((T, half), F32), ((T, width), BF), ((T, width), BF)],
+        [((T, half), F32), ((T, half), F32)] + [((T // 2, width), BF)] * 4,
         [xh, agg, gp, w_self],
+        scratch=[pltpu.VMEM((T, width), F32)],
         name="terms",
     )
-    terms_in = [g_mine, swap_core(g_theirs)]
-    if (blocks.bit_length() - 1) % 2:
-        for x, mask in ((g_mine, 0), (g_theirs, 1)):
-            pairs_of = [(b * reps + r, (b ^ 1) * reps + (r ^ mask)) for b in range(blocks) for r in range(reps)]
-            terms_in.append(lax.ppermute(x, ("blk", "rep"), pairs_of))
+    def swap_pair(x, mask):
+        pairs_of = [(b * reps + r, (b ^ 1) * reps + (r ^ mask)) for b in range(blocks) for r in range(reps)]
+        return lax.ppermute(x, ("blk", "rep"), pairs_of)
+
+    terms_in = [mine_near, swap_core(theirs_near), swap_pair(mine_far, 0), swap_pair(theirs_far, 1)]
     piece = (tiles, T, T)
-    down, own, up = call(
+    near, own, far = call(
         scatter_kernel,
         [(piece, BF), (piece, F32), (piece, BF)],
         [pairs, s_keep, s_other, both],
@@ -452,30 +467,27 @@
         scratch=[pltpu.VMEM((tiles + 1, T, T), BF), pltpu.VMEM((3 * tiles + 1, T, T), F32)],
         name="scatter",
     )
-    from_up = hop(down, -1, 0)
-    from_down = hop(up, 1, 0)
+    from_near = swap_near(near)
+    from_far = swap_far(far)
     d_recv = swap_core(d_send)
     bits = blocks.bit_length() - 1
-    assert blocks == 1 << bits and bits >= 2
-
-    def from_block(x, mask):
-        return lax.ppermute(x, "blk", [(b, b ^ mask) for b in range(blocks)])
+    assert blocks == 1 << bits and bits % 2 and bits > 1
 
     def four(p, q, r, s):
         near = p.astype(F32) + q.astype(F32)
         return (near + (r.astype(F32) + s.astype(F32))).astype(BF)
 
-    at = bits % 2
-    g = four(*terms_in) if at else (terms_in[0].astype(F32) + terms_in[1].astype(F32)).astype(BF)
-    while True:
-        parts = [g] + [from_block(g, k << at) for k in (1, 2, 3)]
-        at += 2
-        if at == bits:
-            break
+    parts = terms_in
+    for at in range(1, bits, 2):
         g = four(*parts)
-    chip = call(chip_kernel, [((tiles + 2, T, T), BF)], [own, from_up, from_down] + parts, name="chip")
+        parts = [g] + [
+            lax.ppermute(g, "blk", [(b, b ^ (k << at)) for b in range(blocks)]) for k in (1, 2, 3)
+        ]
+    chip, w_own = call(chip_kernel, [((tiles + 1, T, T), BF), ((T, T), BF)], [own, from_near, from_far] + parts, name="chip")
     chip, act = lax.optimization_barrier((chip, act))
     chip_y = swap_y(chip)
+    w_near = swap_pair(w_own, 0)
+    w_near_y = swap_pair(w_own, 2)
     act_other = swap_core(act)
     output = call(
         output_kernel,
@@ -485,7 +497,7 @@
         name="output",
     )
     chip_y, output = lax.optimization_barrier((chip_y, output))
-    total = call(total_kernel, [((tiles + 4, T, T), BF)], [chip, chip_y, d_keep, d_recv], name="total")
+    total = call(total_kernel, [((tiles + 4, T, T), BF)], [chip, chip_y, d_keep, d_recv, w_near, w_near_y], name="total")
     total_core = swap_core(total)
     grad_features, grad_self, grad_neigh = call(
         restore_kernel,

time: 66.5 us -> 62.2 us (0.935)
  the two profiles are of different devices: /device:TPU:11 before, /device:TPU:0 now
where the time goes in v4:
time: 62.2 us; the launch traced here: 62 us
  starting transfers between devices  24.8 us (40%)
  waiting for transfers between devices  19.6 us (32%)
  Pallas kernels  16.1 us (26%)
  between operations  1.4 us (2%)
    pallas_call x10, Pallas kernels, call(): pl.pallas_call(kernel, out_shape=shapes[0] if single else shapes, in_spec...  16.1 us
    ppermute x2, waiting for transfers between devices, swap_y(): return lax.ppermute(x, 'rep', [(r, r ^ 2) for r in range(reps)])  8.23 us
    ppermute x2, starting transfers between devices, swap_far(): lax.ppermute(x, 'blk', [(b, (b + 2 * (b % 2) - 1) % blocks) for b in rang...  7.14 us
    ppermute x3, waiting for transfers between devices, shards(): lax.ppermute(g, 'blk', [(b, b ^ k << at) for b in range(blocks)])  4.53 us
    ppermute x3, starting transfers between devices, shards(): lax.ppermute(g, 'blk', [(b, b ^ k << at) for b in range(blocks)])  4.44 us
    ppermute x2, starting transfers between devices, swap_near(): return lax.ppermute(x, 'blk', [(b, b ^ 1) for b in range(blocks)])  4.24 us
    ppermute x2, starting transfers between devices, swap_y(): return lax.ppermute(x, 'rep', [(r, r ^ 2) for r in range(reps)])  3.64 us
    ppermute x4, starting transfers between devices, swap_pair(): return lax.ppermute(x, ('blk', 'rep'), pairs_of)  3.48 us
  transfers between devices with their start and end apart: 22, of which 10 were waited for; matrix products, arithmetic and copies ran while one was open for 0% of the time, Pallas kernels for 16%

profile of v4, /device:TPU:0, one launch (start us, length us, event | category | flops | bytes accessed | tf_op | source)
XLA Modules:
  0.0 62.0 jit_solution(10742246902191920051)
XLA Ops:
  1.3 1.7 %reorder.1 = (bf16[1024,128]{1,0:T(8,128)(2,1)S(1)}, s32[8,128]{1,0:T(8,128)S(1)}) custom-call(s32[8,128]{1,0:T(8,128)} %bitcast.5, bf16[1024,256]{1,0:T(8,128)(2,1)} %x_ref.1, s32[1,48]{1,0:T(1,128)} %bitcast.10, s32[1,48]{1,0:T(1,128)} %bitcast.11, s32[1,1]{1,0:T(1,128)S(6)} %copy.14.count_ref), custom_call_target="tpu_custom_call" | custom-call | tf_op jit(solution)/shard_map/reorder/pallas_call | solution.py:344
  3.5 2.6 %collective-permute-start.2 = (bf16[1024,128]{1,0:T(8,128)(2,1)S(1)}, bf16[1024,128]{1,0:T(8,128)(2,1)S(1)}, u32[]{:S(2)}, u32[]{:S(2)}) collective-permute-start(bf16[1024,128]{1,0:T(8,128)(2,1)S(1)} %get-tuple-element.40.own_ref), channel_id=1, source_target_pairs={{0,4},{4,0},{8,12},{12,8},{16,20},{20,16},{24,28},{28,24},{1,5},{5... | collective-permute-start | bytes 786440 | tf_op jit(solution)/shard_map/ppermute | solution.py:368
  6.1 3.6 %collective-permute-start.3 = (bf16[1024,128]{1,0:T(8,128)(2,1)S(1)}, bf16[1024,128]{1,0:T(8,128)(2,1)S(1)}, u32[]{:S(2)}, u32[]{:S(2)}) collective-permute-start(bf16[1024,128]{1,0:T(8,128)(2,1)S(1)} %get-tuple-element.40.own_ref), channel_id=1, source_target_pairs={{0,28},{4,8},{8,4},{12,16},{16,12},{20,24},{24,20},{28,0},{1,29},{... | collective-permute-start | bytes 786440 | tf_op jit(solution)/shard_map/ppermute | solution.py:371
  9.7 1.2 %collective-permute-done.theirs = s32[8,128]{1,0:T(8,128)S(1)} collective-permute-done((s32[8,128]{1,0:T(8,128)S(1)}, s32[8,128]{1,0:T(8,128)S(1)}, u32[]{:S(2)}, u32[]{:S(2)}) %collective-permute-start) | collective-permute-done | bytes 4128 | tf_op jit(solution)/shard_map/ppermute | solution.py:374
  10.8 5.8 %prepare.1 = (bf16[512,256]{1,0:T(8,128)(2,1)S(1)}, bf16[512,256]{1,0:T(8,128)(2,1)S(1)}, f32[512,256]{1,0:T(8,128)S(1)}, f32[512,128]{1,0:T(8,128)S(1)}, f32[8,...) custom-call(s32[8,128]{1,0:T(8,128)S(1)} %get-tuple-element.39.mine, ...), custom_call_target="tpu_custom_call" | custom-call | tf_op jit(solution)/shard_map/prepare/pallas_call | solution.py:344
  16.6 2.0 %collective-permute-done.2.near_ref = bf16[1024,128]{1,0:T(8,128)(2,1)S(1)} collective-permute-done((bf16[1024,128]{1,0:T(8,128)(2,1)S(1)}, bf16[1024,128]{1,0:T(8,128)(2,1)S(1)}, u32[]{:S(2)}, u32[]{:S(2)}) %collective-permute-start.2) | collective-permute-done | bytes 262176 | tf_op jit(solution)/shard_map/ppermute | solution.py:368
  18.6 1.9 %gather.1 = (bf16[512,128]{1,0:T(8,128)(2,1)S(1)}, bf16[512,128]{1,0:T(8,128)(2,1)S(1)}) custom-call(s32[8,128]{1,0:T(8,128)S(1)} %get-tuple-element.42.pairs_ref, bf16[1024,128]{1,0:T(8,128)(2,1)S(1)} %collective-permute-done.2.near_ref, bf16[1024,128]{1,0:T(8,128)(2,1)S(1)} %get-tuple-element.40.own_ref, ...), custom_call_target="tpu_custom_call" | custom-call | tf_op jit(solution)/shard_map/gather/pallas_call | solution.py:344
  20.6 1.9 %collective-permute-start.5 = (bf16[512,128]{1,0:T(8,128)(2,1)S(1)}, bf16[512,128]{1,0:T(8,128)(2,1)S(1)}, u32[]{:S(2)}, u32[]{:S(2)}) collective-permute-start(bf16[512,128]{1,0:T(8,128)(2,1)S(1)} %get-tuple-element.44.own_ref), channel_id=1, source_target_pairs={{0,2},{1,3},{2,0},{3,1},{4,6},{5,7},{6,4},{7,5},{8,10},{9,11},{10,... | collective-permute-start | bytes 393224 | tf_op jit(solution)/shard_map/ppermute | solution.py:377
  22.5 4.4 %collective-permute-done.5.y_ref = bf16[512,128]{1,0:T(8,128)(2,1)S(1)} collective-permute-done((bf16[512,128]{1,0:T(8,128)(2,1)S(1)}, bf16[512,128]{1,0:T(8,128)(2,1)S(1)}, u32[]{:S(2)}, u32[]{:S(2)}) %collective-permute-start.5) | collective-permute-done | bytes 131104 | tf_op jit(solution)/shard_map/ppermute | solution.py:377
  27.0 2.0 %collective-permute-done.6.diag_ref = bf16[512,128]{1,0:T(8,128)(2,1)S(1)} collective-permute-done((bf16[512,128]{1,0:T(8,128)(2,1)S(1)}, bf16[512,128]{1,0:T(8,128)(2,1)S(1)}, u32[]{:S(2)}, u32[]{:S(2)}) %collective-permute-start.6) | collective-permute-done | bytes 131104 | tf_op jit(solution)/shard_map/ppermute | solution.py:380
  30.9 1.7 %collective-permute-start.11 = (bf16[64,256]{1,0:T(8,128)(2,1)S(1)}, bf16[64,256]{1,0:T(8,128)(2,1)S(1)}, u32[]{:S(2)}, u32[]{:S(2)}) collective-permute-start(bf16[64,256]{1,0:T(8,128)(2,1)S(1)} %get-tuple-element.60), channel_id=1, source_target_pairs={{0,4},{1,5},{2,6},{3,7},{4,0},{5,1},{6,2},{7,3},{8,12},{9,13},{10,... | collective-permute-start | bytes 98312 | tf_op jit(solution)/shard_map/ppermute | solution.py:458
  32.6 2.0 %scatter.1 = (bf16[8,128,128]{2,1,0:T(8,128)(2,1)S(1)}, f32[8,128,128]{2,1,0:T(8,128)S(1)}, bf16[8,128,128]{2,1,0:T(8,128)(2,1)S(1)}) custom-call(s32[8,128]{1,0:T(8,128)S(1)} %get-tuple-element.42.pairs_ref, bf16[128,512]{1,0:T(8,128)(2,1)S(1)} %get-tuple-element.50.mine_ref, bf16[128,512]{1,0:T(8,128)(2,1)S(1)} %collective-permute-done.7.theirs_ref, ...), custom_call_target="tpu_custom_call" | custom-call | tf_op jit(solution)/shard_map/scatter/pallas_call | solution.py:344
  34.6 1.7 %collective-permute-start.8 = (bf16[8,128,128]{2,1,0:T(8,128)(2,1)S(1)}, bf16[8,128,128]{2,1,0:T(8,128)(2,1)S(1)}, u32[]{:S(2)}, u32[]{:S(2)}) collective-permute-start(bf16[8,128,128]{2,1,0:T(8,128)(2,1)S(1)} %get-tuple-element.53), channel_id=1, source_target_pairs={{0,4},{4,0},{8,12},{12,8},{16,20},{20,16},{24,28},{28,24},{1,5},{5... | collective-permute-start | bytes 786440 | tf_op jit(solution)/shard_map/ppermute | solution.py:368
  36.2 3.6 %collective-permute-start.9 = (bf16[8,128,128]{2,1,0:T(8,128)(2,1)S(1)}, bf16[8,128,128]{2,1,0:T(8,128)(2,1)S(1)}, u32[]{:S(2)}, u32[]{:S(2)}) collective-permute-start(bf16[8,128,128]{2,1,0:T(8,128)(2,1)S(1)} %get-tuple-element.54), channel_id=1, source_target_pairs={{0,28},{4,8},{8,4},{12,16},{16,12},{20,24},{24,20},{28,0},{1,29},{... | collective-permute-start | bytes 786440 | tf_op jit(solution)/shard_map/ppermute | solution.py:371
  39.9 1.0 %collective-permute-start.14 = (bf16[64,256]{1,0:T(8,128)(2,1)S(1)}, bf16[64,256]{1,0:T(8,128)(2,1)S(1)}, u32[]{:S(2)}, u32[]{:S(2)}) collective-permute-start(bf16[64,256]{1,0:T(8,128)(2,1)S(1)} %add_convert_fusion.g0_ref), channel_id=1, source_target_pairs={{0,16},{4,20},{8,24},{12,28},{16,0},{20,4},{24,8},{28,12},{1,17},{... | collective-permute-start | bytes 98312 | tf_op jit(solution)/shard_map/ppermute | solution.py:484
  40.9 3.4 %collective-permute-start.15 = (bf16[64,256]{1,0:T(8,128)(2,1)S(1)}, bf16[64,256]{1,0:T(8,128)(2,1)S(1)}, u32[]{:S(2)}, u32[]{:S(2)}) collective-permute-start(bf16[64,256]{1,0:T(8,128)(2,1)S(1)} %add_convert_fusion.g0_ref), channel_id=1, source_target_pairs={{0,24},{4,28},{8,16},{12,20},{16,8},{20,12},{24,0},{28,4},{1,25},{... | collective-permute-start | bytes 98312 | tf_op jit(solution)/shard_map/ppermute | solution.py:484
  44.3 2.9 %collective-permute-done.13.g1_ref = bf16[64,256]{1,0:T(8,128)(2,1)S(1)} collective-permute-done((bf16[64,256]{1,0:T(8,128)(2,1)S(1)}, bf16[64,256]{1,0:T(8,128)(2,1)S(1)}, u32[]{:S(2)}, u32[]{:S(2)}) %collective-permute-start.13) | collective-permute-done | bytes 32800 | tf_op jit(solution)/shard_map/ppermute | solution.py:484
  47.6 1.3 %collective-permute-done.15.g3_ref = bf16[64,256]{1,0:T(8,128)(2,1)S(1)} collective-permute-done((bf16[64,256]{1,0:T(8,128)(2,1)S(1)}, bf16[64,256]{1,0:T(8,128)(2,1)S(1)}, u32[]{:S(2)}, u32[]{:S(2)}) %collective-permute-start.15) | collective-permute-done | bytes 32800 | tf_op jit(solution)/shard_map/ppermute | solution.py:484
  49.0 1.8 %collective-permute-start.16 = (bf16[9,128,128]{2,1,0:T(8,128)(2,1)S(1)}, bf16[9,128,128]{2,1,0:T(8,128)(2,1)S(1)}, u32[]{:S(2)}, u32[]{:S(2)}) collective-permute-start(bf16[9,128,128]{2,1,0:T(8,128)(2,1)S(1)} %get-tuple-element.64.mine_ref), channel_id=1, source_target_pairs={{0,2},{1,3},{2,0},{3,1},{4,6},{5,7},{6,4},{7,5},{8,10},{9,11},{10,... | collective-permute-start | bytes 884744 | tf_op jit(solution)/shard_map/ppermute | solution.py:377
  51.3 1.5 %collective-permute-start.19 = (bf16[128,128]{1,0:T(8,128)(2,1)S(1)}, bf16[128,128]{1,0:T(8,128)(2,1)S(1)}, u32[]{:S(2)}, u32[]{:S(2)}) collective-permute-start(bf16[128,128]{1,0:T(8,128)(2,1)S(1)} %get-tuple-element.70), channel_id=1, source_target_pairs={{0,4},{1,5},{2,6},{3,7},{4,0},{5,1},{6,2},{7,3},{8,12},{9,13},{10,... | collective-permute-start | bytes 98312 | tf_op jit(solution)/shard_map/ppermute | solution.py:458
  53.1 1.5 %output.1 = bf16[1024,256]{1,0:T(8,128)(2,1)} custom-call(s32[1,1024]{1,0:T(1,128)S(1)} %copy-done.2, bf16[512,256]{1,0:T(8,128)(2,1)S(1)} %get-tuple-element.65.own_ref, bf16[512,256]{1,0:T(8,128)(2,1)S(1)} %collective-permute-done.17.core_ref), custom_call_target="tpu_custom_call" | custom-call | tf_op jit(solution)/shard_map/output/pallas_call | solution.py:344
  54.6 3.8 %collective-permute-done.16.theirs_ref = bf16[9,128,128]{2,1,0:T(8,128)(2,1)S(1)} collective-permute-done((bf16[9,128,128]{2,1,0:T(8,128)(2,1)S(1)}, bf16[9,128,128]{2,1,0:T(8,128)(2,1)S(1)}, u32[]{:S(2)}, u32[]{:S(2)}) %collective-permute-start.16) | collective-permute-done | bytes 294944 | tf_op jit(solution)/shard_map/ppermute | solution.py:377
  58.6 1.7 %collective-permute-done.21.core_ref = bf16[12,128,128]{2,1,0:T(8,128)(2,1)S(1)} collective-permute-done((bf16[12,128,128]{2,1,0:T(8,128)(2,1)S(1)}, bf16[12,128,128]{2,1,0:T(8,128)(2,1)S(1)}, u32[]{:S(2)}, u32[]{:S(2)}) %collective-permute-start.21) | collective-permute-done | bytes 393248 | tf_op jit(solution)/shard_map/ppermute | solution.py:374
  60.3 1.7 %restore.1 = (bf16[1024,256]{1,0:T(8,128)(2,1)}, f32[256,256]{1,0:T(8,128)}, f32[256,256]{1,0:T(8,128)}) custom-call(s32[1,1024]{1,0:T(1,128)S(1)} %copy-done.2, bf16[12,128,128]{2,1,0:T(8,128)(2,1)S(1)} %total.1.own_ref, bf16[12,128,128]{2,1,0:T(8,128)(2,1)S(1)} %collective-permute-done.21.core_ref), custom_call_target="tpu_custom_call" | custom-call | tf_op jit(solution)/shard_map/restore/pallas_call | solution.py:344
  (37 shorter events, 4.2 us)
Async XLA Ops:
  3.0 7.8 %collective-permute-start.1 = (bf16[48,128,128]{2,1,0:T(8,128)(2,1)}, bf16[48,128,128]{2,1,0:T(8,128)(2,1)S(1)}, u32[]{:S(2)}, u32[]{:S(2)}) collective-permute-start(bf16[48,128,128]{2,1,0:T(8,128)(2,1)} %bitcast.7), channel_id=1, source_target_pairs={{0,1},{1,0},{2,3},{3,2},{4,5},{5,4},{6,7},{7,6},{8,9},{9,8},{10,11... | collective-permute-start | bytes 4718600 | tf_op jit(solution)/shard_map/ppermute | solution.py:374
  3.5 15.1 %collective-permute-start.2 = (bf16[1024,128]{1,0:T(8,128)(2,1)S(1)}, bf16[1024,128]{1,0:T(8,128)(2,1)S(1)}, u32[]{:S(2)}, u32[]{:S(2)}) collective-permute-start(bf16[1024,128]{1,0:T(8,128)(2,1)S(1)} %get-tuple-element.40.own_ref), channel_id=1, source_target_pairs={{0,4},{4,0},{8,12},{12,8},{16,20},{20,16},{24,28},{28,24},{1,5},{5... | collective-permute-start | bytes 786440 | tf_op jit(solution)/shard_map/ppermute | solution.py:368
  6.1 12.5 %collective-permute-start.3 = (bf16[1024,128]{1,0:T(8,128)(2,1)S(1)}, bf16[1024,128]{1,0:T(8,128)(2,1)S(1)}, u32[]{:S(2)}, u32[]{:S(2)}) collective-permute-start(bf16[1024,128]{1,0:T(8,128)(2,1)S(1)} %get-tuple-element.40.own_ref), channel_id=1, source_target_pairs={{0,28},{4,8},{8,4},{12,16},{16,12},{20,24},{24,20},{28,0},{1,29},{... | collective-permute-start | bytes 786440 | tf_op jit(solution)/shard_map/ppermute | solution.py:371
  9.7 1.2 %collective-permute-start = (s32[8,128]{1,0:T(8,128)S(1)}, s32[8,128]{1,0:T(8,128)S(1)}, u32[]{:S(2)}, u32[]{:S(2)}) collective-permute-start(s32[8,128]{1,0:T(8,128)S(1)} %get-tuple-element.39.mine), channel_id=1, source_target_pairs={{0,1},{1,0},{2,3},{3,2},{4,5},{5,4},{6,7},{7,6},{8,9},{9,8},{10,11... | collective-permute-start | bytes 12296 | tf_op jit(solution)/shard_map/ppermute | solution.py:374
  18.6 10.3 %copy-start.1 = (bf16[256,256]{1,0:T(8,128)(2,1)S(1)}, bf16[256,256]{1,0:T(8,128)(2,1)}, u32[]{:S(2)}) copy-start(bf16[256,256]{1,0:T(8,128)(2,1)} %wn_ref.1) | copy-start | bytes 393220
  20.5 2.0 %collective-permute-start.4 = (bf16[512,128]{1,0:T(8,128)(2,1)S(1)}, bf16[512,128]{1,0:T(8,128)(2,1)S(1)}, u32[]{:S(2)}, u32[]{:S(2)}) collective-permute-start(bf16[512,128]{1,0:T(8,128)(2,1)S(1)} %get-tuple-element.45), channel_id=1, source_target_pairs={{0,1},{1,0},{2,3},{3,2},{4,5},{5,4},{6,7},{7,6},{8,9},{9,8},{10,11... | collective-permute-start | bytes 393224 | tf_op jit(solution)/shard_map/ppermute | solution.py:374
  20.6 6.4 %collective-permute-start.5 = (bf16[512,128]{1,0:T(8,128)(2,1)S(1)}, bf16[512,128]{1,0:T(8,128)(2,1)S(1)}, u32[]{:S(2)}, u32[]{:S(2)}) collective-permute-start(bf16[512,128]{1,0:T(8,128)(2,1)S(1)} %get-tuple-element.44.own_ref), channel_id=1, source_target_pairs={{0,2},{1,3},{2,0},{3,1},{4,6},{5,7},{6,4},{7,5},{8,10},{9,11},{10,... | collective-permute-start | bytes 393224 | tf_op jit(solution)/shard_map/ppermute | solution.py:377
  22.5 6.5 %collective-permute-start.6 = (bf16[512,128]{1,0:T(8,128)(2,1)S(1)}, bf16[512,128]{1,0:T(8,128)(2,1)S(1)}, u32[]{:S(2)}, u32[]{:S(2)}) collective-permute-start(bf16[512,128]{1,0:T(8,128)(2,1)S(1)} %get-tuple-element.45), channel_id=1, source_target_pairs={{0,3},{1,2},{2,1},{3,0},{4,7},{5,6},{6,5},{7,4},{8,11},{9,10},{10,... | collective-permute-start | bytes 393224 | tf_op jit(solution)/shard_map/ppermute | solution.py:380
  29.6 3.0 %collective-permute-start.7 = (bf16[128,512]{1,0:T(8,128)(2,1)S(1)}, bf16[128,512]{1,0:T(8,128)(2,1)S(1)}, u32[]{:S(2)}, u32[]{:S(2)}) collective-permute-start(bf16[128,512]{1,0:T(8,128)(2,1)S(1)} %get-tuple-element.51), channel_id=1, source_target_pairs={{0,1},{1,0},{2,3},{3,2},{4,5},{5,4},{6,7},{7,6},{8,9},{9,8},{10,11... | collective-permute-start | bytes 393224 | tf_op jit(solution)/shard_map/ppermute | solution.py:374
  30.5 9.3 %collective-permute-start.10 = (bf16[64,256]{1,0:T(8,128)(2,1)S(1)}, bf16[64,256]{1,0:T(8,128)(2,1)S(1)}, u32[]{:S(2)}, u32[]{:S(2)}) collective-permute-start(bf16[64,256]{1,0:T(8,128)(2,1)S(1)} %get-tuple-element.59), channel_id=1, source_target_pairs={{0,1},{1,0},{2,3},{3,2},{4,5},{5,4},{6,7},{7,6},{8,9},{9,8},{10,11... | collective-permute-start | bytes 98312 | tf_op jit(solution)/shard_map/ppermute | solution.py:374
  30.9 8.9 %collective-permute-start.11 = (bf16[64,256]{1,0:T(8,128)(2,1)S(1)}, bf16[64,256]{1,0:T(8,128)(2,1)S(1)}, u32[]{:S(2)}, u32[]{:S(2)}) collective-permute-start(bf16[64,256]{1,0:T(8,128)(2,1)S(1)} %get-tuple-element.60), channel_id=1, source_target_pairs={{0,4},{1,5},{2,6},{3,7},{4,0},{5,1},{6,2},{7,3},{8,12},{9,13},{10,... | collective-permute-start | bytes 98312 | tf_op jit(solution)/shard_map/ppermute | solution.py:458
  32.6 7.2 %collective-permute-start.12 = (bf16[64,256]{1,0:T(8,128)(2,1)S(1)}, bf16[64,256]{1,0:T(8,128)(2,1)S(1)}, u32[]{:S(2)}, u32[]{:S(2)}) collective-permute-start(bf16[64,256]{1,0:T(8,128)(2,1)S(1)} %get-tuple-element.61), channel_id=1, source_target_pairs={{0,5},{1,4},{2,7},{3,6},{4,1},{5,0},{6,3},{7,2},{8,13},{9,12},{10,... | collective-permute-start | bytes 98312 | tf_op jit(solution)/shard_map/ppermute | solution.py:458
  32.6 20.5 %copy-start.2 = (s32[1,1024]{1,0:T(1,128)S(1)}, s32[1,1024]{1,0:T(1,128)}, u32[]{:S(2)}) copy-start(s32[1,1024]{1,0:T(1,128)} %order_ref.3) | copy-start | bytes 12292
  34.6 14.3 %collective-permute-start.8 = (bf16[8,128,128]{2,1,0:T(8,128)(2,1)S(1)}, bf16[8,128,128]{2,1,0:T(8,128)(2,1)S(1)}, u32[]{:S(2)}, u32[]{:S(2)}) collective-permute-start(bf16[8,128,128]{2,1,0:T(8,128)(2,1)S(1)} %get-tuple-element.53), channel_id=1, source_target_pairs={{0,4},{4,0},{8,12},{12,8},{16,20},{20,16},{24,28},{28,24},{1,5},{5... | collective-permute-start | bytes 786440 | tf_op jit(solution)/shard_map/ppermute | solution.py:368
  36.2 12.7 %collective-permute-start.9 = (bf16[8,128,128]{2,1,0:T(8,128)(2,1)S(1)}, bf16[8,128,128]{2,1,0:T(8,128)(2,1)S(1)}, u32[]{:S(2)}, u32[]{:S(2)}) collective-permute-start(bf16[8,128,128]{2,1,0:T(8,128)(2,1)S(1)} %get-tuple-element.54), channel_id=1, source_target_pairs={{0,28},{4,8},{8,4},{12,16},{16,12},{20,24},{24,20},{28,0},{1,29},{... | collective-permute-start | bytes 786440 | tf_op jit(solution)/shard_map/ppermute | solution.py:371
  39.8 7.4 %collective-permute-start.13 = (bf16[64,256]{1,0:T(8,128)(2,1)S(1)}, bf16[64,256]{1,0:T(8,128)(2,1)S(1)}, u32[]{:S(2)}, u32[]{:S(2)}) collective-permute-start(bf16[64,256]{1,0:T(8,128)(2,1)S(1)} %add_convert_fusion.g0_ref), channel_id=1, source_target_pairs={{0,8},{4,12},{8,0},{12,4},{16,24},{20,28},{24,16},{28,20},{1,9},{5... | collective-permute-start | bytes 98312 | tf_op jit(solution)/shard_map/ppermute | solution.py:484
  39.9 7.7 %collective-permute-start.14 = (bf16[64,256]{1,0:T(8,128)(2,1)S(1)}, bf16[64,256]{1,0:T(8,128)(2,1)S(1)}, u32[]{:S(2)}, u32[]{:S(2)}) collective-permute-start(bf16[64,256]{1,0:T(8,128)(2,1)S(1)} %add_convert_fusion.g0_ref), channel_id=1, source_target_pairs={{0,16},{4,20},{8,24},{12,28},{16,0},{20,4},{24,8},{28,12},{1,17},{... | collective-permute-start | bytes 98312 | tf_op jit(solution)/shard_map/ppermute | solution.py:484
  40.9 7.9 %collective-permute-start.15 = (bf16[64,256]{1,0:T(8,128)(2,1)S(1)}, bf16[64,256]{1,0:T(8,128)(2,1)S(1)}, u32[]{:S(2)}, u32[]{:S(2)}) collective-permute-start(bf16[64,256]{1,0:T(8,128)(2,1)S(1)} %add_convert_fusion.g0_ref), channel_id=1, source_target_pairs={{0,24},{4,28},{8,16},{12,20},{16,8},{20,12},{24,0},{28,4},{1,25},{... | collective-permute-start | bytes 98312 | tf_op jit(solution)/shard_map/ppermute | solution.py:484
  49.0 9.4 %collective-permute-start.16 = (bf16[9,128,128]{2,1,0:T(8,128)(2,1)S(1)}, bf16[9,128,128]{2,1,0:T(8,128)(2,1)S(1)}, u32[]{:S(2)}, u32[]{:S(2)}) collective-permute-start(bf16[9,128,128]{2,1,0:T(8,128)(2,1)S(1)} %get-tuple-element.64.mine_ref), channel_id=1, source_target_pairs={{0,2},{1,3},{2,0},{3,1},{4,6},{5,7},{6,4},{7,5},{8,10},{9,11},{10,... | collective-permute-start | bytes 884744 | tf_op jit(solution)/shard_map/ppermute | solution.py:377
  50.8 2.3 %collective-permute-start.17 = (bf16[512,256]{1,0:T(8,128)(2,1)S(1)}, bf16[512,256]{1,0:T(8,128)(2,1)S(1)}, u32[]{:S(2)}, u32[]{:S(2)}) collective-permute-start(bf16[512,256]{1,0:T(8,128)(2,1)S(1)} %get-tuple-element.65.own_ref), channel_id=1, source_target_pairs={{0,1},{1,0},{2,3},{3,2},{4,5},{5,4},{6,7},{7,6},{8,9},{9,8},{10,11... | collective-permute-start | bytes 786440 | tf_op jit(solution)/shard_map/ppermute | solution.py:374
  50.8 7.6 %collective-permute-start.18 = (f32[128,512]{1,0:T(8,128)S(1)}, f32[128,512]{1,0:T(8,128)S(1)}, u32[]{:S(2)}, u32[]{:S(2)}) collective-permute-start(f32[128,512]{1,0:T(8,128)S(1)} %get-tuple-element.69), channel_id=1, source_target_pairs={{0,1},{1,0},{2,3},{3,2},{4,5},{5,4},{6,7},{7,6},{8,9},{9,8},{10,11... | collective-permute-start | bytes 786440 | tf_op jit(solution)/shard_map/ppermute | solution.py:374
  51.3 7.1 %collective-permute-start.19 = (bf16[128,128]{1,0:T(8,128)(2,1)S(1)}, bf16[128,128]{1,0:T(8,128)(2,1)S(1)}, u32[]{:S(2)}, u32[]{:S(2)}) collective-permute-start(bf16[128,128]{1,0:T(8,128)(2,1)S(1)} %get-tuple-element.70), channel_id=1, source_target_pairs={{0,4},{1,5},{2,6},{3,7},{4,0},{5,1},{6,2},{7,3},{8,12},{9,13},{10,... | collective-permute-start | bytes 98312 | tf_op jit(solution)/shard_map/ppermute | solution.py:458
  52.8 5.6 %collective-permute-start.20 = (bf16[128,128]{1,0:T(8,128)(2,1)S(1)}, bf16[128,128]{1,0:T(8,128)(2,1)S(1)}, u32[]{:S(2)}, u32[]{:S(2)}) collective-permute-start(bf16[128,128]{1,0:T(8,128)(2,1)S(1)} %get-tuple-element.70), channel_id=1, source_target_pairs={{0,6},{1,7},{2,4},{3,5},{4,2},{5,3},{6,0},{7,1},{8,14},{9,15},{10,... | collective-permute-start | bytes 98312 | tf_op jit(solution)/shard_map/ppermute | solution.py:458
  58.5 1.8 %collective-permute-start.21 = (bf16[12,128,128]{2,1,0:T(8,128)(2,1)S(1)}, bf16[12,128,128]{2,1,0:T(8,128)(2,1)S(1)}, u32[]{:S(2)}, u32[]{:S(2)}) collective-permute-start(bf16[12,128,128]{2,1,0:T(8,128)(2,1)S(1)} %total.1.own_ref), channel_id=1, source_target_pairs={{0,1},{1,0},{2,3},{3,2},{4,5},{5,4},{6,7},{7,6},{8,9},{9,8},{10,11... | collective-permute-start | bytes 1179656 | tf_op jit(solution)/shard_map/ppermute | solution.py:374
  (1 other events, 9.4 us)

commit v5 on v4

--- a/solution.py
+++ b/solution.py
@@ -53,33 +53,25 @@
     return pl.ds(pl.multiple_of(index * T, T), T)
 
 
-def reorder_kernel(order_hbm, x_hbm, rows_hbm, cols_hbm, count_ref, out_ref, idx_ref, order, x, rows, cols, sems):
-    c = core_of()
+def reorder_kernel(order_hbm, x_hbm, out_ref, order, x, sems):
     total = out_ref.shape[0]
-    copies = [
-        pltpu.make_async_copy(src, dst, sems.at[i])
-        for i, (src, dst) in enumerate(
-            (
-                (order_hbm, order),
-                (x_hbm.at[:, half_lanes(c)], x),
-                (rows_hbm, rows),
-                (cols_hbm, cols),
-            )
-        )
-    ]
-    for copy in copies:
-        copy.start()
-    copies[0].wait()
+    first = pltpu.make_async_copy(order_hbm, order, sems.at[0])
+    second = pltpu.make_async_copy(x_hbm.at[:, half_lanes(core_of())], x, sems.at[1])
+    first.start()
+    second.start()
+    first.wait()
     columns = [order_column(order[i : i + 1, :].astype(F32)) for i in range(total // T)]
-    copies[1].wait()
+    second.wait()
     for i in range(total // T):
         out_ref[i * T : (i + 1) * T, :] = mm(onehot_rows(columns[i], total), x[...]).astype(BF)
-    for copy in copies[2:]:
-        copy.wait()
-    slots = rows.shape[1]
+
+
+def index_kernel(count_ref, rows_ref, cols_ref, after_ref, idx_ref):
+    del after_ref
+    slots = rows_ref.shape[1]
     idx_ref[...] = jnp.zeros_like(idx_ref)
-    idx_ref[0:1, 0:slots] = rows[...]
-    idx_ref[1:2, 0:slots] = cols[...]
+    idx_ref[0:1, 0:slots] = rows_ref[...]
+    idx_ref[1:2, 0:slots] = cols_ref[...]
     idx_ref[2:3, :] = jnp.full((1, T), count_ref[0, 0], jnp.int32)
 
 
@@ -205,7 +197,7 @@
 
 
 def dense_kernel(
-    own_ref, core_ref, y_ref, diag_ref, hs_ref, gh_ref, sc_ref, sr_ref, wn_ref,
+    own_ref, y_ref, diag_ref, core_ref, hs_ref, gh_ref, sc_ref, sr_ref, wn_ref,
     act_ref, gp_ref, agg_ref, keep_ref, send_ref,
 ):
     c = core_of()
@@ -302,9 +294,9 @@
     out_ref[tiles + 2 * (1 - y) + 1 - x] = near_y_ref[...]
 
 
-def restore_kernel(order_ref, own_ref, core_ref, out_ref, self_ref, neigh_ref, full):
+def restore_kernel(order_ref, own_ref, core_ref, out_hbm, self_hbm, neigh_hbm, full, out, self_sum, neigh_sum, sems):
     c = core_of()
-    rows = out_ref.shape[0]
+    rows = out.shape[0]
     half = T // 2
     for side, ref in ((c, own_ref), (1 - c, core_ref)):
         for x in range(2):
@@ -312,15 +304,26 @@
             for i in range(2):
                 cut = slice(i * T, (i + 1) * T)
                 rows_of = slice(i * half, (i + 1) * half)
-                self_ref[at, cut] = ref[rows // T + x, rows_of, :].astype(F32)
-                neigh_ref[at, cut] = ref[rows // T + 2 + x, rows_of, :].astype(F32)
+                self_sum[at, cut] = ref[rows // T + x, rows_of, :].astype(F32)
+                neigh_sum[at, cut] = ref[rows // T + 2 + x, rows_of, :].astype(F32)
+    copies = [
+        pltpu.make_async_copy(self_sum, self_hbm, sems.at[0]),
+        pltpu.make_async_copy(neigh_sum, neigh_hbm, sems.at[1]),
+    ]
+    for copy in copies:
+        copy.start()
     for i in range(rows // T):
         cut = slice(i * T, (i + 1) * T)
         full[pl.ds(pl.multiple_of(c * T, T), T), cut] = own_ref[i]
         full[pl.ds(pl.multiple_of((1 - c) * T, T), T), cut] = core_ref[i]
     for j in range(rows // 256):
+        here = slice(j * 256, (j + 1) * 256)
         hot = onehot_inverse(order_ref[...], j * 256, 256)
-        out_ref[j * 256 : (j + 1) * 256, :] = mm_nt(hot, full[...]).astype(BF)
+        out[here, :] = mm_nt(hot, full[...]).astype(BF)
+        copies.append(pltpu.make_async_copy(out.at[here], out_hbm.at[here], sems.at[2 + j]))
+        copies[-1].start()
+    for copy in copies:
+        copy.wait()
 
 
 def output_kernel(order_ref, own_ref, core_ref, out_ref, full):
@@ -391,24 +394,24 @@
     smem = pltpu.SMEM
     dma = pltpu.SemaphoreType.DMA
 
-    feats_c, mine = call(
+    feats_c = call(
         reorder_kernel,
-        [((rows, T), BF), ((8, T), jnp.int32)],
-        [order8, features, stay(tile_rows[0]), stay(tile_cols[0]), tile_count],
-        spaces={0: hbm, 1: hbm, 2: hbm, 3: hbm, 4: smem},
-        scratch=[
-            pltpu.VMEM((tiles, T), jnp.int32),
-            pltpu.VMEM((rows, T), BF),
-            pltpu.VMEM((1, slots), jnp.int32),
-            pltpu.VMEM((1, slots), jnp.int32),
-            dma((4,)),
-        ],
+        [((rows, T), BF)],
+        [order8, features],
+        spaces={0: hbm, 1: hbm},
+        scratch=[pltpu.VMEM((tiles, T), jnp.int32), pltpu.VMEM((rows, T), BF), dma((2,))],
         name="reorder",
+    )
+    mine = call(
+        index_kernel,
+        [((8, T), jnp.int32)],
+        [tile_count, stay(tile_rows[0]), stay(tile_cols[0]), feats_c],
+        spaces={0: smem, 3: pl.ANY},
+        name="index",
     )
     near = swap_near(feats_c)
     far = swap_far(feats_c)
     theirs = swap_core(mine)
-    va, _ = lax.optimization_barrier((va, feats_c))
     vb = swap_core(va)
     va = stay(va)
     xh, gh, hs, sc, sr, both, pairs = call(
@@ -442,7 +445,7 @@
     act, gp, agg, s_keep, s_send = call(
         dense_kernel,
         [((half, width), BF), ((half, width), BF), ((half, width), BF), ((T, half), BF), ((T, half), BF)],
-        [here, from_core, from_y, from_diag, hs, gh, sc, sr, w_neigh],
+        [here, from_y, from_diag, from_core, hs, gh, sc, sr, w_neigh],
         name="dense",
     )
     s_other = swap_core(s_send)
@@ -503,7 +506,14 @@
         restore_kernel,
         [((rows, width), BF), ((width, width), F32), ((width, width), F32)],
         [order, total, total_core],
-        scratch=[pltpu.VMEM((width, rows), BF)],
+        out_spaces={i: pl.ANY for i in range(3)},
+        scratch=[
+            pltpu.VMEM((width, rows), BF),
+            pltpu.VMEM((rows, width), BF),
+            pltpu.VMEM((width, width), F32),
+            pltpu.VMEM((width, width), F32),
+            dma((2 + rows // 256,)),
+        ],
         name="restore",
     )
     return output, grad_features, grad_self, grad_neigh

time: 62.2 us -> 60.7 us (0.976)
  waiting for transfers between devices: 19.6 us -> 17.4 us
    ppermute x2, waiting for transfers between devices: 2.02 us -> 1 us  [swap_near(): return lax.ppermute(x, 'blk', [(b, b ^ 1) for b in range(blocks)])]
    ppermute x2, waiting for transfers between devices: 8.23 us -> 7.42 us  [swap_y(): return lax.ppermute(x, 'rep', [(r, r ^ 2) for r in range(reps)])]
    pallas_call x10 -> x11, Pallas kernels: 16.1 us -> 16.6 us  [call(): pl.pallas_call(kernel, out_shape=shapes[0] if single else shapes, in_spec...]
  transfers between devices with their start and end apart: 22 -> 22, of which waited for: 10 -> 10; matrix products, arithmetic and copies ran while one was open for 0% -> 0% of each run, Pallas kernels for 16% -> 20%
where the time goes in v5:
time: 60.7 us; the launch traced here: 60.5 us
  starting transfers between devices  25 us (41%)
  waiting for transfers between devices  17.4 us (29%)
  Pallas kernels  16.6 us (27%)
  between operations  1.4 us (2%)
    pallas_call x11, Pallas kernels, call(): pl.pallas_call(kernel, out_shape=shapes[0] if single else shapes, in_spec...  16.6 us
    ppermute x2, waiting for transfers between devices, swap_y(): return lax.ppermute(x, 'rep', [(r, r ^ 2) for r in range(reps)])  7.42 us
    ppermute x2, starting transfers between devices, swap_far(): lax.ppermute(x, 'blk', [(b, (b + 2 * (b % 2) - 1) % blocks) for b in rang...  7.14 us
    ppermute x3, starting transfers between devices, shards(): lax.ppermute(g, 'blk', [(b, b ^ k << at) for b in range(blocks)])  4.44 us
    ppermute x3, waiting for transfers between devices, shards(): lax.ppermute(g, 'blk', [(b, b ^ k << at) for b in range(blocks)])  4.35 us
    ppermute x2, starting transfers between devices, swap_near(): return lax.ppermute(x, 'blk', [(b, b ^ 1) for b in range(blocks)])  4.19 us
    ppermute x4, starting transfers between devices, swap_pair(): return lax.ppermute(x, ('blk', 'rep'), pairs_of)  3.7 us
    ppermute x2, starting transfers between devices, swap_y(): return lax.ppermute(x, 'rep', [(r, r ^ 2) for r in range(reps)])  3.39 us
  transfers between devices with their start and end apart: 22, of which 10 were waited for; matrix products, arithmetic and copies ran while one was open for 0% of the time, Pallas kernels for 20%

profile of v5, /device:TPU:0, one launch (start us, length us, event | category | flops | bytes accessed | tf_op | source)
XLA Modules:
  0.0 60.5 jit_solution(13573837781424324234)
XLA Ops:
  1.1 1.7 %reorder.1.after_ref.own_ref = bf16[1024,128]{1,0:T(8,128)(2,1)S(1)} custom-call(s32[8,128]{1,0:T(8,128)} %bitcast.5, bf16[1024,256]{1,0:T(8,128)(2,1)} %x_ref.1), custom_call_target="tpu_custom_call" | custom-call | tf_op jit(solution)/shard_map/reorder/pallas_call | solution.py:347
  2.8 2.6 %collective-permute-start.2 = (bf16[1024,128]{1,0:T(8,128)(2,1)S(1)}, bf16[1024,128]{1,0:T(8,128)(2,1)S(1)}, u32[]{:S(2)}, u32[]{:S(2)}) collective-permute-start(bf16[1024,128]{1,0:T(8,128)(2,1)S(1)} %reorder.1.after_ref.own_ref), channel_id=1, source_target_pairs={{0,4},{4,0},{8,12},{12,8},{16,20},{20,16},{24,28},{28,24},{1,5},{5... | collective-permute-start | bytes 786440 | tf_op jit(solution)/shard_map/ppermute | solution.py:371
  5.4 3.6 %collective-permute-start.3 = (bf16[1024,128]{1,0:T(8,128)(2,1)S(1)}, bf16[1024,128]{1,0:T(8,128)(2,1)S(1)}, u32[]{:S(2)}, u32[]{:S(2)}) collective-permute-start(bf16[1024,128]{1,0:T(8,128)(2,1)S(1)} %reorder.1.after_ref.own_ref), channel_id=1, source_target_pairs={{0,28},{4,8},{8,4},{12,16},{16,12},{20,24},{24,20},{28,0},{1,29},{... | collective-permute-start | bytes 786440 | tf_op jit(solution)/shard_map/ppermute | solution.py:374
  10.3 1.2 %collective-permute-done.theirs = s32[8,128]{1,0:T(8,128)S(1)} collective-permute-done((s32[8,128]{1,0:T(8,128)S(1)}, s32[8,128]{1,0:T(8,128)S(1)}, u32[]{:S(2)}, u32[]{:S(2)}) %collective-permute-start) | collective-permute-done | bytes 4128 | tf_op jit(solution)/shard_map/ppermute | solution.py:377
  11.5 5.8 %prepare.1 = (bf16[512,256]{1,0:T(8,128)(2,1)S(1)}, bf16[512,256]{1,0:T(8,128)(2,1)S(1)}, f32[512,256]{1,0:T(8,128)S(1)}, f32[512,128]{1,0:T(8,128)S(1)}, f32[8,...) custom-call(s32[8,128]{1,0:T(8,128)S(1)} %index.1.mine, ...), custom_call_target="tpu_custom_call" | custom-call | tf_op jit(solution)/shard_map/prepare/pallas_call | solution.py:347
  17.3 0.7 %collective-permute-done.2.near_ref = bf16[1024,128]{1,0:T(8,128)(2,1)S(1)} collective-permute-done((bf16[1024,128]{1,0:T(8,128)(2,1)S(1)}, bf16[1024,128]{1,0:T(8,128)(2,1)S(1)}, u32[]{:S(2)}, u32[]{:S(2)}) %collective-permute-start.2) | collective-permute-done | bytes 262176 | tf_op jit(solution)/shard_map/ppermute | solution.py:371
  18.0 1.9 %gather.1 = (bf16[512,128]{1,0:T(8,128)(2,1)S(1)}, bf16[512,128]{1,0:T(8,128)(2,1)S(1)}) custom-call(s32[8,128]{1,0:T(8,128)S(1)} %get-tuple-element.36.pairs_ref, bf16[1024,128]{1,0:T(8,128)(2,1)S(1)} %collective-permute-done.2.near_ref, bf16[1024,128]{1,0:T(8,128)(2,1)S(1)} %reorder.1.after_ref.own_ref, ...), custom_call_target="tpu_custom_call" | custom-call | tf_op jit(solution)/shard_map/gather/pallas_call | solution.py:347
  19.9 1.8 %collective-permute-start.4 = (bf16[512,128]{1,0:T(8,128)(2,1)S(1)}, bf16[512,128]{1,0:T(8,128)(2,1)S(1)}, u32[]{:S(2)}, u32[]{:S(2)}) collective-permute-start(bf16[512,128]{1,0:T(8,128)(2,1)S(1)} %get-tuple-element.38.own_ref), channel_id=1, source_target_pairs={{0,2},{1,3},{2,0},{3,1},{4,6},{5,7},{6,4},{7,5},{8,10},{9,11},{10,... | collective-permute-start | bytes 393224 | tf_op jit(solution)/shard_map/ppermute | solution.py:380
  22.1 3.7 %collective-permute-done.4.y_ref = bf16[512,128]{1,0:T(8,128)(2,1)S(1)} collective-permute-done((bf16[512,128]{1,0:T(8,128)(2,1)S(1)}, bf16[512,128]{1,0:T(8,128)(2,1)S(1)}, u32[]{:S(2)}, u32[]{:S(2)}) %collective-permute-start.4) | collective-permute-done | bytes 131104 | tf_op jit(solution)/shard_map/ppermute | solution.py:380
  25.8 1.7 %collective-permute-done.5.diag_ref = bf16[512,128]{1,0:T(8,128)(2,1)S(1)} collective-permute-done((bf16[512,128]{1,0:T(8,128)(2,1)S(1)}, bf16[512,128]{1,0:T(8,128)(2,1)S(1)}, u32[]{:S(2)}, u32[]{:S(2)}) %collective-permute-start.5) | collective-permute-done | bytes 131104 | tf_op jit(solution)/shard_map/ppermute | solution.py:383
  29.5 1.5 %collective-permute-start.11 = (bf16[64,256]{1,0:T(8,128)(2,1)S(1)}, bf16[64,256]{1,0:T(8,128)(2,1)S(1)}, u32[]{:S(2)}, u32[]{:S(2)}) collective-permute-start(bf16[64,256]{1,0:T(8,128)(2,1)S(1)} %get-tuple-element.54), channel_id=1, source_target_pairs={{0,4},{1,5},{2,6},{3,7},{4,0},{5,1},{6,2},{7,3},{8,12},{9,13},{10,... | collective-permute-start | bytes 98312 | tf_op jit(solution)/shard_map/ppermute | solution.py:461
  31.2 2.0 %scatter.1 = (bf16[8,128,128]{2,1,0:T(8,128)(2,1)S(1)}, f32[8,128,128]{2,1,0:T(8,128)S(1)}, bf16[8,128,128]{2,1,0:T(8,128)(2,1)S(1)}) custom-call(s32[8,128]{1,0:T(8,128)S(1)} %get-tuple-element.36.pairs_ref, bf16[128,512]{1,0:T(8,128)(2,1)S(1)} %get-tuple-element.44.mine_ref, bf16[128,512]{1,0:T(8,128)(2,1)S(1)} %collective-permute-done.7.theirs_ref, ...), custom_call_target="tpu_custom_call" | custom-call | tf_op jit(solution)/shard_map/scatter/pallas_call | solution.py:347
  33.2 1.6 %collective-permute-start.8 = (bf16[8,128,128]{2,1,0:T(8,128)(2,1)S(1)}, bf16[8,128,128]{2,1,0:T(8,128)(2,1)S(1)}, u32[]{:S(2)}, u32[]{:S(2)}) collective-permute-start(bf16[8,128,128]{2,1,0:T(8,128)(2,1)S(1)} %get-tuple-element.47), channel_id=1, source_target_pairs={{0,4},{4,0},{8,12},{12,8},{16,20},{20,16},{24,28},{28,24},{1,5},{5... | collective-permute-start | bytes 786440 | tf_op jit(solution)/shard_map/ppermute | solution.py:371
  34.8 3.6 %collective-permute-start.9 = (bf16[8,128,128]{2,1,0:T(8,128)(2,1)S(1)}, bf16[8,128,128]{2,1,0:T(8,128)(2,1)S(1)}, u32[]{:S(2)}, u32[]{:S(2)}) collective-permute-start(bf16[8,128,128]{2,1,0:T(8,128)(2,1)S(1)} %get-tuple-element.48), channel_id=1, source_target_pairs={{0,28},{4,8},{8,4},{12,16},{16,12},{20,24},{24,20},{28,0},{1,29},{... | collective-permute-start | bytes 786440 | tf_op jit(solution)/shard_map/ppermute | solution.py:374
  38.5 1.0 %collective-permute-start.14 = (bf16[64,256]{1,0:T(8,128)(2,1)S(1)}, bf16[64,256]{1,0:T(8,128)(2,1)S(1)}, u32[]{:S(2)}, u32[]{:S(2)}) collective-permute-start(bf16[64,256]{1,0:T(8,128)(2,1)S(1)} %add_convert_fusion.g0_ref), channel_id=1, source_target_pairs={{0,16},{4,20},{8,24},{12,28},{16,0},{20,4},{24,8},{28,12},{1,17},{... | collective-permute-start | bytes 98312 | tf_op jit(solution)/shard_map/ppermute | solution.py:487
  39.5 3.4 %collective-permute-start.15 = (bf16[64,256]{1,0:T(8,128)(2,1)S(1)}, bf16[64,256]{1,0:T(8,128)(2,1)S(1)}, u32[]{:S(2)}, u32[]{:S(2)}) collective-permute-start(bf16[64,256]{1,0:T(8,128)(2,1)S(1)} %add_convert_fusion.g0_ref), channel_id=1, source_target_pairs={{0,24},{4,28},{8,16},{12,20},{16,8},{20,12},{24,0},{28,4},{1,25},{... | collective-permute-start | bytes 98312 | tf_op jit(solution)/shard_map/ppermute | solution.py:487
  42.9 2.8 %collective-permute-done.13.g1_ref = bf16[64,256]{1,0:T(8,128)(2,1)S(1)} collective-permute-done((bf16[64,256]{1,0:T(8,128)(2,1)S(1)}, bf16[64,256]{1,0:T(8,128)(2,1)S(1)}, u32[]{:S(2)}, u32[]{:S(2)}) %collective-permute-start.13) | collective-permute-done | bytes 32800 | tf_op jit(solution)/shard_map/ppermute | solution.py:487
  46.0 1.3 %collective-permute-done.15.g3_ref = bf16[64,256]{1,0:T(8,128)(2,1)S(1)} collective-permute-done((bf16[64,256]{1,0:T(8,128)(2,1)S(1)}, bf16[64,256]{1,0:T(8,128)(2,1)S(1)}, u32[]{:S(2)}, u32[]{:S(2)}) %collective-permute-start.15) | collective-permute-done | bytes 32800 | tf_op jit(solution)/shard_map/ppermute | solution.py:487
  47.6 1.6 %collective-permute-start.16 = (bf16[9,128,128]{2,1,0:T(8,128)(2,1)S(1)}, bf16[9,128,128]{2,1,0:T(8,128)(2,1)S(1)}, u32[]{:S(2)}, u32[]{:S(2)}) collective-permute-start(bf16[9,128,128]{2,1,0:T(8,128)(2,1)S(1)} %get-tuple-element.58.mine_ref), channel_id=1, source_target_pairs={{0,2},{1,3},{2,0},{3,1},{4,6},{5,7},{6,4},{7,5},{8,10},{9,11},{10,... | collective-permute-start | bytes 884744 | tf_op jit(solution)/shard_map/ppermute | solution.py:380
  49.7 1.5 %collective-permute-start.19 = (bf16[128,128]{1,0:T(8,128)(2,1)S(1)}, bf16[128,128]{1,0:T(8,128)(2,1)S(1)}, u32[]{:S(2)}, u32[]{:S(2)}) collective-permute-start(bf16[128,128]{1,0:T(8,128)(2,1)S(1)} %get-tuple-element.64), channel_id=1, source_target_pairs={{0,4},{1,5},{2,6},{3,7},{4,0},{5,1},{6,2},{7,3},{8,12},{9,13},{10,... | collective-permute-start | bytes 98312 | tf_op jit(solution)/shard_map/ppermute | solution.py:461
  51.7 1.5 %output.1 = bf16[1024,256]{1,0:T(8,128)(2,1)} custom-call(s32[1,1024]{1,0:T(1,128)S(1)} %copy-done.2, bf16[512,256]{1,0:T(8,128)(2,1)S(1)} %get-tuple-element.59.own_ref, bf16[512,256]{1,0:T(8,128)(2,1)S(1)} %collective-permute-done.17.core_ref), custom_call_target="tpu_custom_call" | custom-call | tf_op jit(solution)/shard_map/output/pallas_call | solution.py:347
  53.2 3.7 %collective-permute-done.16.theirs_ref = bf16[9,128,128]{2,1,0:T(8,128)(2,1)S(1)} collective-permute-done((bf16[9,128,128]{2,1,0:T(8,128)(2,1)S(1)}, bf16[9,128,128]{2,1,0:T(8,128)(2,1)S(1)}, u32[]{:S(2)}, u32[]{:S(2)}) %collective-permute-start.16) | collective-permute-done | bytes 294944 | tf_op jit(solution)/shard_map/ppermute | solution.py:380
  57.2 1.7 %collective-permute-done.21.core_ref = bf16[12,128,128]{2,1,0:T(8,128)(2,1)S(1)} collective-permute-done((bf16[12,128,128]{2,1,0:T(8,128)(2,1)S(1)}, bf16[12,128,128]{2,1,0:T(8,128)(2,1)S(1)}, u32[]{:S(2)}, u32[]{:S(2)}) %collective-permute-start.21) | collective-permute-done | bytes 393248 | tf_op jit(solution)/shard_map/ppermute | solution.py:377
  58.9 1.6 %restore.1 = (bf16[1024,256]{1,0:T(8,128)(2,1)}, f32[256,256]{1,0:T(8,128)}, f32[256,256]{1,0:T(8,128)}) custom-call(s32[1,1024]{1,0:T(1,128)S(1)} %copy-done.2, bf16[12,128,128]{2,1,0:T(8,128)(2,1)S(1)} %total.1.own_ref, bf16[12,128,128]{2,1,0:T(8,128)(2,1)S(1)} %collective-permute-done.21.core_ref), custom_call_target="tpu_custom_call" | custom-call | tf_op jit(solution)/shard_map/restore/pallas_call | solution.py:347
  (38 shorter events, 5.8 us)
Async XLA Ops:
  0.6 10.9 %collective-permute-start.1 = (bf16[48,128,128]{2,1,0:T(8,128)(2,1)}, bf16[48,128,128]{2,1,0:T(8,128)(2,1)S(1)}, u32[]{:S(2)}, u32[]{:S(2)}) collective-permute-start(bf16[48,128,128]{2,1,0:T(8,128)(2,1)} %bitcast.7), channel_id=1, source_target_pairs={{0,1},{1,0},{2,3},{3,2},{4,5},{5,4},{6,7},{7,6},{8,9},{9,8},{10,11... | collective-permute-start | bytes 4718600 | tf_op jit(solution)/shard_map/ppermute | solution.py:377
  2.8 15.2 %collective-permute-start.2 = (bf16[1024,128]{1,0:T(8,128)(2,1)S(1)}, bf16[1024,128]{1,0:T(8,128)(2,1)S(1)}, u32[]{:S(2)}, u32[]{:S(2)}) collective-permute-start(bf16[1024,128]{1,0:T(8,128)(2,1)S(1)} %reorder.1.after_ref.own_ref), channel_id=1, source_target_pairs={{0,4},{4,0},{8,12},{12,8},{16,20},{20,16},{24,28},{28,24},{1,5},{5... | collective-permute-start | bytes 786440 | tf_op jit(solution)/shard_map/ppermute | solution.py:371
  5.4 12.6 %collective-permute-start.3 = (bf16[1024,128]{1,0:T(8,128)(2,1)S(1)}, bf16[1024,128]{1,0:T(8,128)(2,1)S(1)}, u32[]{:S(2)}, u32[]{:S(2)}) collective-permute-start(bf16[1024,128]{1,0:T(8,128)(2,1)S(1)} %reorder.1.after_ref.own_ref), channel_id=1, source_target_pairs={{0,28},{4,8},{8,4},{12,16},{16,12},{20,24},{24,20},{28,0},{1,29},{... | collective-permute-start | bytes 786440 | tf_op jit(solution)/shard_map/ppermute | solution.py:374
  10.3 1.2 %collective-permute-start = (s32[8,128]{1,0:T(8,128)S(1)}, s32[8,128]{1,0:T(8,128)S(1)}, u32[]{:S(2)}, u32[]{:S(2)}) collective-permute-start(s32[8,128]{1,0:T(8,128)S(1)} %index.1.mine), channel_id=1, source_target_pairs={{0,1},{1,0},{2,3},{3,2},{4,5},{5,4},{6,7},{7,6},{8,9},{9,8},{10,11... | collective-permute-start | bytes 12296 | tf_op jit(solution)/shard_map/ppermute | solution.py:377
  18.0 9.6 %copy-start.1 = (bf16[256,256]{1,0:T(8,128)(2,1)S(1)}, bf16[256,256]{1,0:T(8,128)(2,1)}, u32[]{:S(2)}) copy-start(bf16[256,256]{1,0:T(8,128)(2,1)} %wn_ref.1) | copy-start | bytes 393220
  19.9 5.9 %collective-permute-start.4 = (bf16[512,128]{1,0:T(8,128)(2,1)S(1)}, bf16[512,128]{1,0:T(8,128)(2,1)S(1)}, u32[]{:S(2)}, u32[]{:S(2)}) collective-permute-start(bf16[512,128]{1,0:T(8,128)(2,1)S(1)} %get-tuple-element.38.own_ref), channel_id=1, source_target_pairs={{0,2},{1,3},{2,0},{3,1},{4,6},{5,7},{6,4},{7,5},{8,10},{9,11},{10,... | collective-permute-start | bytes 393224 | tf_op jit(solution)/shard_map/ppermute | solution.py:380
  21.8 5.8 %collective-permute-start.5 = (bf16[512,128]{1,0:T(8,128)(2,1)S(1)}, bf16[512,128]{1,0:T(8,128)(2,1)S(1)}, u32[]{:S(2)}, u32[]{:S(2)}) collective-permute-start(bf16[512,128]{1,0:T(8,128)(2,1)S(1)} %get-tuple-element.39), channel_id=1, source_target_pairs={{0,3},{1,2},{2,1},{3,0},{4,7},{5,6},{6,5},{7,4},{8,11},{9,10},{10,... | collective-permute-start | bytes 393224 | tf_op jit(solution)/shard_map/ppermute | solution.py:383
  21.8 5.8 %collective-permute-start.6 = (bf16[512,128]{1,0:T(8,128)(2,1)S(1)}, bf16[512,128]{1,0:T(8,128)(2,1)S(1)}, u32[]{:S(2)}, u32[]{:S(2)}) collective-permute-start(bf16[512,128]{1,0:T(8,128)(2,1)S(1)} %get-tuple-element.39), channel_id=1, source_target_pairs={{0,1},{1,0},{2,3},{3,2},{4,5},{5,4},{6,7},{7,6},{8,9},{9,8},{10,11... | collective-permute-start | bytes 393224 | tf_op jit(solution)/shard_map/ppermute | solution.py:377
  28.2 3.0 %collective-permute-start.7 = (bf16[128,512]{1,0:T(8,128)(2,1)S(1)}, bf16[128,512]{1,0:T(8,128)(2,1)S(1)}, u32[]{:S(2)}, u32[]{:S(2)}) collective-permute-start(bf16[128,512]{1,0:T(8,128)(2,1)S(1)} %get-tuple-element.45), channel_id=1, source_target_pairs={{0,1},{1,0},{2,3},{3,2},{4,5},{5,4},{6,7},{7,6},{8,9},{9,8},{10,11... | collective-permute-start | bytes 393224 | tf_op jit(solution)/shard_map/ppermute | solution.py:377
  29.3 9.1 %collective-permute-start.10 = (bf16[64,256]{1,0:T(8,128)(2,1)S(1)}, bf16[64,256]{1,0:T(8,128)(2,1)S(1)}, u32[]{:S(2)}, u32[]{:S(2)}) collective-permute-start(bf16[64,256]{1,0:T(8,128)(2,1)S(1)} %get-tuple-element.53), channel_id=1, source_target_pairs={{0,1},{1,0},{2,3},{3,2},{4,5},{5,4},{6,7},{7,6},{8,9},{9,8},{10,11... | collective-permute-start | bytes 98312 | tf_op jit(solution)/shard_map/ppermute | solution.py:377
  29.5 8.9 %collective-permute-start.11 = (bf16[64,256]{1,0:T(8,128)(2,1)S(1)}, bf16[64,256]{1,0:T(8,128)(2,1)S(1)}, u32[]{:S(2)}, u32[]{:S(2)}) collective-permute-start(bf16[64,256]{1,0:T(8,128)(2,1)S(1)} %get-tuple-element.54), channel_id=1, source_target_pairs={{0,4},{1,5},{2,6},{3,7},{4,0},{5,1},{6,2},{7,3},{8,12},{9,13},{10,... | collective-permute-start | bytes 98312 | tf_op jit(solution)/shard_map/ppermute | solution.py:461
  31.0 7.4 %collective-permute-start.12 = (bf16[64,256]{1,0:T(8,128)(2,1)S(1)}, bf16[64,256]{1,0:T(8,128)(2,1)S(1)}, u32[]{:S(2)}, u32[]{:S(2)}) collective-permute-start(bf16[64,256]{1,0:T(8,128)(2,1)S(1)} %get-tuple-element.55), channel_id=1, source_target_pairs={{0,5},{1,4},{2,7},{3,6},{4,1},{5,0},{6,3},{7,2},{8,13},{9,12},{10,... | collective-permute-start | bytes 98312 | tf_op jit(solution)/shard_map/ppermute | solution.py:461
  31.2 20.5 %copy-start.2 = (s32[1,1024]{1,0:T(1,128)S(1)}, s32[1,1024]{1,0:T(1,128)}, u32[]{:S(2)}) copy-start(s32[1,1024]{1,0:T(1,128)} %order_ref.3) | copy-start | bytes 12292
  33.2 14.3 %collective-permute-start.8 = (bf16[8,128,128]{2,1,0:T(8,128)(2,1)S(1)}, bf16[8,128,128]{2,1,0:T(8,128)(2,1)S(1)}, u32[]{:S(2)}, u32[]{:S(2)}) collective-permute-start(bf16[8,128,128]{2,1,0:T(8,128)(2,1)S(1)} %get-tuple-element.47), channel_id=1, source_target_pairs={{0,4},{4,0},{8,12},{12,8},{16,20},{20,16},{24,28},{28,24},{1,5},{5... | collective-permute-start | bytes 786440 | tf_op jit(solution)/shard_map/ppermute | solution.py:371
  34.8 12.7 %collective-permute-start.9 = (bf16[8,128,128]{2,1,0:T(8,128)(2,1)S(1)}, bf16[8,128,128]{2,1,0:T(8,128)(2,1)S(1)}, u32[]{:S(2)}, u32[]{:S(2)}) collective-permute-start(bf16[8,128,128]{2,1,0:T(8,128)(2,1)S(1)} %get-tuple-element.48), channel_id=1, source_target_pairs={{0,28},{4,8},{8,4},{12,16},{16,12},{20,24},{24,20},{28,0},{1,29},{... | collective-permute-start | bytes 786440 | tf_op jit(solution)/shard_map/ppermute | solution.py:374
  38.4 7.2 %collective-permute-start.13 = (bf16[64,256]{1,0:T(8,128)(2,1)S(1)}, bf16[64,256]{1,0:T(8,128)(2,1)S(1)}, u32[]{:S(2)}, u32[]{:S(2)}) collective-permute-start(bf16[64,256]{1,0:T(8,128)(2,1)S(1)} %add_convert_fusion.g0_ref), channel_id=1, source_target_pairs={{0,8},{4,12},{8,0},{12,4},{16,24},{20,28},{24,16},{28,20},{1,9},{5... | collective-permute-start | bytes 98312 | tf_op jit(solution)/shard_map/ppermute | solution.py:487
  38.5 7.5 %collective-permute-start.14 = (bf16[64,256]{1,0:T(8,128)(2,1)S(1)}, bf16[64,256]{1,0:T(8,128)(2,1)S(1)}, u32[]{:S(2)}, u32[]{:S(2)}) collective-permute-start(bf16[64,256]{1,0:T(8,128)(2,1)S(1)} %add_convert_fusion.g0_ref), channel_id=1, source_target_pairs={{0,16},{4,20},{8,24},{12,28},{16,0},{20,4},{24,8},{28,12},{1,17},{... | collective-permute-start | bytes 98312 | tf_op jit(solution)/shard_map/ppermute | solution.py:487
  39.5 7.7 %collective-permute-start.15 = (bf16[64,256]{1,0:T(8,128)(2,1)S(1)}, bf16[64,256]{1,0:T(8,128)(2,1)S(1)}, u32[]{:S(2)}, u32[]{:S(2)}) collective-permute-start(bf16[64,256]{1,0:T(8,128)(2,1)S(1)} %add_convert_fusion.g0_ref), channel_id=1, source_target_pairs={{0,24},{4,28},{8,16},{12,20},{16,8},{20,12},{24,0},{28,4},{1,25},{... | collective-permute-start | bytes 98312 | tf_op jit(solution)/shard_map/ppermute | solution.py:487
  47.6 9.3 %collective-permute-start.16 = (bf16[9,128,128]{2,1,0:T(8,128)(2,1)S(1)}, bf16[9,128,128]{2,1,0:T(8,128)(2,1)S(1)}, u32[]{:S(2)}, u32[]{:S(2)}) collective-permute-start(bf16[9,128,128]{2,1,0:T(8,128)(2,1)S(1)} %get-tuple-element.58.mine_ref), channel_id=1, source_target_pairs={{0,2},{1,3},{2,0},{3,1},{4,6},{5,7},{6,4},{7,5},{8,10},{9,11},{10,... | collective-permute-start | bytes 884744 | tf_op jit(solution)/shard_map/ppermute | solution.py:380
  49.2 2.5 %collective-permute-start.17 = (bf16[512,256]{1,0:T(8,128)(2,1)S(1)}, bf16[512,256]{1,0:T(8,128)(2,1)S(1)}, u32[]{:S(2)}, u32[]{:S(2)}) collective-permute-start(bf16[512,256]{1,0:T(8,128)(2,1)S(1)} %get-tuple-element.59.own_ref), channel_id=1, source_target_pairs={{0,1},{1,0},{2,3},{3,2},{4,5},{5,4},{6,7},{7,6},{8,9},{9,8},{10,11... | collective-permute-start | bytes 786440 | tf_op jit(solution)/shard_map/ppermute | solution.py:377
  49.2 7.8 %collective-permute-start.18 = (f32[128,512]{1,0:T(8,128)S(1)}, f32[128,512]{1,0:T(8,128)S(1)}, u32[]{:S(2)}, u32[]{:S(2)}) collective-permute-start(f32[128,512]{1,0:T(8,128)S(1)} %get-tuple-element.63), channel_id=1, source_target_pairs={{0,1},{1,0},{2,3},{3,2},{4,5},{5,4},{6,7},{7,6},{8,9},{9,8},{10,11... | collective-permute-start | bytes 786440 | tf_op jit(solution)/shard_map/ppermute | solution.py:377
  49.7 7.3 %collective-permute-start.19 = (bf16[128,128]{1,0:T(8,128)(2,1)S(1)}, bf16[128,128]{1,0:T(8,128)(2,1)S(1)}, u32[]{:S(2)}, u32[]{:S(2)}) collective-permute-start(bf16[128,128]{1,0:T(8,128)(2,1)S(1)} %get-tuple-element.64), channel_id=1, source_target_pairs={{0,4},{1,5},{2,6},{3,7},{4,0},{5,1},{6,2},{7,3},{8,12},{9,13},{10,... | collective-permute-start | bytes 98312 | tf_op jit(solution)/shard_map/ppermute | solution.py:461
  51.2 5.8 %collective-permute-start.20 = (bf16[128,128]{1,0:T(8,128)(2,1)S(1)}, bf16[128,128]{1,0:T(8,128)(2,1)S(1)}, u32[]{:S(2)}, u32[]{:S(2)}) collective-permute-start(bf16[128,128]{1,0:T(8,128)(2,1)S(1)} %get-tuple-element.64), channel_id=1, source_target_pairs={{0,6},{1,7},{2,4},{3,5},{4,2},{5,3},{6,0},{7,1},{8,14},{9,15},{10,... | collective-permute-start | bytes 98312 | tf_op jit(solution)/shard_map/ppermute | solution.py:461
  57.1 1.8 %collective-permute-start.21 = (bf16[12,128,128]{2,1,0:T(8,128)(2,1)S(1)}, bf16[12,128,128]{2,1,0:T(8,128)(2,1)S(1)}, u32[]{:S(2)}, u32[]{:S(2)}) collective-permute-start(bf16[12,128,128]{2,1,0:T(8,128)(2,1)S(1)} %total.1.own_ref), channel_id=1, source_target_pairs={{0,1},{1,0},{2,3},{3,2},{4,5},{5,4},{6,7},{7,6},{8,9},{9,8},{10,11... | collective-permute-start | bytes 1179656 | tf_op jit(solution)/shard_map/ppermute | solution.py:377
  (1 other events, 8.7 us)

commit v6 on v5

--- a/solution.py
+++ b/solution.py
@@ -75,72 +75,54 @@
     idx_ref[2:3, :] = jnp.full((1, T), count_ref[0, 0], jnp.int32)
 
 
-def pair_slots(mine, theirs, slots, row_tiles, pairs, out_ref, pending):
-    dead = row_tiles
-    nothing = 2 * slots
-    beyond = 3 * row_tiles
-
-    def clear(i, _):
-        out_ref[0, i] = dead
-        out_ref[1, i] = nothing
-        out_ref[2, i] = nothing
-        out_ref[3, i] = beyond
-        out_ref[4, i] = beyond
-        return 0
-
-    lax.fori_loop(0, pairs, clear, 0)
-    for r in range(row_tiles + 1):
-        pending[0, r] = -1
-        pending[1, r] = beyond
-
-    def emit(n, r, a, b, col_a, col_b):
-        out_ref[0, n] = r
-        out_ref[1, n] = a
-        out_ref[2, n] = b
-        out_ref[3, n] = col_a
-        out_ref[4, n] = col_b
-
-    n = jnp.int32(0)
-    for base, idx in ((0, mine), (slots, theirs)):
-        count = idx[2, 0]
-
-        def place(s, n, base=base, idx=idx, count=count):
-            live = s < count
-            r = jnp.where(live, idx[0, s], dead)
-            col = jnp.where(live, idx[1, s], beyond)
-            first = pending[0, r]
-            whole = first >= 0
-
-            @pl.when(whole)
-            def _():
-                emit(n, r, first, base + s, pending[1, r], col)
-                pending[0, r] = -1
-
-            @pl.when(jnp.logical_not(whole))
-            def _():
-                pending[0, r] = base + s
-                pending[1, r] = col
-
-            return n + whole.astype(jnp.int32)
-
-        n = lax.fori_loop(0, slots, place, n)
-
-    def rest(r, n):
-        first = pending[0, r]
-        left = first >= 0
-
-        @pl.when(left)
-        def _():
-            emit(n, r, first, nothing, pending[1, r], beyond)
-
-        return n + left.astype(jnp.int32)
-
-    lax.fori_loop(0, row_tiles, rest, n)
+def pair_slots(mine, theirs, slots, row_tiles, out_ref):
+    lane = lax.broadcasted_iota(jnp.int32, mine.shape, 1)
+    here = lane < slots
+    theirs = pltpu.roll(theirs, slots, 1)
+    both = jnp.where(here, mine, theirs)
+    live = jnp.where(here, lane, lane - slots) < jnp.broadcast_to(both[2:3, :], lane.shape)
+    live = jnp.logical_and(live, lane < 2 * slots)
+    rows = jnp.where(live, jnp.broadcast_to(both[0:1, :], lane.shape), row_tiles).astype(F32)
+
+    def along(x):
+        return jnp.broadcast_to(x, (T, T))
+
+    def down(x):
+        return jnp.transpose(along(x))
+
+    def parity(x):
+        return x - 2.0 * jnp.floor(x * 0.5)
+
+    def count(where):
+        return jnp.sum(jnp.where(where, 1.0, 0.0), axis=0, keepdims=True)
+
+    first = lax.broadcasted_iota(jnp.int32, (T, T), 0).astype(F32)
+    second = lax.broadcasted_iota(jnp.int32, (T, T), 1).astype(F32)
+    row_a, row_d = along(rows[0:1, :]), down(rows[0:1, :])
+    rank = count(jnp.logical_and(row_a == row_d, first < second))
+    rank_d = down(rank)
+    odd = parity(rank_d) > 0.5
+    before = count(jnp.logical_and(row_d < row_a, jnp.logical_not(odd)))
+    place = jnp.where(rows[0:1, :] < row_tiles, before + jnp.floor(rank * 0.5), -1.0)
+    hit = down(place) == second
+    col_d = down(both[1:2, :].astype(F32))
+
+    def pick(value, default, which):
+        chosen = jnp.logical_and(hit, which)
+        return (default + jnp.sum(jnp.where(chosen, value - default, 0.0), axis=0, keepdims=True)).astype(jnp.int32)
+
+    even = jnp.logical_not(odd)
+    out_ref[...] = jnp.zeros_like(out_ref)
+    out_ref[0:1, :] = pick(row_d, float(row_tiles), even)
+    out_ref[1:2, :] = pick(first, 2.0 * slots, even)
+    out_ref[2:3, :] = pick(first, 2.0 * slots, odd)
+    out_ref[3:4, :] = pick(col_d, 3.0 * row_tiles, even)
+    out_ref[4:5, :] = pick(col_d, 3.0 * row_tiles, odd)
 
 
 def prepare_kernel(
     mine, theirs, va_any, vb_any, order_ref, degree_ref, x_ref, g_ref, w_ref,
-    xh_ref, gh_ref, hs_ref, sc_ref, sr_ref, tiles_ref, pairs_ref, pending, sems,
+    xh_ref, gh_ref, hs_ref, sc_ref, sr_ref, tiles_ref, pairs_ref, sems,
 ):
     c = core_of()
     rows = x_ref.shape[0]
@@ -152,7 +134,7 @@
     for copy in copies:
         copy.start()
     tiles_ref[2 * slots] = jnp.zeros((T, T), BF)
-    pair_slots(mine, theirs, slots, rows // T, slots + rows // T // 2, pairs_ref, pending)
+    pair_slots(mine[...], theirs[...], slots, rows // T, pairs_ref)
     tiles = rows // T // 2
     deg = jnp.broadcast_to(degree_ref[...].astype(F32), (8, rows)).astype(BF)
     for i in range(tiles):
@@ -218,12 +200,16 @@
     send_ref[...] = (mm_nt(wn_ref[pl.ds(pl.multiple_of((1 - c) * T, T), T), :], gp) * row).astype(BF)
 
 
-def terms_kernel(xh_ref, agg_ref, gp_ref, ws_ref, keep_ref, send_ref, *refs):
+def dself_kernel(gp_ref, ws_ref, keep_ref, send_ref):
+    c = core_of()
+    keep_ref[...] = mm_nt(ws_ref[pl.ds(pl.multiple_of(c * T, T), T), :], gp_ref[...])
+    send_ref[...] = mm_nt(ws_ref[pl.ds(pl.multiple_of((1 - c) * T, T), T), :], gp_ref[...])
+
+
+def terms_kernel(xh_ref, agg_ref, gp_ref, *refs):
     c, y = core_of(), y_of()
     term_refs, full_ref = refs[:4], refs[4]
     gp = gp_ref[...]
-    keep_ref[...] = mm_nt(ws_ref[pl.ds(pl.multiple_of(c * T, T), T), :], gp)
-    send_ref[...] = mm_nt(ws_ref[pl.ds(pl.multiple_of((1 - c) * T, T), T), :], gp)
 
     half = T // 2
     x = lax.rem(lax.axis_index("blk"), 2)
@@ -426,9 +412,8 @@
             ((8, T), jnp.int32),
         ],
         [mine, theirs, va, vb, order8, deg, features, out_grad, stay(w_self)],
-        spaces={0: smem, 1: smem, 2: pl.ANY, 3: pl.ANY},
-        out_spaces={6: smem},
-        scratch=[pltpu.SMEM((2, 16), jnp.int32), dma((2,))],
+        spaces={2: pl.ANY, 3: pl.ANY},
+        scratch=[dma((2,))],
         name="prepare",
     )
     here, other = call(
@@ -449,10 +434,10 @@
         name="dense",
     )
     s_other = swap_core(s_send)
-    d_keep, d_send, mine_near, mine_far, theirs_near, theirs_far = call(
+    mine_near, mine_far, theirs_near, theirs_far = call(
         terms_kernel,
-        [((T, half), F32), ((T, half), F32)] + [((T // 2, width), BF)] * 4,
-        [xh, agg, gp, w_self],
+        [((T // 2, width), BF)] * 4,
+        [xh, agg, gp],
         scratch=[pltpu.VMEM((T, width), F32)],
         name="terms",
     )
@@ -472,6 +457,7 @@
     )
     from_near = swap_near(near)
     from_far = swap_far(far)
+    d_keep, d_send = call(dself_kernel, [((T, half), F32)] * 2, [gp, w_self], name="dself")
     d_recv = swap_core(d_send)
     bits = blocks.bit_length() - 1
     assert blocks == 1 << bits and bits % 2 and bits > 1

time: 60.7 us -> 60.4 us (level)
  Pallas kernels: 16.6 us -> 13.7 us
  waiting for transfers between devices: 17.4 us -> 20 us
    ppermute x2, waiting for transfers between devices: 1 us -> 3.95 us  [swap_near(): return lax.ppermute(x, 'blk', [(b, b ^ 1) for b in range(blocks)])]
    pallas_call x11 -> x12, Pallas kernels: 16.6 us -> 13.7 us  [call(): pl.pallas_call(kernel, out_shape=shapes[0] if single else shapes, in_spec...]
  transfers between devices with their start and end apart: 22 -> 22, of which waited for: 10 -> 10; matrix products, arithmetic and copies ran while one was open for 0% -> 0% of each run, Pallas kernels for 20% -> 16%
where the time goes in v6:
time: 60.4 us; the launch traced here: 60.2 us
  starting transfers between devices  25.1 us (42%)
  waiting for transfers between devices  20 us (33%)
  Pallas kernels  13.7 us (23%)
  between operations  1.4 us (2%)
    pallas_call x12, Pallas kernels, call(): pl.pallas_call(kernel, out_shape=shapes[0] if single else shapes, in_spec...  13.7 us
    ppermute x2, starting transfers between devices, swap_far(): lax.ppermute(x, 'blk', [(b, (b + 2 * (b % 2) - 1) % blocks) for b in rang...  7.15 us
    ppermute x2, waiting for transfers between devices, swap_y(): return lax.ppermute(x, 'rep', [(r, r ^ 2) for r in range(reps)])  7.03 us
    ppermute x3, starting transfers between devices, shards(): lax.ppermute(g, 'blk', [(b, b ^ k << at) for b in range(blocks)])  4.44 us
    ppermute x3, waiting for transfers between devices, shards(): lax.ppermute(g, 'blk', [(b, b ^ k << at) for b in range(blocks)])  4.35 us
    ppermute x2, starting transfers between devices, swap_near(): return lax.ppermute(x, 'blk', [(b, b ^ 1) for b in range(blocks)])  4.19 us
    ppermute x2, waiting for transfers between devices, swap_near(): return lax.ppermute(x, 'blk', [(b, b ^ 1) for b in range(blocks)])  3.95 us
    ppermute x4, starting transfers between devices, swap_pair(): return lax.ppermute(x, ('blk', 'rep'), pairs_of)  3.71 us
  transfers between devices with their start and end apart: 22, of which 10 were waited for; matrix products, arithmetic and copies ran while one was open for 0% of the time, Pallas kernels for 16%

profile of v6, /device:TPU:0, one launch (start us, length us, event | category | flops | bytes accessed | tf_op | source)
XLA Modules:
  0.0 60.2 jit_solution(17853628041512109696)
XLA Ops:
  1.1 1.7 %reorder.1.after_ref.own_ref = bf16[1024,128]{1,0:T(8,128)(2,1)S(1)} custom-call(s32[8,128]{1,0:T(8,128)} %bitcast.5, bf16[1024,256]{1,0:T(8,128)(2,1)} %x_ref.1), custom_call_target="tpu_custom_call" | custom-call | tf_op jit(solution)/shard_map/reorder/pallas_call | solution.py:333
  2.8 2.6 %collective-permute-start.2 = (bf16[1024,128]{1,0:T(8,128)(2,1)S(1)}, bf16[1024,128]{1,0:T(8,128)(2,1)S(1)}, u32[]{:S(2)}, u32[]{:S(2)}) collective-permute-start(bf16[1024,128]{1,0:T(8,128)(2,1)S(1)} %reorder.1.after_ref.own_ref), channel_id=1, source_target_pairs={{0,4},{4,0},{8,12},{12,8},{16,20},{20,16},{24,28},{28,24},{1,5},{5... | collective-permute-start | bytes 786440 | tf_op jit(solution)/shard_map/ppermute | solution.py:357
  5.4 3.6 %collective-permute-start.3 = (bf16[1024,128]{1,0:T(8,128)(2,1)S(1)}, bf16[1024,128]{1,0:T(8,128)(2,1)S(1)}, u32[]{:S(2)}, u32[]{:S(2)}) collective-permute-start(bf16[1024,128]{1,0:T(8,128)(2,1)S(1)} %reorder.1.after_ref.own_ref), channel_id=1, source_target_pairs={{0,28},{4,8},{8,4},{12,16},{16,12},{20,24},{24,20},{28,0},{1,29},{... | collective-permute-start | bytes 786440 | tf_op jit(solution)/shard_map/ppermute | solution.py:360
  10.3 1.2 %collective-permute-done.theirs = s32[8,128]{1,0:T(8,128)S(1)} collective-permute-done((s32[8,128]{1,0:T(8,128)S(1)}, s32[8,128]{1,0:T(8,128)S(1)}, u32[]{:S(2)}, u32[]{:S(2)}) %collective-permute-start) | collective-permute-done | bytes 4128 | tf_op jit(solution)/shard_map/ppermute | solution.py:363
  11.5 2.8 %prepare.1 = (bf16[512,256]{1,0:T(8,128)(2,1)S(1)}, bf16[512,256]{1,0:T(8,128)(2,1)S(1)}, f32[512,256]{1,0:T(8,128)S(1)}, f32[512,128]{1,0:T(8,128)S(1)}, f32[8,...) custom-call(s32[8,128]{1,0:T(8,128)S(1)} %index.1.mine, ...), custom_call_target="tpu_custom_call" | custom-call | tf_op jit(solution)/shard_map/prepare/pallas_call | solution.py:333
  14.3 3.7 %collective-permute-done.2.near_ref = bf16[1024,128]{1,0:T(8,128)(2,1)S(1)} collective-permute-done((bf16[1024,128]{1,0:T(8,128)(2,1)S(1)}, bf16[1024,128]{1,0:T(8,128)(2,1)S(1)}, u32[]{:S(2)}, u32[]{:S(2)}) %collective-permute-start.2) | collective-permute-done | bytes 262176 | tf_op jit(solution)/shard_map/ppermute | solution.py:357
  18.0 1.9 %gather.1 = (bf16[512,128]{1,0:T(8,128)(2,1)S(1)}, bf16[512,128]{1,0:T(8,128)(2,1)S(1)}) custom-call(s32[8,128]{1,0:T(8,128)S(1)} %get-tuple-element.36.pairs_ref, bf16[1024,128]{1,0:T(8,128)(2,1)S(1)} %collective-permute-done.2.near_ref, bf16[1024,128]{1,0:T(8,128)(2,1)S(1)} %reorder.1.after_ref.own_ref, ...), custom_call_target="tpu_custom_call" | custom-call | tf_op jit(solution)/shard_map/gather/pallas_call | solution.py:333
  19.9 1.8 %collective-permute-start.4 = (bf16[512,128]{1,0:T(8,128)(2,1)S(1)}, bf16[512,128]{1,0:T(8,128)(2,1)S(1)}, u32[]{:S(2)}, u32[]{:S(2)}) collective-permute-start(bf16[512,128]{1,0:T(8,128)(2,1)S(1)} %get-tuple-element.38.own_ref), channel_id=1, source_target_pairs={{0,2},{1,3},{2,0},{3,1},{4,6},{5,7},{6,4},{7,5},{8,10},{9,11},{10,... | collective-permute-start | bytes 393224 | tf_op jit(solution)/shard_map/ppermute | solution.py:366
  22.1 3.7 %collective-permute-done.4.y_ref = bf16[512,128]{1,0:T(8,128)(2,1)S(1)} collective-permute-done((bf16[512,128]{1,0:T(8,128)(2,1)S(1)}, bf16[512,128]{1,0:T(8,128)(2,1)S(1)}, u32[]{:S(2)}, u32[]{:S(2)}) %collective-permute-start.4) | collective-permute-done | bytes 131104 | tf_op jit(solution)/shard_map/ppermute | solution.py:366
  25.8 1.7 %collective-permute-done.5.diag_ref = bf16[512,128]{1,0:T(8,128)(2,1)S(1)} collective-permute-done((bf16[512,128]{1,0:T(8,128)(2,1)S(1)}, bf16[512,128]{1,0:T(8,128)(2,1)S(1)}, u32[]{:S(2)}, u32[]{:S(2)}) %collective-permute-start.5) | collective-permute-done | bytes 131104 | tf_op jit(solution)/shard_map/ppermute | solution.py:369
  29.2 1.5 %collective-permute-start.11 = (bf16[64,256]{1,0:T(8,128)(2,1)S(1)}, bf16[64,256]{1,0:T(8,128)(2,1)S(1)}, u32[]{:S(2)}, u32[]{:S(2)}) collective-permute-start(bf16[64,256]{1,0:T(8,128)(2,1)S(1)} %get-tuple-element.54), channel_id=1, source_target_pairs={{0,4},{1,5},{2,6},{3,7},{4,0},{5,1},{6,2},{7,3},{8,12},{9,13},{10,... | collective-permute-start | bytes 98312 | tf_op jit(solution)/shard_map/ppermute | solution.py:446
  30.9 2.0 %scatter.1 = (bf16[8,128,128]{2,1,0:T(8,128)(2,1)S(1)}, f32[8,128,128]{2,1,0:T(8,128)S(1)}, bf16[8,128,128]{2,1,0:T(8,128)(2,1)S(1)}) custom-call(s32[8,128]{1,0:T(8,128)S(1)} %get-tuple-element.36.pairs_ref, bf16[128,512]{1,0:T(8,128)(2,1)S(1)} %get-tuple-element.44.mine_ref, bf16[128,512]{1,0:T(8,128)(2,1)S(1)} %collective-permute-done.7.theirs_ref, ...), custom_call_target="tpu_custom_call" | custom-call | tf_op jit(solution)/shard_map/scatter/pallas_call | solution.py:333
  32.9 1.6 %collective-permute-start.8 = (bf16[8,128,128]{2,1,0:T(8,128)(2,1)S(1)}, bf16[8,128,128]{2,1,0:T(8,128)(2,1)S(1)}, u32[]{:S(2)}, u32[]{:S(2)}) collective-permute-start(bf16[8,128,128]{2,1,0:T(8,128)(2,1)S(1)} %get-tuple-element.47), channel_id=1, source_target_pairs={{0,4},{4,0},{8,12},{12,8},{16,20},{20,16},{24,28},{28,24},{1,5},{5... | collective-permute-start | bytes 786440 | tf_op jit(solution)/shard_map/ppermute | solution.py:357
  34.5 3.6 %collective-permute-start.9 = (bf16[8,128,128]{2,1,0:T(8,128)(2,1)S(1)}, bf16[8,128,128]{2,1,0:T(8,128)(2,1)S(1)}, u32[]{:S(2)}, u32[]{:S(2)}) collective-permute-start(bf16[8,128,128]{2,1,0:T(8,128)(2,1)S(1)} %get-tuple-element.48), channel_id=1, source_target_pairs={{0,28},{4,8},{8,4},{12,16},{16,12},{20,24},{24,20},{28,0},{1,29},{... | collective-permute-start | bytes 786440 | tf_op jit(solution)/shard_map/ppermute | solution.py:360
  38.2 1.0 %collective-permute-start.14 = (bf16[64,256]{1,0:T(8,128)(2,1)S(1)}, bf16[64,256]{1,0:T(8,128)(2,1)S(1)}, u32[]{:S(2)}, u32[]{:S(2)}) collective-permute-start(bf16[64,256]{1,0:T(8,128)(2,1)S(1)} %add_convert_fusion.g0_ref), channel_id=1, source_target_pairs={{0,16},{4,20},{8,24},{12,28},{16,0},{20,4},{24,8},{28,12},{1,17},{... | collective-permute-start | bytes 98312 | tf_op jit(solution)/shard_map/ppermute | solution.py:473
  39.2 3.4 %collective-permute-start.15 = (bf16[64,256]{1,0:T(8,128)(2,1)S(1)}, bf16[64,256]{1,0:T(8,128)(2,1)S(1)}, u32[]{:S(2)}, u32[]{:S(2)}) collective-permute-start(bf16[64,256]{1,0:T(8,128)(2,1)S(1)} %add_convert_fusion.g0_ref), channel_id=1, source_target_pairs={{0,24},{4,28},{8,16},{12,20},{16,8},{20,12},{24,0},{28,4},{1,25},{... | collective-permute-start | bytes 98312 | tf_op jit(solution)/shard_map/ppermute | solution.py:473
  42.6 2.7 %collective-permute-done.13.g1_ref = bf16[64,256]{1,0:T(8,128)(2,1)S(1)} collective-permute-done((bf16[64,256]{1,0:T(8,128)(2,1)S(1)}, bf16[64,256]{1,0:T(8,128)(2,1)S(1)}, u32[]{:S(2)}, u32[]{:S(2)}) %collective-permute-start.13) | collective-permute-done | bytes 32800 | tf_op jit(solution)/shard_map/ppermute | solution.py:473
  45.7 1.3 %collective-permute-done.15.g3_ref = bf16[64,256]{1,0:T(8,128)(2,1)S(1)} collective-permute-done((bf16[64,256]{1,0:T(8,128)(2,1)S(1)}, bf16[64,256]{1,0:T(8,128)(2,1)S(1)}, u32[]{:S(2)}, u32[]{:S(2)}) %collective-permute-start.15) | collective-permute-done | bytes 32800 | tf_op jit(solution)/shard_map/ppermute | solution.py:473
  47.3 1.6 %collective-permute-start.16 = (bf16[9,128,128]{2,1,0:T(8,128)(2,1)S(1)}, bf16[9,128,128]{2,1,0:T(8,128)(2,1)S(1)}, u32[]{:S(2)}, u32[]{:S(2)}) collective-permute-start(bf16[9,128,128]{2,1,0:T(8,128)(2,1)S(1)} %get-tuple-element.58.mine_ref), channel_id=1, source_target_pairs={{0,2},{1,3},{2,0},{3,1},{4,6},{5,7},{6,4},{7,5},{8,10},{9,11},{10,... | collective-permute-start | bytes 884744 | tf_op jit(solution)/shard_map/ppermute | solution.py:366
  49.8 1.5 %collective-permute-start.19 = (bf16[128,128]{1,0:T(8,128)(2,1)S(1)}, bf16[128,128]{1,0:T(8,128)(2,1)S(1)}, u32[]{:S(2)}, u32[]{:S(2)}) collective-permute-start(bf16[128,128]{1,0:T(8,128)(2,1)S(1)} %get-tuple-element.64), channel_id=1, source_target_pairs={{0,4},{1,5},{2,6},{3,7},{4,0},{5,1},{6,2},{7,3},{8,12},{9,13},{10,... | collective-permute-start | bytes 98312 | tf_op jit(solution)/shard_map/ppermute | solution.py:446
  51.8 1.5 %output.1 = bf16[1024,256]{1,0:T(8,128)(2,1)} custom-call(s32[1,1024]{1,0:T(1,128)S(1)} %copy-done.2, bf16[512,256]{1,0:T(8,128)(2,1)S(1)} %get-tuple-element.59.own_ref, bf16[512,256]{1,0:T(8,128)(2,1)S(1)} %collective-permute-done.17.core_ref), custom_call_target="tpu_custom_call" | custom-call | tf_op jit(solution)/shard_map/output/pallas_call | solution.py:333
  53.3 3.3 %collective-permute-done.16.theirs_ref = bf16[9,128,128]{2,1,0:T(8,128)(2,1)S(1)} collective-permute-done((bf16[9,128,128]{2,1,0:T(8,128)(2,1)S(1)}, bf16[9,128,128]{2,1,0:T(8,128)(2,1)S(1)}, u32[]{:S(2)}, u32[]{:S(2)}) %collective-permute-start.16) | collective-permute-done | bytes 294944 | tf_op jit(solution)/shard_map/ppermute | solution.py:366
  56.9 1.7 %collective-permute-done.21.core_ref = bf16[12,128,128]{2,1,0:T(8,128)(2,1)S(1)} collective-permute-done((bf16[12,128,128]{2,1,0:T(8,128)(2,1)S(1)}, bf16[12,128,128]{2,1,0:T(8,128)(2,1)S(1)}, u32[]{:S(2)}, u32[]{:S(2)}) %collective-permute-start.21) | collective-permute-done | bytes 393248 | tf_op jit(solution)/shard_map/ppermute | solution.py:363
  58.6 1.6 %restore.1 = (bf16[1024,256]{1,0:T(8,128)(2,1)}, f32[256,256]{1,0:T(8,128)}, f32[256,256]{1,0:T(8,128)}) custom-call(s32[1,1024]{1,0:T(1,128)S(1)} %copy-done.2, bf16[12,128,128]{2,1,0:T(8,128)(2,1)S(1)} %total.1.own_ref, bf16[12,128,128]{2,1,0:T(8,128)(2,1)S(1)} %collective-permute-done.21.core_ref), custom_call_target="tpu_custom_call" | custom-call | tf_op jit(solution)/shard_map/restore/pallas_call | solution.py:333
  (39 shorter events, 5.9 us)
Async XLA Ops:
  0.6 10.9 %collective-permute-start.1 = (bf16[48,128,128]{2,1,0:T(8,128)(2,1)}, bf16[48,128,128]{2,1,0:T(8,128)(2,1)S(1)}, u32[]{:S(2)}, u32[]{:S(2)}) collective-permute-start(bf16[48,128,128]{2,1,0:T(8,128)(2,1)} %bitcast.7), channel_id=1, source_target_pairs={{0,1},{1,0},{2,3},{3,2},{4,5},{5,4},{6,7},{7,6},{8,9},{9,8},{10,11... | collective-permute-start | bytes 4718600 | tf_op jit(solution)/shard_map/ppermute | solution.py:363
  2.8 15.2 %collective-permute-start.2 = (bf16[1024,128]{1,0:T(8,128)(2,1)S(1)}, bf16[1024,128]{1,0:T(8,128)(2,1)S(1)}, u32[]{:S(2)}, u32[]{:S(2)}) collective-permute-start(bf16[1024,128]{1,0:T(8,128)(2,1)S(1)} %reorder.1.after_ref.own_ref), channel_id=1, source_target_pairs={{0,4},{4,0},{8,12},{12,8},{16,20},{20,16},{24,28},{28,24},{1,5},{5... | collective-permute-start | bytes 786440 | tf_op jit(solution)/shard_map/ppermute | solution.py:357
  5.4 12.6 %collective-permute-start.3 = (bf16[1024,128]{1,0:T(8,128)(2,1)S(1)}, bf16[1024,128]{1,0:T(8,128)(2,1)S(1)}, u32[]{:S(2)}, u32[]{:S(2)}) collective-permute-start(bf16[1024,128]{1,0:T(8,128)(2,1)S(1)} %reorder.1.after_ref.own_ref), channel_id=1, source_target_pairs={{0,28},{4,8},{8,4},{12,16},{16,12},{20,24},{24,20},{28,0},{1,29},{... | collective-permute-start | bytes 786440 | tf_op jit(solution)/shard_map/ppermute | solution.py:360
  10.3 1.2 %collective-permute-start = (s32[8,128]{1,0:T(8,128)S(1)}, s32[8,128]{1,0:T(8,128)S(1)}, u32[]{:S(2)}, u32[]{:S(2)}) collective-permute-start(s32[8,128]{1,0:T(8,128)S(1)} %index.1.mine), channel_id=1, source_target_pairs={{0,1},{1,0},{2,3},{3,2},{4,5},{5,4},{6,7},{7,6},{8,9},{9,8},{10,11... | collective-permute-start | bytes 12296 | tf_op jit(solution)/shard_map/ppermute | solution.py:363
  19.9 5.9 %collective-permute-start.4 = (bf16[512,128]{1,0:T(8,128)(2,1)S(1)}, bf16[512,128]{1,0:T(8,128)(2,1)S(1)}, u32[]{:S(2)}, u32[]{:S(2)}) collective-permute-start(bf16[512,128]{1,0:T(8,128)(2,1)S(1)} %get-tuple-element.38.own_ref), channel_id=1, source_target_pairs={{0,2},{1,3},{2,0},{3,1},{4,6},{5,7},{6,4},{7,5},{8,10},{9,11},{10,... | collective-permute-start | bytes 393224 | tf_op jit(solution)/shard_map/ppermute | solution.py:366
  21.8 5.8 %collective-permute-start.5 = (bf16[512,128]{1,0:T(8,128)(2,1)S(1)}, bf16[512,128]{1,0:T(8,128)(2,1)S(1)}, u32[]{:S(2)}, u32[]{:S(2)}) collective-permute-start(bf16[512,128]{1,0:T(8,128)(2,1)S(1)} %get-tuple-element.39), channel_id=1, source_target_pairs={{0,3},{1,2},{2,1},{3,0},{4,7},{5,6},{6,5},{7,4},{8,11},{9,10},{10,... | collective-permute-start | bytes 393224 | tf_op jit(solution)/shard_map/ppermute | solution.py:369
  21.8 5.8 %collective-permute-start.6 = (bf16[512,128]{1,0:T(8,128)(2,1)S(1)}, bf16[512,128]{1,0:T(8,128)(2,1)S(1)}, u32[]{:S(2)}, u32[]{:S(2)}) collective-permute-start(bf16[512,128]{1,0:T(8,128)(2,1)S(1)} %get-tuple-element.39), channel_id=1, source_target_pairs={{0,1},{1,0},{2,3},{3,2},{4,5},{5,4},{6,7},{7,6},{8,9},{9,8},{10,11... | collective-permute-start | bytes 393224 | tf_op jit(solution)/shard_map/ppermute | solution.py:363
  28.2 2.7 %collective-permute-start.7 = (bf16[128,512]{1,0:T(8,128)(2,1)S(1)}, bf16[128,512]{1,0:T(8,128)(2,1)S(1)}, u32[]{:S(2)}, u32[]{:S(2)}) collective-permute-start(bf16[128,512]{1,0:T(8,128)(2,1)S(1)} %get-tuple-element.45), channel_id=1, source_target_pairs={{0,1},{1,0},{2,3},{3,2},{4,5},{5,4},{6,7},{7,6},{8,9},{9,8},{10,11... | collective-permute-start | bytes 393224 | tf_op jit(solution)/shard_map/ppermute | solution.py:363
  29.0 9.1 %collective-permute-start.10 = (bf16[64,256]{1,0:T(8,128)(2,1)S(1)}, bf16[64,256]{1,0:T(8,128)(2,1)S(1)}, u32[]{:S(2)}, u32[]{:S(2)}) collective-permute-start(bf16[64,256]{1,0:T(8,128)(2,1)S(1)} %get-tuple-element.53), channel_id=1, source_target_pairs={{0,1},{1,0},{2,3},{3,2},{4,5},{5,4},{6,7},{7,6},{8,9},{9,8},{10,11... | collective-permute-start | bytes 98312 | tf_op jit(solution)/shard_map/ppermute | solution.py:363
  29.2 8.9 %collective-permute-start.11 = (bf16[64,256]{1,0:T(8,128)(2,1)S(1)}, bf16[64,256]{1,0:T(8,128)(2,1)S(1)}, u32[]{:S(2)}, u32[]{:S(2)}) collective-permute-start(bf16[64,256]{1,0:T(8,128)(2,1)S(1)} %get-tuple-element.54), channel_id=1, source_target_pairs={{0,4},{1,5},{2,6},{3,7},{4,0},{5,1},{6,2},{7,3},{8,12},{9,13},{10,... | collective-permute-start | bytes 98312 | tf_op jit(solution)/shard_map/ppermute | solution.py:446
  30.7 7.4 %collective-permute-start.12 = (bf16[64,256]{1,0:T(8,128)(2,1)S(1)}, bf16[64,256]{1,0:T(8,128)(2,1)S(1)}, u32[]{:S(2)}, u32[]{:S(2)}) collective-permute-start(bf16[64,256]{1,0:T(8,128)(2,1)S(1)} %get-tuple-element.55), channel_id=1, source_target_pairs={{0,5},{1,4},{2,7},{3,6},{4,1},{5,0},{6,3},{7,2},{8,13},{9,12},{10,... | collective-permute-start | bytes 98312 | tf_op jit(solution)/shard_map/ppermute | solution.py:446
  30.9 18.0 %copy-start = (bf16[256,256]{1,0:T(8,128)(2,1)S(1)}, bf16[256,256]{1,0:T(8,128)(2,1)}, u32[]{:S(2)}) copy-start(bf16[256,256]{1,0:T(8,128)(2,1)} %ws_ref.1) | copy-start | bytes 393220
  32.9 18.9 %copy-start.2 = (s32[1,1024]{1,0:T(1,128)S(1)}, s32[1,1024]{1,0:T(1,128)}, u32[]{:S(2)}) copy-start(s32[1,1024]{1,0:T(1,128)} %order_ref.3) | copy-start | bytes 12292
  32.9 14.3 %collective-permute-start.8 = (bf16[8,128,128]{2,1,0:T(8,128)(2,1)S(1)}, bf16[8,128,128]{2,1,0:T(8,128)(2,1)S(1)}, u32[]{:S(2)}, u32[]{:S(2)}) collective-permute-start(bf16[8,128,128]{2,1,0:T(8,128)(2,1)S(1)} %get-tuple-element.47), channel_id=1, source_target_pairs={{0,4},{4,0},{8,12},{12,8},{16,20},{20,16},{24,28},{28,24},{1,5},{5... | collective-permute-start | bytes 786440 | tf_op jit(solution)/shard_map/ppermute | solution.py:357
  34.5 12.7 %collective-permute-start.9 = (bf16[8,128,128]{2,1,0:T(8,128)(2,1)S(1)}, bf16[8,128,128]{2,1,0:T(8,128)(2,1)S(1)}, u32[]{:S(2)}, u32[]{:S(2)}) collective-permute-start(bf16[8,128,128]{2,1,0:T(8,128)(2,1)S(1)} %get-tuple-element.48), channel_id=1, source_target_pairs={{0,28},{4,8},{8,4},{12,16},{16,12},{20,24},{24,20},{28,0},{1,29},{... | collective-permute-start | bytes 786440 | tf_op jit(solution)/shard_map/ppermute | solution.py:360
  38.1 7.2 %collective-permute-start.13 = (bf16[64,256]{1,0:T(8,128)(2,1)S(1)}, bf16[64,256]{1,0:T(8,128)(2,1)S(1)}, u32[]{:S(2)}, u32[]{:S(2)}) collective-permute-start(bf16[64,256]{1,0:T(8,128)(2,1)S(1)} %add_convert_fusion.g0_ref), channel_id=1, source_target_pairs={{0,8},{4,12},{8,0},{12,4},{16,24},{20,28},{24,16},{28,20},{1,9},{5... | collective-permute-start | bytes 98312 | tf_op jit(solution)/shard_map/ppermute | solution.py:473
  38.2 7.5 %collective-permute-start.14 = (bf16[64,256]{1,0:T(8,128)(2,1)S(1)}, bf16[64,256]{1,0:T(8,128)(2,1)S(1)}, u32[]{:S(2)}, u32[]{:S(2)}) collective-permute-start(bf16[64,256]{1,0:T(8,128)(2,1)S(1)} %add_convert_fusion.g0_ref), channel_id=1, source_target_pairs={{0,16},{4,20},{8,24},{12,28},{16,0},{20,4},{24,8},{28,12},{1,17},{... | collective-permute-start | bytes 98312 | tf_op jit(solution)/shard_map/ppermute | solution.py:473
  39.2 7.7 %collective-permute-start.15 = (bf16[64,256]{1,0:T(8,128)(2,1)S(1)}, bf16[64,256]{1,0:T(8,128)(2,1)S(1)}, u32[]{:S(2)}, u32[]{:S(2)}) collective-permute-start(bf16[64,256]{1,0:T(8,128)(2,1)S(1)} %add_convert_fusion.g0_ref), channel_id=1, source_target_pairs={{0,24},{4,28},{8,16},{12,20},{16,8},{20,12},{24,0},{28,4},{1,25},{... | collective-permute-start | bytes 98312 | tf_op jit(solution)/shard_map/ppermute | solution.py:473
  47.3 9.3 %collective-permute-start.16 = (bf16[9,128,128]{2,1,0:T(8,128)(2,1)S(1)}, bf16[9,128,128]{2,1,0:T(8,128)(2,1)S(1)}, u32[]{:S(2)}, u32[]{:S(2)}) collective-permute-start(bf16[9,128,128]{2,1,0:T(8,128)(2,1)S(1)} %get-tuple-element.58.mine_ref), channel_id=1, source_target_pairs={{0,2},{1,3},{2,0},{3,1},{4,6},{5,7},{6,4},{7,5},{8,10},{9,11},{10,... | collective-permute-start | bytes 884744 | tf_op jit(solution)/shard_map/ppermute | solution.py:366
  48.9 2.9 %collective-permute-start.17 = (bf16[512,256]{1,0:T(8,128)(2,1)S(1)}, bf16[512,256]{1,0:T(8,128)(2,1)S(1)}, u32[]{:S(2)}, u32[]{:S(2)}) collective-permute-start(bf16[512,256]{1,0:T(8,128)(2,1)S(1)} %get-tuple-element.59.own_ref), channel_id=1, source_target_pairs={{0,1},{1,0},{2,3},{3,2},{4,5},{5,4},{6,7},{7,6},{8,9},{9,8},{10,11... | collective-permute-start | bytes 786440 | tf_op jit(solution)/shard_map/ppermute | solution.py:363
  49.2 7.5 %collective-permute-start.18 = (f32[128,512]{1,0:T(8,128)S(1)}, f32[128,512]{1,0:T(8,128)S(1)}, u32[]{:S(2)}, u32[]{:S(2)}) collective-permute-start(f32[128,512]{1,0:T(8,128)S(1)} %get-tuple-element.63), channel_id=1, source_target_pairs={{0,1},{1,0},{2,3},{3,2},{4,5},{5,4},{6,7},{7,6},{8,9},{9,8},{10,11... | collective-permute-start | bytes 786440 | tf_op jit(solution)/shard_map/ppermute | solution.py:363
  49.8 6.9 %collective-permute-start.19 = (bf16[128,128]{1,0:T(8,128)(2,1)S(1)}, bf16[128,128]{1,0:T(8,128)(2,1)S(1)}, u32[]{:S(2)}, u32[]{:S(2)}) collective-permute-start(bf16[128,128]{1,0:T(8,128)(2,1)S(1)} %get-tuple-element.64), channel_id=1, source_target_pairs={{0,4},{1,5},{2,6},{3,7},{4,0},{5,1},{6,2},{7,3},{8,12},{9,13},{10,... | collective-permute-start | bytes 98312 | tf_op jit(solution)/shard_map/ppermute | solution.py:446
  51.3 5.4 %collective-permute-start.20 = (bf16[128,128]{1,0:T(8,128)(2,1)S(1)}, bf16[128,128]{1,0:T(8,128)(2,1)S(1)}, u32[]{:S(2)}, u32[]{:S(2)}) collective-permute-start(bf16[128,128]{1,0:T(8,128)(2,1)S(1)} %get-tuple-element.64), channel_id=1, source_target_pairs={{0,6},{1,7},{2,4},{3,5},{4,2},{5,3},{6,0},{7,1},{8,14},{9,15},{10,... | collective-permute-start | bytes 98312 | tf_op jit(solution)/shard_map/ppermute | solution.py:446
  56.8 1.8 %collective-permute-start.21 = (bf16[12,128,128]{2,1,0:T(8,128)(2,1)S(1)}, bf16[12,128,128]{2,1,0:T(8,128)(2,1)S(1)}, u32[]{:S(2)}, u32[]{:S(2)}) collective-permute-start(bf16[12,128,128]{2,1,0:T(8,128)(2,1)S(1)} %total.1.own_ref), channel_id=1, source_target_pairs={{0,1},{1,0},{2,3},{3,2},{4,5},{5,4},{6,7},{7,6},{8,9},{9,8},{10,11... | collective-permute-start | bytes 1179656 | tf_op jit(solution)/shard_map/ppermute | solution.py:363
  (1 other events, 9.6 us)

commit v7 on v6

--- a/solution.py
+++ b/solution.py
@@ -98,26 +98,47 @@
 
     first = lax.broadcasted_iota(jnp.int32, (T, T), 0).astype(F32)
     second = lax.broadcasted_iota(jnp.int32, (T, T), 1).astype(F32)
-    row_a, row_d = along(rows[0:1, :]), down(rows[0:1, :])
-    rank = count(jnp.logical_and(row_a == row_d, first < second))
+    cols = both[1:2, :].astype(F32)
+    own = jnp.logical_and(cols >= row_tiles, cols < 2 * row_tiles)
+    key = rows[0:1, :] + jnp.where(own, 64.0, 0.0)
+    key_a, key_d = along(key), down(key)
+    row_d, col_d = down(rows[0:1, :]), down(cols)
+    own_a, own_d = along(jnp.where(own, 1.0, 0.0)), down(jnp.where(own, 1.0, 0.0))
+    rank = count(jnp.logical_and(key_a == key_d, first < second))
     rank_d = down(rank)
     odd = parity(rank_d) > 0.5
-    before = count(jnp.logical_and(row_d < row_a, jnp.logical_not(odd)))
+    even = jnp.logical_not(odd)
+    lower = jnp.logical_and(key_d < key_a, own_d == own_a)
+    before = count(jnp.logical_and(lower, even))
     place = jnp.where(rows[0:1, :] < row_tiles, before + jnp.floor(rank * 0.5), -1.0)
     hit = down(place) == second
-    col_d = down(both[1:2, :].astype(F32))
+    alive = row_d < row_tiles
 
     def pick(value, default, which):
-        chosen = jnp.logical_and(hit, which)
-        return (default + jnp.sum(jnp.where(chosen, value - default, 0.0), axis=0, keepdims=True)).astype(jnp.int32)
-
-    even = jnp.logical_not(odd)
+        return (default + jnp.sum(jnp.where(which, value - default, 0.0), axis=0, keepdims=True)).astype(jnp.int32)
+
     out_ref[...] = jnp.zeros_like(out_ref)
-    out_ref[0:1, :] = pick(row_d, float(row_tiles), even)
-    out_ref[1:2, :] = pick(first, 2.0 * slots, even)
-    out_ref[2:3, :] = pick(first, 2.0 * slots, odd)
-    out_ref[3:4, :] = pick(col_d, 3.0 * row_tiles, even)
-    out_ref[4:5, :] = pick(col_d, 3.0 * row_tiles, odd)
+    for base, mark in ((0, 0.0), (8, 1.0)):
+        of_class = own_d == mark
+        chosen = jnp.logical_and(hit, of_class)
+        one, two = jnp.logical_and(chosen, even), jnp.logical_and(chosen, odd)
+        out_ref[base : base + 1, :] = pick(row_d, float(row_tiles), one)
+        out_ref[base + 1 : base + 2, :] = pick(first, 2.0 * slots, one)
+        out_ref[base + 2 : base + 3, :] = pick(first, 2.0 * slots, two)
+        out_ref[base + 3 : base + 4, :] = pick(col_d, 3.0 * row_tiles, one)
+        out_ref[base + 4 : base + 5, :] = pick(col_d, 3.0 * row_tiles, two)
+        pairs = count(jnp.logical_and(jnp.logical_and(of_class, alive), even))
+        out_ref[base + 5 : base + 6, :] = pairs.astype(jnp.int32)
+
+
+def for_pairs(pairs_ref, base, most, body):
+    size = (most + 3) // 4
+    for start in range(0, most, size):
+
+        @pl.when(pairs_ref[base + 5, 0] > start)
+        def _(start=start):
+            for p in range(start, min(start + size, most)):
+                body(p)
 
 
 def prepare_kernel(
@@ -156,23 +177,40 @@
     return 2 - 2 * lax.rem(lax.axis_index("blk"), 2)
 
 
-def gather_kernel(pairs_ref, near_ref, own_ref, far_ref, tiles_ref, here_ref, other_ref, win, acc):
-    c, near = core_of(), near_part()
+def gather_pair(pairs_ref, base, p, tiles_ref, window, acc):
+    left = jnp.concatenate([tiles_ref[pairs_ref[base + 1, p]], tiles_ref[pairs_ref[base + 2, p]]], axis=1)
+    right = jnp.concatenate([window(pairs_ref[base + 3, p]), window(pairs_ref[base + 4, p])], axis=0)
+    acc[pairs_ref[base, p]] += mm(left, right)
+
+
+def gather_own_kernel(pairs_ref, own_ref, tiles_ref, acc, win):
     rows = own_ref.shape[0]
     tiles = rows // T
+    win[0:rows, :] = own_ref[...]
+    win[rows : rows + T, :] = jnp.zeros((T, T), BF)
+    acc[...] = jnp.zeros_like(acc)
+
+    def window(col):
+        return win[pl.ds(pl.multiple_of(jnp.minimum(col - tiles, tiles) * T, T), T), :]
+
+    most = (tiles_ref.shape[0] - 1 + tiles) // 2
+    for_pairs(pairs_ref, 8, most, lambda p: gather_pair(pairs_ref, 8, p, tiles_ref, window, acc))
+
+
+def gather_kernel(pairs_ref, near_ref, start_ref, far_ref, tiles_ref, here_ref, other_ref, win, acc):
+    c, near = core_of(), near_part()
+    rows = near_ref.shape[0]
+    tiles = rows // T
     win[pl.ds(pl.multiple_of(near * rows, rows), rows), :] = near_ref[...]
-    win[rows : 2 * rows, :] = own_ref[...]
     win[pl.ds(pl.multiple_of((2 - near) * rows, rows), rows), :] = far_ref[...]
     win[3 * rows : 3 * rows + T, :] = jnp.zeros((T, T), BF)
-    acc[...] = jnp.zeros_like(acc)
+    acc[...] = start_ref[...]
 
     def window(col):
         return win[pl.ds(pl.multiple_of(col * T, T), T), :]
 
-    for p in range((tiles_ref.shape[0] - 1 + tiles) // 2):
-        left = jnp.concatenate([tiles_ref[pairs_ref[1, p]], tiles_ref[pairs_ref[2, p]]], axis=1)
-        right = jnp.concatenate([window(pairs_ref[3, p]), window(pairs_ref[4, p])], axis=0)
-        acc[pairs_ref[0, p]] += mm(left, right)
+    most = (tiles_ref.shape[0] - 1 + tiles) // 2
+    for_pairs(pairs_ref, 0, most, lambda p: gather_pair(pairs_ref, 0, p, tiles_ref, window, acc))
     for i in range(tiles // 2):
         here_ref[i * T : (i + 1) * T, :] = acc[c * (tiles // 2) + i].astype(BF)
         other_ref[i * T : (i + 1) * T, :] = acc[(1 - c) * (tiles // 2) + i].astype(BF)
@@ -229,11 +267,8 @@
         term(agg_ref)
 
 
-def scatter_kernel(
-    pairs_ref, mine_ref, theirs_ref, tiles_ref,
-    near_ref, own_ref, far_ref, src, acc,
-):
-    c, near = core_of(), near_part()
+def scatter_pairs(pairs_ref, base, mine_ref, theirs_ref, tiles_ref, src, acc, at):
+    c = core_of()
     half = mine_ref.shape[1]
     tiles = 2 * half // T
     ht = tiles // 2
@@ -243,15 +278,34 @@
         src[(1 - c) * ht + i] = theirs_ref[:, cut]
     src[tiles] = jnp.zeros((T, T), BF)
     acc[...] = jnp.zeros_like(acc)
-    for p in range((tiles_ref.shape[0] - 1 + tiles) // 2):
-        right = jnp.concatenate([tiles_ref[pairs_ref[1, p]], tiles_ref[pairs_ref[2, p]]], axis=1)
-        prod = mm(src[pairs_ref[0, p]], right)
-        acc[pairs_ref[3, p]] += prod[:, :T]
-        acc[pairs_ref[4, p]] += prod[:, T:]
+
+    def body(p):
+        right = jnp.concatenate(
+            [tiles_ref[pairs_ref[base + 1, p]], tiles_ref[pairs_ref[base + 2, p]]], axis=1
+        )
+        prod = mm(src[pairs_ref[base, p]], right)
+        acc[at(pairs_ref[base + 3, p])] += prod[:, :T]
+        acc[at(pairs_ref[base + 4, p])] += prod[:, T:]
+
+    for_pairs(pairs_ref, base, (tiles_ref.shape[0] - 1 + tiles) // 2, body)
+
+
+def scatter_kernel(pairs_ref, mine_ref, theirs_ref, tiles_ref, near_ref, far_ref, src, acc):
+    near = near_part()
+    tiles = near_ref.shape[0]
+    scatter_pairs(pairs_ref, 0, mine_ref, theirs_ref, tiles_ref, src, acc, lambda col: col)
     for i in range(tiles):
         near_ref[i] = acc[near * tiles + i].astype(BF)
-        own_ref[i] = acc[tiles + i]
         far_ref[i] = acc[(2 - near) * tiles + i].astype(BF)
+
+
+def scatter_own_kernel(pairs_ref, mine_ref, theirs_ref, tiles_ref, after_ref, own_ref, src, acc):
+    del after_ref
+    tiles = own_ref.shape[0]
+    scatter_pairs(
+        pairs_ref, 8, mine_ref, theirs_ref, tiles_ref, src, acc, lambda col: jnp.minimum(col - tiles, tiles)
+    )
+    own_ref[...] = acc[0:tiles]
 
 
 def chip_kernel(own_ref, a_ref, b_ref, g0_ref, g1_ref, g2_ref, g3_ref, out_ref, weights_ref):
@@ -409,17 +463,25 @@
             ((half, T), F32),
             ((8, half), F32),
             ((2 * slots + 1, T, T), BF),
-            ((8, T), jnp.int32),
+            ((16, T), jnp.int32),
         ],
         [mine, theirs, va, vb, order8, deg, features, out_grad, stay(w_self)],
         spaces={2: pl.ANY, 3: pl.ANY},
         scratch=[dma((2,))],
         name="prepare",
     )
+    part = call(
+        gather_own_kernel,
+        [((tiles + 1, T, T), F32)],
+        [pairs, feats_c, both],
+        spaces={0: smem},
+        scratch=[pltpu.VMEM((rows + T, T), BF)],
+        name="gather_own",
+    )
     here, other = call(
         gather_kernel,
         [((half, T), BF), ((half, T), BF)],
-        [pairs, near, feats_c, far, both],
+        [pairs, near, part, far, both],
         spaces={0: smem},
         scratch=[pltpu.VMEM((3 * rows + T, T), BF), pltpu.VMEM((tiles + 1, T, T), F32)],
         name="gather",
@@ -447,13 +509,21 @@
 
     terms_in = [mine_near, swap_core(theirs_near), swap_pair(mine_far, 0), swap_pair(theirs_far, 1)]
     piece = (tiles, T, T)
-    near, own, far = call(
+    near, far = call(
         scatter_kernel,
-        [(piece, BF), (piece, F32), (piece, BF)],
+        [(piece, BF)] * 2,
         [pairs, s_keep, s_other, both],
         spaces={0: smem},
         scratch=[pltpu.VMEM((tiles + 1, T, T), BF), pltpu.VMEM((3 * tiles + 1, T, T), F32)],
         name="scatter",
+    )
+    own = call(
+        scatter_own_kernel,
+        [(piece, F32)],
+        [pairs, s_keep, s_other, both, near],
+        spaces={0: smem, 4: pl.ANY},
+        scratch=[pltpu.VMEM((tiles + 1, T, T), BF), pltpu.VMEM((tiles + 1, T, T), F32)],
+        name="scatter_own",
     )
     from_near = swap_near(near)
     from_far = swap_far(far)

time: 60.4 us -> 60 us (level)
  waiting for transfers between devices: 20 us -> 16.8 us
  Pallas kernels: 13.7 us -> 16.2 us
    pallas_call x12 -> x14, Pallas kernels: 13.7 us -> 16.2 us  [call(): pl.pallas_call(kernel, out_shape=shapes[0] if single else shapes, in_spec...]
    ppermute x2, waiting for transfers between devices: 3.95 us -> 2.08 us  [swap_near(): return lax.ppermute(x, 'blk', [(b, b ^ 1) for b in range(blocks)])]
    ppermute x3, waiting for transfers between devices: 4.35 us -> 2.72 us  [shards(): lax.ppermute(g, 'blk', [(b, b ^ k << at) for b in range(blocks)])]
    ppermute x2, starting transfers between devices: 7.15 us -> 7.93 us  [swap_far(): lax.ppermute(x, 'blk', [(b, (b + 2 * (b % 2) - 1) % blocks) for b in rang...]
    ppermute x2, starting transfers between devices: 3.39 us -> 4.06 us  [swap_y(): return lax.ppermute(x, 'rep', [(r, r ^ 2) for r in range(reps)])]
  transfers between devices with their start and end apart: 22 -> 22, of which waited for: 10 -> 9; matrix products, arithmetic and copies ran while one was open for 0% -> 0% of each run, Pallas kernels for 16% -> 20%
where the time goes in v7:
time: 60 us; the launch traced here: 60.1 us
  starting transfers between devices  25.6 us (43%)
  waiting for transfers between devices  16.8 us (28%)
  Pallas kernels  16.2 us (27%)
  between operations  1.43 us (2%)
    pallas_call x14, Pallas kernels, call(): pl.pallas_call(kernel, out_shape=shapes[0] if single else shapes, in_spec...  16.2 us
    ppermute x2, starting transfers between devices, swap_far(): lax.ppermute(x, 'blk', [(b, (b + 2 * (b % 2) - 1) % blocks) for b in rang...  7.93 us
    ppermute x2, waiting for transfers between devices, swap_y(): return lax.ppermute(x, 'rep', [(r, r ^ 2) for r in range(reps)])  7.11 us
    ppermute x3, starting transfers between devices, shards(): lax.ppermute(g, 'blk', [(b, b ^ k << at) for b in range(blocks)])  4.44 us
    ppermute x2, starting transfers between devices, swap_y(): return lax.ppermute(x, 'rep', [(r, r ^ 2) for r in range(reps)])  4.06 us
    ppermute x2, starting transfers between devices, swap_near(): return lax.ppermute(x, 'blk', [(b, b ^ 1) for b in range(blocks)])  3.98 us
    ppermute x4, starting transfers between devices, swap_pair(): return lax.ppermute(x, ('blk', 'rep'), pairs_of)  3.22 us
    ppermute x8, waiting for transfers between devices, swap_core(): return lax.ppermute(x, 'rep', [(r, r ^ 1) for r in range(reps)])  2.89 us
  transfers between devices with their start and end apart: 22, of which 9 were waited for; matrix products, arithmetic and copies ran while one was open for 0% of the time, Pallas kernels for 20%

profile of v7, /device:TPU:0, one launch (start us, length us, event | category | flops | bytes accessed | tf_op | source)
XLA Modules:
  0.0 60.1 jit_solution(17661880145306817550)
XLA Ops:
  1.1 1.7 %reorder.1.after_ref.own_ref = bf16[1024,128]{1,0:T(8,128)(2,1)S(1)} custom-call(s32[8,128]{1,0:T(8,128)} %bitcast.5, bf16[1024,256]{1,0:T(8,128)(2,1)} %x_ref.1), custom_call_target="tpu_custom_call" | custom-call | tf_op jit(solution)/shard_map/reorder/pallas_call | solution.py:387
  2.8 2.6 %collective-permute-start.2 = (bf16[1024,128]{1,0:T(8,128)(2,1)S(1)}, bf16[1024,128]{1,0:T(8,128)(2,1)S(1)}, u32[]{:S(2)}, u32[]{:S(2)}) collective-permute-start(bf16[1024,128]{1,0:T(8,128)(2,1)S(1)} %reorder.1.after_ref.own_ref), channel_id=1, source_target_pairs={{0,4},{4,0},{8,12},{12,8},{16,20},{20,16},{24,28},{28,24},{1,5},{5... | collective-permute-start | bytes 786440 | tf_op jit(solution)/shard_map/ppermute | solution.py:411
  5.4 3.6 %collective-permute-start.3 = (bf16[1024,128]{1,0:T(8,128)(2,1)S(1)}, bf16[1024,128]{1,0:T(8,128)(2,1)S(1)}, u32[]{:S(2)}, u32[]{:S(2)}) collective-permute-start(bf16[1024,128]{1,0:T(8,128)(2,1)S(1)} %reorder.1.after_ref.own_ref), channel_id=1, source_target_pairs={{0,28},{4,8},{8,4},{12,16},{16,12},{20,24},{24,20},{28,0},{1,29},{... | collective-permute-start | bytes 786440 | tf_op jit(solution)/shard_map/ppermute | solution.py:414
  10.3 1.2 %collective-permute-done.theirs = s32[8,128]{1,0:T(8,128)S(1)} collective-permute-done((s32[8,128]{1,0:T(8,128)S(1)}, s32[8,128]{1,0:T(8,128)S(1)}, u32[]{:S(2)}, u32[]{:S(2)}) %collective-permute-start) | collective-permute-done | bytes 4128 | tf_op jit(solution)/shard_map/ppermute | solution.py:417
  11.5 2.9 %prepare.1 = (bf16[512,256]{1,0:T(8,128)(2,1)S(1)}, bf16[512,256]{1,0:T(8,128)(2,1)S(1)}, f32[512,256]{1,0:T(8,128)S(1)}, f32[512,128]{1,0:T(8,128)S(1)}, f32[8,...) custom-call(s32[8,128]{1,0:T(8,128)S(1)} %index.1.mine, ...), custom_call_target="tpu_custom_call" | custom-call | tf_op jit(solution)/shard_map/prepare/pallas_call | solution.py:387
  14.4 1.5 %gather_own.1.start_ref = f32[9,128,128]{2,1,0:T(8,128)S(1)} custom-call(s32[16,128]{1,0:T(8,128)S(1)} %get-tuple-element.35.pairs_ref, bf16[1024,128]{1,0:T(8,128)(2,1)S(1)} %reorder.1.after_ref.own_ref, bf16[97,128,128]{2,1,0:T(8,128)(2,1)S(1)} %get-tuple-element.36.tiles_ref), custom_call_target="tpu_custom_call" | custom-call | tf_op jit(solution)/shard_map/gather_own/pallas_call | solution.py:387
  15.9 2.1 %collective-permute-done.2.near_ref = bf16[1024,128]{1,0:T(8,128)(2,1)S(1)} collective-permute-done((bf16[1024,128]{1,0:T(8,128)(2,1)S(1)}, bf16[1024,128]{1,0:T(8,128)(2,1)S(1)}, u32[]{:S(2)}, u32[]{:S(2)}) %collective-permute-start.2) | collective-permute-done | bytes 262176 | tf_op jit(solution)/shard_map/ppermute | solution.py:411
  18.0 1.6 %gather.1 = (bf16[512,128]{1,0:T(8,128)(2,1)S(1)}, bf16[512,128]{1,0:T(8,128)(2,1)S(1)}) custom-call(s32[16,128]{1,0:T(8,128)S(1)} %get-tuple-element.35.pairs_ref, bf16[1024,128]{1,0:T(8,128)(2,1)S(1)} %collective-permute-done.2.near_ref, f32[9,128,128]{2,1,0:T(8,128)S(1)} %gather_own.1.start_ref, bf16[1024,128]{1,0:T(8,128)(2,1)S(1)} %collective-permute-done.3.far_ref, ...), custom_call_target="tpu_custom_call" | custom-call | tf_op jit(solution)/shard_map/gather/pallas_call | solution.py:387
  19.6 2.2 %collective-permute-start.4 = (bf16[512,128]{1,0:T(8,128)(2,1)S(1)}, bf16[512,128]{1,0:T(8,128)(2,1)S(1)}, u32[]{:S(2)}, u32[]{:S(2)}) collective-permute-start(bf16[512,128]{1,0:T(8,128)(2,1)S(1)} %get-tuple-element.37.own_ref), channel_id=1, source_target_pairs={{0,2},{1,3},{2,0},{3,1},{4,6},{5,7},{6,4},{7,5},{8,10},{9,11},{10,... | collective-permute-start | bytes 393224 | tf_op jit(solution)/shard_map/ppermute | solution.py:420
  22.0 3.7 %collective-permute-done.4.y_ref = bf16[512,128]{1,0:T(8,128)(2,1)S(1)} collective-permute-done((bf16[512,128]{1,0:T(8,128)(2,1)S(1)}, bf16[512,128]{1,0:T(8,128)(2,1)S(1)}, u32[]{:S(2)}, u32[]{:S(2)}) %collective-permute-start.4) | collective-permute-done | bytes 131104 | tf_op jit(solution)/shard_map/ppermute | solution.py:420
  25.7 1.9 %collective-permute-done.5.diag_ref = bf16[512,128]{1,0:T(8,128)(2,1)S(1)} collective-permute-done((bf16[512,128]{1,0:T(8,128)(2,1)S(1)}, bf16[512,128]{1,0:T(8,128)(2,1)S(1)}, u32[]{:S(2)}, u32[]{:S(2)}) %collective-permute-start.5) | collective-permute-done | bytes 131104 | tf_op jit(solution)/shard_map/ppermute | solution.py:423
  29.3 1.0 %collective-permute-start.11 = (bf16[64,256]{1,0:T(8,128)(2,1)S(1)}, bf16[64,256]{1,0:T(8,128)(2,1)S(1)}, u32[]{:S(2)}, u32[]{:S(2)}) collective-permute-start(bf16[64,256]{1,0:T(8,128)(2,1)S(1)} %get-tuple-element.52), channel_id=1, source_target_pairs={{0,4},{1,5},{2,6},{3,7},{4,0},{5,1},{6,2},{7,3},{8,12},{9,13},{10,... | collective-permute-start | bytes 98312 | tf_op jit(solution)/shard_map/ppermute | solution.py:508
  30.8 1.7 %scatter.1 = (bf16[8,128,128]{2,1,0:T(8,128)(2,1)S(1)}, bf16[8,128,128]{2,1,0:T(8,128)(2,1)S(1)}) custom-call(s32[16,128]{1,0:T(8,128)S(1)} %get-tuple-element.35.pairs_ref, bf16[128,512]{1,0:T(8,128)(2,1)S(1)} %get-tuple-element.43.mine_ref, bf16[128,512]{1,0:T(8,128)(2,1)S(1)} %collective-permute-done.7.theirs_ref, ...), custom_call_target="tpu_custom_call" | custom-call | tf_op jit(solution)/shard_map/scatter/pallas_call | solution.py:387
  32.5 1.4 %collective-permute-start.8 = (bf16[8,128,128]{2,1,0:T(8,128)(2,1)S(1)}, bf16[8,128,128]{2,1,0:T(8,128)(2,1)S(1)}, u32[]{:S(2)}, u32[]{:S(2)}) collective-permute-start(bf16[8,128,128]{2,1,0:T(8,128)(2,1)S(1)} %get-tuple-element.45.after_ref), channel_id=1, source_target_pairs={{0,4},{4,0},{8,12},{12,8},{16,20},{20,16},{24,28},{28,24},{1,5},{5... | collective-permute-start | bytes 786440 | tf_op jit(solution)/shard_map/ppermute | solution.py:411
  33.9 4.4 %collective-permute-start.9 = (bf16[8,128,128]{2,1,0:T(8,128)(2,1)S(1)}, bf16[8,128,128]{2,1,0:T(8,128)(2,1)S(1)}, u32[]{:S(2)}, u32[]{:S(2)}) collective-permute-start(bf16[8,128,128]{2,1,0:T(8,128)(2,1)S(1)} %get-tuple-element.46), channel_id=1, source_target_pairs={{0,28},{4,8},{8,4},{12,16},{16,12},{20,24},{24,20},{28,0},{1,29},{... | collective-permute-start | bytes 786440 | tf_op jit(solution)/shard_map/ppermute | solution.py:414
  39.4 3.4 %collective-permute-start.15 = (bf16[64,256]{1,0:T(8,128)(2,1)S(1)}, bf16[64,256]{1,0:T(8,128)(2,1)S(1)}, u32[]{:S(2)}, u32[]{:S(2)}) collective-permute-start(bf16[64,256]{1,0:T(8,128)(2,1)S(1)} %add_convert_fusion.g0_ref), channel_id=1, source_target_pairs={{0,24},{4,28},{8,16},{12,20},{16,8},{20,12},{24,0},{28,4},{1,25},{... | collective-permute-start | bytes 98312 | tf_op jit(solution)/shard_map/ppermute | solution.py:543
  42.7 1.6 %scatter_own.1.own_ref = f32[8,128,128]{2,1,0:T(8,128)S(1)} custom-call(s32[16,128]{1,0:T(8,128)S(1)} %get-tuple-element.35.pairs_ref, bf16[128,512]{1,0:T(8,128)(2,1)S(1)} %get-tuple-element.43.mine_ref, bf16[128,512]{1,0:T(8,128)(2,1)S(1)} %collective-permute-done.7.theirs_ref, bf16[97,128,128]{2,1,0:T(8,128)(2,1)S(1)} %get-tuple-element.36.tiles_ref, ...), custom_call_target="tpu_custom_call" | custom-call | tf_op jit(solution)/shard_map/scatter_own/pallas_call | solution.py:387
  44.4 1.1 %collective-permute-done.13.g1_ref = bf16[64,256]{1,0:T(8,128)(2,1)S(1)} collective-permute-done((bf16[64,256]{1,0:T(8,128)(2,1)S(1)}, bf16[64,256]{1,0:T(8,128)(2,1)S(1)}, u32[]{:S(2)}, u32[]{:S(2)}) %collective-permute-start.13) | collective-permute-done | bytes 32800 | tf_op jit(solution)/shard_map/ppermute | solution.py:543
  45.8 1.3 %collective-permute-done.15.g3_ref = bf16[64,256]{1,0:T(8,128)(2,1)S(1)} collective-permute-done((bf16[64,256]{1,0:T(8,128)(2,1)S(1)}, bf16[64,256]{1,0:T(8,128)(2,1)S(1)}, u32[]{:S(2)}, u32[]{:S(2)}) %collective-permute-start.15) | collective-permute-done | bytes 32800 | tf_op jit(solution)/shard_map/ppermute | solution.py:543
  47.2 1.8 %collective-permute-start.16 = (bf16[9,128,128]{2,1,0:T(8,128)(2,1)S(1)}, bf16[9,128,128]{2,1,0:T(8,128)(2,1)S(1)}, u32[]{:S(2)}, u32[]{:S(2)}) collective-permute-start(bf16[9,128,128]{2,1,0:T(8,128)(2,1)S(1)} %get-tuple-element.56.mine_ref), channel_id=1, source_target_pairs={{0,2},{1,3},{2,0},{3,1},{4,6},{5,7},{6,4},{7,5},{8,10},{9,11},{10,... | collective-permute-start | bytes 884744 | tf_op jit(solution)/shard_map/ppermute | solution.py:420
  51.6 1.5 %output.1 = bf16[1024,256]{1,0:T(8,128)(2,1)} custom-call(s32[1,1024]{1,0:T(1,128)S(1)} %copy-done.2, bf16[512,256]{1,0:T(8,128)(2,1)S(1)} %get-tuple-element.57.own_ref, bf16[512,256]{1,0:T(8,128)(2,1)S(1)} %collective-permute-done.17.core_ref), custom_call_target="tpu_custom_call" | custom-call | tf_op jit(solution)/shard_map/output/pallas_call | solution.py:387
  53.2 3.4 %collective-permute-done.16.theirs_ref = bf16[9,128,128]{2,1,0:T(8,128)(2,1)S(1)} collective-permute-done((bf16[9,128,128]{2,1,0:T(8,128)(2,1)S(1)}, bf16[9,128,128]{2,1,0:T(8,128)(2,1)S(1)}, u32[]{:S(2)}, u32[]{:S(2)}) %collective-permute-start.16) | collective-permute-done | bytes 294944 | tf_op jit(solution)/shard_map/ppermute | solution.py:420
  56.8 1.7 %collective-permute-done.21.core_ref = bf16[12,128,128]{2,1,0:T(8,128)(2,1)S(1)} collective-permute-done((bf16[12,128,128]{2,1,0:T(8,128)(2,1)S(1)}, bf16[12,128,128]{2,1,0:T(8,128)(2,1)S(1)}, u32[]{:S(2)}, u32[]{:S(2)}) %collective-permute-start.21) | collective-permute-done | bytes 393248 | tf_op jit(solution)/shard_map/ppermute | solution.py:417
  58.5 1.6 %restore.1 = (bf16[1024,256]{1,0:T(8,128)(2,1)}, f32[256,256]{1,0:T(8,128)}, f32[256,256]{1,0:T(8,128)}) custom-call(s32[1,1024]{1,0:T(1,128)S(1)} %copy-done.2, bf16[12,128,128]{2,1,0:T(8,128)(2,1)S(1)} %total.1.own_ref, bf16[12,128,128]{2,1,0:T(8,128)(2,1)S(1)} %collective-permute-done.21.core_ref), custom_call_target="tpu_custom_call" | custom-call | tf_op jit(solution)/shard_map/restore/pallas_call | solution.py:387
  (41 shorter events, 7.8 us)
Async XLA Ops:
  0.6 10.9 %collective-permute-start.1 = (bf16[48,128,128]{2,1,0:T(8,128)(2,1)}, bf16[48,128,128]{2,1,0:T(8,128)(2,1)S(1)}, u32[]{:S(2)}, u32[]{:S(2)}) collective-permute-start(bf16[48,128,128]{2,1,0:T(8,128)(2,1)} %bitcast.7), channel_id=1, source_target_pairs={{0,1},{1,0},{2,3},{3,2},{4,5},{5,4},{6,7},{7,6},{8,9},{9,8},{10,11... | collective-permute-start | bytes 4718600 | tf_op jit(solution)/shard_map/ppermute | solution.py:417
  2.8 15.2 %collective-permute-start.2 = (bf16[1024,128]{1,0:T(8,128)(2,1)S(1)}, bf16[1024,128]{1,0:T(8,128)(2,1)S(1)}, u32[]{:S(2)}, u32[]{:S(2)}) collective-permute-start(bf16[1024,128]{1,0:T(8,128)(2,1)S(1)} %reorder.1.after_ref.own_ref), channel_id=1, source_target_pairs={{0,4},{4,0},{8,12},{12,8},{16,20},{20,16},{24,28},{28,24},{1,5},{5... | collective-permute-start | bytes 786440 | tf_op jit(solution)/shard_map/ppermute | solution.py:411
  5.4 12.6 %collective-permute-start.3 = (bf16[1024,128]{1,0:T(8,128)(2,1)S(1)}, bf16[1024,128]{1,0:T(8,128)(2,1)S(1)}, u32[]{:S(2)}, u32[]{:S(2)}) collective-permute-start(bf16[1024,128]{1,0:T(8,128)(2,1)S(1)} %reorder.1.after_ref.own_ref), channel_id=1, source_target_pairs={{0,28},{4,8},{8,4},{12,16},{16,12},{20,24},{24,20},{28,0},{1,29},{... | collective-permute-start | bytes 786440 | tf_op jit(solution)/shard_map/ppermute | solution.py:414
  10.3 1.2 %collective-permute-start = (s32[8,128]{1,0:T(8,128)S(1)}, s32[8,128]{1,0:T(8,128)S(1)}, u32[]{:S(2)}, u32[]{:S(2)}) collective-permute-start(s32[8,128]{1,0:T(8,128)S(1)} %index.1.mine), channel_id=1, source_target_pairs={{0,1},{1,0},{2,3},{3,2},{4,5},{5,4},{6,7},{7,6},{8,9},{9,8},{10,11... | collective-permute-start | bytes 12296 | tf_op jit(solution)/shard_map/ppermute | solution.py:417
  15.9 11.8 %copy-start.1 = (bf16[256,256]{1,0:T(8,128)(2,1)S(1)}, bf16[256,256]{1,0:T(8,128)(2,1)}, u32[]{:S(2)}) copy-start(bf16[256,256]{1,0:T(8,128)(2,1)} %wn_ref.1) | copy-start | bytes 393220
  19.6 6.1 %collective-permute-start.4 = (bf16[512,128]{1,0:T(8,128)(2,1)S(1)}, bf16[512,128]{1,0:T(8,128)(2,1)S(1)}, u32[]{:S(2)}, u32[]{:S(2)}) collective-permute-start(bf16[512,128]{1,0:T(8,128)(2,1)S(1)} %get-tuple-element.37.own_ref), channel_id=1, source_target_pairs={{0,2},{1,3},{2,0},{3,1},{4,6},{5,7},{6,4},{7,5},{8,10},{9,11},{10,... | collective-permute-start | bytes 393224 | tf_op jit(solution)/shard_map/ppermute | solution.py:420
  21.8 5.9 %collective-permute-start.5 = (bf16[512,128]{1,0:T(8,128)(2,1)S(1)}, bf16[512,128]{1,0:T(8,128)(2,1)S(1)}, u32[]{:S(2)}, u32[]{:S(2)}) collective-permute-start(bf16[512,128]{1,0:T(8,128)(2,1)S(1)} %get-tuple-element.38), channel_id=1, source_target_pairs={{0,3},{1,2},{2,1},{3,0},{4,7},{5,6},{6,5},{7,4},{8,11},{9,10},{10,... | collective-permute-start | bytes 393224 | tf_op jit(solution)/shard_map/ppermute | solution.py:423
  21.8 5.9 %collective-permute-start.6 = (bf16[512,128]{1,0:T(8,128)(2,1)S(1)}, bf16[512,128]{1,0:T(8,128)(2,1)S(1)}, u32[]{:S(2)}, u32[]{:S(2)}) collective-permute-start(bf16[512,128]{1,0:T(8,128)(2,1)S(1)} %get-tuple-element.38), channel_id=1, source_target_pairs={{0,1},{1,0},{2,3},{3,2},{4,5},{5,4},{6,7},{7,6},{8,9},{9,8},{10,11... | collective-permute-start | bytes 393224 | tf_op jit(solution)/shard_map/ppermute | solution.py:417
  28.3 2.5 %collective-permute-start.7 = (bf16[128,512]{1,0:T(8,128)(2,1)S(1)}, bf16[128,512]{1,0:T(8,128)(2,1)S(1)}, u32[]{:S(2)}, u32[]{:S(2)}) collective-permute-start(bf16[128,512]{1,0:T(8,128)(2,1)S(1)} %get-tuple-element.44), channel_id=1, source_target_pairs={{0,1},{1,0},{2,3},{3,2},{4,5},{5,4},{6,7},{7,6},{8,9},{9,8},{10,11... | collective-permute-start | bytes 393224 | tf_op jit(solution)/shard_map/ppermute | solution.py:417
  28.9 9.4 %collective-permute-start.10 = (bf16[64,256]{1,0:T(8,128)(2,1)S(1)}, bf16[64,256]{1,0:T(8,128)(2,1)S(1)}, u32[]{:S(2)}, u32[]{:S(2)}) collective-permute-start(bf16[64,256]{1,0:T(8,128)(2,1)S(1)} %get-tuple-element.51), channel_id=1, source_target_pairs={{0,1},{1,0},{2,3},{3,2},{4,5},{5,4},{6,7},{7,6},{8,9},{9,8},{10,11... | collective-permute-start | bytes 98312 | tf_op jit(solution)/shard_map/ppermute | solution.py:417
  29.3 9.0 %collective-permute-start.11 = (bf16[64,256]{1,0:T(8,128)(2,1)S(1)}, bf16[64,256]{1,0:T(8,128)(2,1)S(1)}, u32[]{:S(2)}, u32[]{:S(2)}) collective-permute-start(bf16[64,256]{1,0:T(8,128)(2,1)S(1)} %get-tuple-element.52), channel_id=1, source_target_pairs={{0,4},{1,5},{2,6},{3,7},{4,0},{5,1},{6,2},{7,3},{8,12},{9,13},{10,... | collective-permute-start | bytes 98312 | tf_op jit(solution)/shard_map/ppermute | solution.py:508
  30.3 7.9 %collective-permute-start.12 = (bf16[64,256]{1,0:T(8,128)(2,1)S(1)}, bf16[64,256]{1,0:T(8,128)(2,1)S(1)}, u32[]{:S(2)}, u32[]{:S(2)}) collective-permute-start(bf16[64,256]{1,0:T(8,128)(2,1)S(1)} %get-tuple-element.53), channel_id=1, source_target_pairs={{0,5},{1,4},{2,7},{3,6},{4,1},{5,0},{6,3},{7,2},{8,13},{9,12},{10,... | collective-permute-start | bytes 98312 | tf_op jit(solution)/shard_map/ppermute | solution.py:508
  32.5 14.6 %collective-permute-start.8 = (bf16[8,128,128]{2,1,0:T(8,128)(2,1)S(1)}, bf16[8,128,128]{2,1,0:T(8,128)(2,1)S(1)}, u32[]{:S(2)}, u32[]{:S(2)}) collective-permute-start(bf16[8,128,128]{2,1,0:T(8,128)(2,1)S(1)} %get-tuple-element.45.after_ref), channel_id=1, source_target_pairs={{0,4},{4,0},{8,12},{12,8},{16,20},{20,16},{24,28},{28,24},{1,5},{5... | collective-permute-start | bytes 786440 | tf_op jit(solution)/shard_map/ppermute | solution.py:411
  33.9 13.2 %collective-permute-start.9 = (bf16[8,128,128]{2,1,0:T(8,128)(2,1)S(1)}, bf16[8,128,128]{2,1,0:T(8,128)(2,1)S(1)}, u32[]{:S(2)}, u32[]{:S(2)}) collective-permute-start(bf16[8,128,128]{2,1,0:T(8,128)(2,1)S(1)} %get-tuple-element.46), channel_id=1, source_target_pairs={{0,28},{4,8},{8,4},{12,16},{16,12},{20,24},{24,20},{28,0},{1,29},{... | collective-permute-start | bytes 786440 | tf_op jit(solution)/shard_map/ppermute | solution.py:414
  38.3 10.8 %copy-start = (bf16[256,256]{1,0:T(8,128)(2,1)S(1)}, bf16[256,256]{1,0:T(8,128)(2,1)}, u32[]{:S(2)}) copy-start(bf16[256,256]{1,0:T(8,128)(2,1)} %ws_ref.1) | copy-start | bytes 393220
  38.3 7.2 %collective-permute-start.13 = (bf16[64,256]{1,0:T(8,128)(2,1)S(1)}, bf16[64,256]{1,0:T(8,128)(2,1)S(1)}, u32[]{:S(2)}, u32[]{:S(2)}) collective-permute-start(bf16[64,256]{1,0:T(8,128)(2,1)S(1)} %add_convert_fusion.g0_ref), channel_id=1, source_target_pairs={{0,8},{4,12},{8,0},{12,4},{16,24},{20,28},{24,16},{28,20},{1,9},{5... | collective-permute-start | bytes 98312 | tf_op jit(solution)/shard_map/ppermute | solution.py:543
  38.4 7.5 %collective-permute-start.14 = (bf16[64,256]{1,0:T(8,128)(2,1)S(1)}, bf16[64,256]{1,0:T(8,128)(2,1)S(1)}, u32[]{:S(2)}, u32[]{:S(2)}) collective-permute-start(bf16[64,256]{1,0:T(8,128)(2,1)S(1)} %add_convert_fusion.g0_ref), channel_id=1, source_target_pairs={{0,16},{4,20},{8,24},{12,28},{16,0},{20,4},{24,8},{28,12},{1,17},{... | collective-permute-start | bytes 98312 | tf_op jit(solution)/shard_map/ppermute | solution.py:543
  39.4 7.7 %collective-permute-start.15 = (bf16[64,256]{1,0:T(8,128)(2,1)S(1)}, bf16[64,256]{1,0:T(8,128)(2,1)S(1)}, u32[]{:S(2)}, u32[]{:S(2)}) collective-permute-start(bf16[64,256]{1,0:T(8,128)(2,1)S(1)} %add_convert_fusion.g0_ref), channel_id=1, source_target_pairs={{0,24},{4,28},{8,16},{12,20},{16,8},{20,12},{24,0},{28,4},{1,25},{... | collective-permute-start | bytes 98312 | tf_op jit(solution)/shard_map/ppermute | solution.py:543
  47.2 9.4 %collective-permute-start.16 = (bf16[9,128,128]{2,1,0:T(8,128)(2,1)S(1)}, bf16[9,128,128]{2,1,0:T(8,128)(2,1)S(1)}, u32[]{:S(2)}, u32[]{:S(2)}) collective-permute-start(bf16[9,128,128]{2,1,0:T(8,128)(2,1)S(1)} %get-tuple-element.56.mine_ref), channel_id=1, source_target_pairs={{0,2},{1,3},{2,0},{3,1},{4,6},{5,7},{6,4},{7,5},{8,10},{9,11},{10,... | collective-permute-start | bytes 884744 | tf_op jit(solution)/shard_map/ppermute | solution.py:420
  49.0 2.6 %collective-permute-start.17 = (bf16[512,256]{1,0:T(8,128)(2,1)S(1)}, bf16[512,256]{1,0:T(8,128)(2,1)S(1)}, u32[]{:S(2)}, u32[]{:S(2)}) collective-permute-start(bf16[512,256]{1,0:T(8,128)(2,1)S(1)} %get-tuple-element.57.own_ref), channel_id=1, source_target_pairs={{0,1},{1,0},{2,3},{3,2},{4,5},{5,4},{6,7},{7,6},{8,9},{9,8},{10,11... | collective-permute-start | bytes 786440 | tf_op jit(solution)/shard_map/ppermute | solution.py:417
  49.4 7.2 %collective-permute-start.18 = (f32[128,512]{1,0:T(8,128)S(1)}, f32[128,512]{1,0:T(8,128)S(1)}, u32[]{:S(2)}, u32[]{:S(2)}) collective-permute-start(f32[128,512]{1,0:T(8,128)S(1)} %get-tuple-element.61), channel_id=1, source_target_pairs={{0,1},{1,0},{2,3},{3,2},{4,5},{5,4},{6,7},{7,6},{8,9},{9,8},{10,11... | collective-permute-start | bytes 786440 | tf_op jit(solution)/shard_map/ppermute | solution.py:417
  49.9 6.7 %collective-permute-start.19 = (bf16[128,128]{1,0:T(8,128)(2,1)S(1)}, bf16[128,128]{1,0:T(8,128)(2,1)S(1)}, u32[]{:S(2)}, u32[]{:S(2)}) collective-permute-start(bf16[128,128]{1,0:T(8,128)(2,1)S(1)} %get-tuple-element.62), channel_id=1, source_target_pairs={{0,4},{1,5},{2,6},{3,7},{4,0},{5,1},{6,2},{7,3},{8,12},{9,13},{10,... | collective-permute-start | bytes 98312 | tf_op jit(solution)/shard_map/ppermute | solution.py:508
  50.6 6.0 %collective-permute-start.20 = (bf16[128,128]{1,0:T(8,128)(2,1)S(1)}, bf16[128,128]{1,0:T(8,128)(2,1)S(1)}, u32[]{:S(2)}, u32[]{:S(2)}) collective-permute-start(bf16[128,128]{1,0:T(8,128)(2,1)S(1)} %get-tuple-element.62), channel_id=1, source_target_pairs={{0,6},{1,7},{2,4},{3,5},{4,2},{5,3},{6,0},{7,1},{8,14},{9,15},{10,... | collective-permute-start | bytes 98312 | tf_op jit(solution)/shard_map/ppermute | solution.py:508
  56.7 1.8 %collective-permute-start.21 = (bf16[12,128,128]{2,1,0:T(8,128)(2,1)S(1)}, bf16[12,128,128]{2,1,0:T(8,128)(2,1)S(1)}, u32[]{:S(2)}, u32[]{:S(2)}) collective-permute-start(bf16[12,128,128]{2,1,0:T(8,128)(2,1)S(1)} %total.1.own_ref), channel_id=1, source_target_pairs={{0,1},{1,0},{2,3},{3,2},{4,5},{5,4},{6,7},{7,6},{8,9},{9,8},{10,11... | collective-permute-start | bytes 1179656 | tf_op jit(solution)/shard_map/ppermute | solution.py:417
  (1 other events, 7.3 us)

commit v8 on v7

--- a/solution.py
+++ b/solution.py
@@ -131,14 +131,14 @@
         out_ref[base + 5 : base + 6, :] = pairs.astype(jnp.int32)
 
 
-def for_pairs(pairs_ref, base, most, body):
-    size = (most + 3) // 4
-    for start in range(0, most, size):
-
-        @pl.when(pairs_ref[base + 5, 0] > start)
-        def _(start=start):
-            for p in range(start, min(start + size, most)):
-                body(p)
+def for_pairs(pairs_ref, base, usual, most, body):
+    for p in range(usual):
+        body(p)
+
+    @pl.when(pairs_ref[base + 5, 0] > usual)
+    def _():
+        for p in range(usual, most):
+            body(p)
 
 
 def prepare_kernel(
@@ -194,7 +194,7 @@
         return win[pl.ds(pl.multiple_of(jnp.minimum(col - tiles, tiles) * T, T), T), :]
 
     most = (tiles_ref.shape[0] - 1 + tiles) // 2
-    for_pairs(pairs_ref, 8, most, lambda p: gather_pair(pairs_ref, 8, p, tiles_ref, window, acc))
+    for_pairs(pairs_ref, 8, most // 2, most, lambda p: gather_pair(pairs_ref, 8, p, tiles_ref, window, acc))
 
 
 def gather_kernel(pairs_ref, near_ref, start_ref, far_ref, tiles_ref, here_ref, other_ref, win, acc):
@@ -210,7 +210,7 @@
         return win[pl.ds(pl.multiple_of(col * T, T), T), :]
 
     most = (tiles_ref.shape[0] - 1 + tiles) // 2
-    for_pairs(pairs_ref, 0, most, lambda p: gather_pair(pairs_ref, 0, p, tiles_ref, window, acc))
+    for_pairs(pairs_ref, 0, most * 3 // 4, most, lambda p: gather_pair(pairs_ref, 0, p, tiles_ref, window, acc))
     for i in range(tiles // 2):
         here_ref[i * T : (i + 1) * T, :] = acc[c * (tiles // 2) + i].astype(BF)
         other_ref[i * T : (i + 1) * T, :] = acc[(1 - c) * (tiles // 2) + i].astype(BF)
@@ -287,7 +287,8 @@
         acc[at(pairs_ref[base + 3, p])] += prod[:, :T]
         acc[at(pairs_ref[base + 4, p])] += prod[:, T:]
 
-    for_pairs(pairs_ref, base, (tiles_ref.shape[0] - 1 + tiles) // 2, body)
+    most = (tiles_ref.shape[0] - 1 + tiles) // 2
+    for_pairs(pairs_ref, base, most // 2 if base else most * 3 // 4, most, body)
 
 
 def scatter_kernel(pairs_ref, mine_ref, theirs_ref, tiles_ref, near_ref, far_ref, src, acc):

time: 60 us -> 59.9 us (level)
  starting transfers between devices: 25.6 us -> 25 us
    ppermute x2, starting transfers between devices: 7.93 us -> 7.14 us  [swap_far(): lax.ppermute(x, 'blk', [(b, (b + 2 * (b % 2) - 1) % blocks) for b in rang...]
    ppermute x2, starting transfers between devices: 4.06 us -> 3.39 us  [swap_y(): return lax.ppermute(x, 'rep', [(r, r ^ 2) for r in range(reps)])]
  transfers between devices with their start and end apart: 22 -> 22, of which waited for: 9 -> 10; matrix products, arithmetic and copies ran while one was open for 0% -> 0% of each run, Pallas kernels for 20% -> 20%
where the time goes in v8:
time: 59.9 us; the launch traced here: 59.6 us
  starting transfers between devices  25 us (42%)
  waiting for transfers between devices  17.2 us (29%)
  Pallas kernels  15.9 us (27%)
  between operations  1.43 us (2%)
    pallas_call x14, Pallas kernels, call(): pl.pallas_call(kernel, out_shape=shapes[0] if single else shapes, in_spec...  15.9 us
    ppermute x2, starting transfers between devices, swap_far(): lax.ppermute(x, 'blk', [(b, (b + 2 * (b % 2) - 1) % blocks) for b in rang...  7.14 us
    ppermute x2, waiting for transfers between devices, swap_y(): return lax.ppermute(x, 'rep', [(r, r ^ 2) for r in range(reps)])  7.04 us
    ppermute x3, starting transfers between devices, shards(): lax.ppermute(g, 'blk', [(b, b ^ k << at) for b in range(blocks)])  4.44 us
    ppermute x2, starting transfers between devices, swap_near(): return lax.ppermute(x, 'blk', [(b, b ^ 1) for b in range(blocks)])  4.19 us
    ppermute x4, starting transfers between devices, swap_pair(): return lax.ppermute(x, ('blk', 'rep'), pairs_of)  3.7 us
    ppermute x2, starting transfers between devices, swap_y(): return lax.ppermute(x, 'rep', [(r, r ^ 2) for r in range(reps)])  3.39 us
    ppermute x3, waiting for transfers between devices, shards(): lax.ppermute(g, 'blk', [(b, b ^ k << at) for b in range(blocks)])  2.94 us
  transfers between devices with their start and end apart: 22, of which 10 were waited for; matrix products, arithmetic and copies ran while one was open for 0% of the time, Pallas kernels for 20%

profile of v8, /device:TPU:0, one launch (start us, length us, event | category | flops | bytes accessed | tf_op | source)
XLA Modules:
  0.0 59.6 jit_solution(967884786494806187)
XLA Ops:
  1.1 1.7 %reorder.1.after_ref.own_ref = bf16[1024,128]{1,0:T(8,128)(2,1)S(1)} custom-call(s32[8,128]{1,0:T(8,128)} %bitcast.5, bf16[1024,256]{1,0:T(8,128)(2,1)} %x_ref.1), custom_call_target="tpu_custom_call" | custom-call | tf_op jit(solution)/shard_map/reorder/pallas_call | solution.py:388
  2.8 2.6 %collective-permute-start.2 = (bf16[1024,128]{1,0:T(8,128)(2,1)S(1)}, bf16[1024,128]{1,0:T(8,128)(2,1)S(1)}, u32[]{:S(2)}, u32[]{:S(2)}) collective-permute-start(bf16[1024,128]{1,0:T(8,128)(2,1)S(1)} %reorder.1.after_ref.own_ref), channel_id=1, source_target_pairs={{0,4},{4,0},{8,12},{12,8},{16,20},{20,16},{24,28},{28,24},{1,5},{5... | collective-permute-start | bytes 786440 | tf_op jit(solution)/shard_map/ppermute | solution.py:412
  5.4 3.6 %collective-permute-start.3 = (bf16[1024,128]{1,0:T(8,128)(2,1)S(1)}, bf16[1024,128]{1,0:T(8,128)(2,1)S(1)}, u32[]{:S(2)}, u32[]{:S(2)}) collective-permute-start(bf16[1024,128]{1,0:T(8,128)(2,1)S(1)} %reorder.1.after_ref.own_ref), channel_id=1, source_target_pairs={{0,28},{4,8},{8,4},{12,16},{16,12},{20,24},{24,20},{28,0},{1,29},{... | collective-permute-start | bytes 786440 | tf_op jit(solution)/shard_map/ppermute | solution.py:415
  11.5 2.9 %prepare.1 = (bf16[512,256]{1,0:T(8,128)(2,1)S(1)}, bf16[512,256]{1,0:T(8,128)(2,1)S(1)}, f32[512,256]{1,0:T(8,128)S(1)}, f32[512,128]{1,0:T(8,128)S(1)}, f32[8,...) custom-call(s32[8,128]{1,0:T(8,128)S(1)} %index.1.mine, ...), custom_call_target="tpu_custom_call" | custom-call | tf_op jit(solution)/shard_map/prepare/pallas_call | solution.py:388
  14.4 1.3 %gather_own.1.start_ref = f32[9,128,128]{2,1,0:T(8,128)S(1)} custom-call(s32[16,128]{1,0:T(8,128)S(1)} %get-tuple-element.35.pairs_ref, bf16[1024,128]{1,0:T(8,128)(2,1)S(1)} %reorder.1.after_ref.own_ref, bf16[97,128,128]{2,1,0:T(8,128)(2,1)S(1)} %get-tuple-element.36.tiles_ref), custom_call_target="tpu_custom_call" | custom-call | tf_op jit(solution)/shard_map/gather_own/pallas_call | solution.py:388
  15.7 2.3 %collective-permute-done.2.near_ref = bf16[1024,128]{1,0:T(8,128)(2,1)S(1)} collective-permute-done((bf16[1024,128]{1,0:T(8,128)(2,1)S(1)}, bf16[1024,128]{1,0:T(8,128)(2,1)S(1)}, u32[]{:S(2)}, u32[]{:S(2)}) %collective-permute-start.2) | collective-permute-done | bytes 262176 | tf_op jit(solution)/shard_map/ppermute | solution.py:412
  18.0 1.7 %gather.1 = (bf16[512,128]{1,0:T(8,128)(2,1)S(1)}, bf16[512,128]{1,0:T(8,128)(2,1)S(1)}) custom-call(s32[16,128]{1,0:T(8,128)S(1)} %get-tuple-element.35.pairs_ref, bf16[1024,128]{1,0:T(8,128)(2,1)S(1)} %collective-permute-done.2.near_ref, f32[9,128,128]{2,1,0:T(8,128)S(1)} %gather_own.1.start_ref, bf16[1024,128]{1,0:T(8,128)(2,1)S(1)} %collective-permute-done.3.far_ref, ...), custom_call_target="tpu_custom_call" | custom-call | tf_op jit(solution)/shard_map/gather/pallas_call | solution.py:388
  19.7 1.8 %collective-permute-start.4 = (bf16[512,128]{1,0:T(8,128)(2,1)S(1)}, bf16[512,128]{1,0:T(8,128)(2,1)S(1)}, u32[]{:S(2)}, u32[]{:S(2)}) collective-permute-start(bf16[512,128]{1,0:T(8,128)(2,1)S(1)} %get-tuple-element.37.own_ref), channel_id=1, source_target_pairs={{0,2},{1,3},{2,0},{3,1},{4,6},{5,7},{6,4},{7,5},{8,10},{9,11},{10,... | collective-permute-start | bytes 393224 | tf_op jit(solution)/shard_map/ppermute | solution.py:421
  21.9 3.7 %collective-permute-done.4.y_ref = bf16[512,128]{1,0:T(8,128)(2,1)S(1)} collective-permute-done((bf16[512,128]{1,0:T(8,128)(2,1)S(1)}, bf16[512,128]{1,0:T(8,128)(2,1)S(1)}, u32[]{:S(2)}, u32[]{:S(2)}) %collective-permute-start.4) | collective-permute-done | bytes 131104 | tf_op jit(solution)/shard_map/ppermute | solution.py:421
  25.6 1.7 %collective-permute-done.5.diag_ref = bf16[512,128]{1,0:T(8,128)(2,1)S(1)} collective-permute-done((bf16[512,128]{1,0:T(8,128)(2,1)S(1)}, bf16[512,128]{1,0:T(8,128)(2,1)S(1)}, u32[]{:S(2)}, u32[]{:S(2)}) %collective-permute-start.5) | collective-permute-done | bytes 131104 | tf_op jit(solution)/shard_map/ppermute | solution.py:424
  29.0 1.5 %collective-permute-start.11 = (bf16[64,256]{1,0:T(8,128)(2,1)S(1)}, bf16[64,256]{1,0:T(8,128)(2,1)S(1)}, u32[]{:S(2)}, u32[]{:S(2)}) collective-permute-start(bf16[64,256]{1,0:T(8,128)(2,1)S(1)} %get-tuple-element.52), channel_id=1, source_target_pairs={{0,4},{1,5},{2,6},{3,7},{4,0},{5,1},{6,2},{7,3},{8,12},{9,13},{10,... | collective-permute-start | bytes 98312 | tf_op jit(solution)/shard_map/ppermute | solution.py:509
  30.7 1.7 %scatter.1 = (bf16[8,128,128]{2,1,0:T(8,128)(2,1)S(1)}, bf16[8,128,128]{2,1,0:T(8,128)(2,1)S(1)}) custom-call(s32[16,128]{1,0:T(8,128)S(1)} %get-tuple-element.35.pairs_ref, bf16[128,512]{1,0:T(8,128)(2,1)S(1)} %get-tuple-element.43.mine_ref, bf16[128,512]{1,0:T(8,128)(2,1)S(1)} %collective-permute-done.7.theirs_ref, ...), custom_call_target="tpu_custom_call" | custom-call | tf_op jit(solution)/shard_map/scatter/pallas_call | solution.py:388
  32.4 1.6 %collective-permute-start.8 = (bf16[8,128,128]{2,1,0:T(8,128)(2,1)S(1)}, bf16[8,128,128]{2,1,0:T(8,128)(2,1)S(1)}, u32[]{:S(2)}, u32[]{:S(2)}) collective-permute-start(bf16[8,128,128]{2,1,0:T(8,128)(2,1)S(1)} %get-tuple-element.45.after_ref), channel_id=1, source_target_pairs={{0,4},{4,0},{8,12},{12,8},{16,20},{20,16},{24,28},{28,24},{1,5},{5... | collective-permute-start | bytes 786440 | tf_op jit(solution)/shard_map/ppermute | solution.py:412
  34.0 3.6 %collective-permute-start.9 = (bf16[8,128,128]{2,1,0:T(8,128)(2,1)S(1)}, bf16[8,128,128]{2,1,0:T(8,128)(2,1)S(1)}, u32[]{:S(2)}, u32[]{:S(2)}) collective-permute-start(bf16[8,128,128]{2,1,0:T(8,128)(2,1)S(1)} %get-tuple-element.46), channel_id=1, source_target_pairs={{0,28},{4,8},{8,4},{12,16},{16,12},{20,24},{24,20},{28,0},{1,29},{... | collective-permute-start | bytes 786440 | tf_op jit(solution)/shard_map/ppermute | solution.py:415
  38.7 3.4 %collective-permute-start.15 = (bf16[64,256]{1,0:T(8,128)(2,1)S(1)}, bf16[64,256]{1,0:T(8,128)(2,1)S(1)}, u32[]{:S(2)}, u32[]{:S(2)}) collective-permute-start(bf16[64,256]{1,0:T(8,128)(2,1)S(1)} %add_convert_fusion.g0_ref), channel_id=1, source_target_pairs={{0,24},{4,28},{8,16},{12,20},{16,8},{20,12},{24,0},{28,4},{1,25},{... | collective-permute-start | bytes 98312 | tf_op jit(solution)/shard_map/ppermute | solution.py:544
  42.1 1.4 %scatter_own.1.own_ref = f32[8,128,128]{2,1,0:T(8,128)S(1)} custom-call(s32[16,128]{1,0:T(8,128)S(1)} %get-tuple-element.35.pairs_ref, bf16[128,512]{1,0:T(8,128)(2,1)S(1)} %get-tuple-element.43.mine_ref, bf16[128,512]{1,0:T(8,128)(2,1)S(1)} %collective-permute-done.7.theirs_ref, bf16[97,128,128]{2,1,0:T(8,128)(2,1)S(1)} %get-tuple-element.36.tiles_ref, ...), custom_call_target="tpu_custom_call" | custom-call | tf_op jit(solution)/shard_map/scatter_own/pallas_call | solution.py:388
  43.5 1.3 %collective-permute-done.13.g1_ref = bf16[64,256]{1,0:T(8,128)(2,1)S(1)} collective-permute-done((bf16[64,256]{1,0:T(8,128)(2,1)S(1)}, bf16[64,256]{1,0:T(8,128)(2,1)S(1)}, u32[]{:S(2)}, u32[]{:S(2)}) %collective-permute-start.13) | collective-permute-done | bytes 32800 | tf_op jit(solution)/shard_map/ppermute | solution.py:544
  45.1 1.3 %collective-permute-done.15.g3_ref = bf16[64,256]{1,0:T(8,128)(2,1)S(1)} collective-permute-done((bf16[64,256]{1,0:T(8,128)(2,1)S(1)}, bf16[64,256]{1,0:T(8,128)(2,1)S(1)}, u32[]{:S(2)}, u32[]{:S(2)}) %collective-permute-start.15) | collective-permute-done | bytes 32800 | tf_op jit(solution)/shard_map/ppermute | solution.py:544
  46.8 1.6 %collective-permute-start.16 = (bf16[9,128,128]{2,1,0:T(8,128)(2,1)S(1)}, bf16[9,128,128]{2,1,0:T(8,128)(2,1)S(1)}, u32[]{:S(2)}, u32[]{:S(2)}) collective-permute-start(bf16[9,128,128]{2,1,0:T(8,128)(2,1)S(1)} %get-tuple-element.56.mine_ref), channel_id=1, source_target_pairs={{0,2},{1,3},{2,0},{3,1},{4,6},{5,7},{6,4},{7,5},{8,10},{9,11},{10,... | collective-permute-start | bytes 884744 | tf_op jit(solution)/shard_map/ppermute | solution.py:421
  49.2 1.5 %collective-permute-start.19 = (bf16[128,128]{1,0:T(8,128)(2,1)S(1)}, bf16[128,128]{1,0:T(8,128)(2,1)S(1)}, u32[]{:S(2)}, u32[]{:S(2)}) collective-permute-start(bf16[128,128]{1,0:T(8,128)(2,1)S(1)} %get-tuple-element.62), channel_id=1, source_target_pairs={{0,4},{1,5},{2,6},{3,7},{4,0},{5,1},{6,2},{7,3},{8,12},{9,13},{10,... | collective-permute-start | bytes 98312 | tf_op jit(solution)/shard_map/ppermute | solution.py:509
  51.2 1.5 %output.1 = bf16[1024,256]{1,0:T(8,128)(2,1)} custom-call(s32[1,1024]{1,0:T(1,128)S(1)} %copy-done.2, bf16[512,256]{1,0:T(8,128)(2,1)S(1)} %get-tuple-element.57.own_ref, bf16[512,256]{1,0:T(8,128)(2,1)S(1)} %collective-permute-done.17.core_ref), custom_call_target="tpu_custom_call" | custom-call | tf_op jit(solution)/shard_map/output/pallas_call | solution.py:388
  52.8 3.3 %collective-permute-done.16.theirs_ref = bf16[9,128,128]{2,1,0:T(8,128)(2,1)S(1)} collective-permute-done((bf16[9,128,128]{2,1,0:T(8,128)(2,1)S(1)}, bf16[9,128,128]{2,1,0:T(8,128)(2,1)S(1)}, u32[]{:S(2)}, u32[]{:S(2)}) %collective-permute-start.16) | collective-permute-done | bytes 294944 | tf_op jit(solution)/shard_map/ppermute | solution.py:421
  56.3 1.7 %collective-permute-done.21.core_ref = bf16[12,128,128]{2,1,0:T(8,128)(2,1)S(1)} collective-permute-done((bf16[12,128,128]{2,1,0:T(8,128)(2,1)S(1)}, bf16[12,128,128]{2,1,0:T(8,128)(2,1)S(1)}, u32[]{:S(2)}, u32[]{:S(2)}) %collective-permute-start.21) | collective-permute-done | bytes 393248 | tf_op jit(solution)/shard_map/ppermute | solution.py:418
  58.0 1.6 %restore.1 = (bf16[1024,256]{1,0:T(8,128)(2,1)}, f32[256,256]{1,0:T(8,128)}, f32[256,256]{1,0:T(8,128)}) custom-call(s32[1,1024]{1,0:T(1,128)S(1)} %copy-done.2, bf16[12,128,128]{2,1,0:T(8,128)(2,1)S(1)} %total.1.own_ref, bf16[12,128,128]{2,1,0:T(8,128)(2,1)S(1)} %collective-permute-done.21.core_ref), custom_call_target="tpu_custom_call" | custom-call | tf_op jit(solution)/shard_map/restore/pallas_call | solution.py:388
  (41 shorter events, 8.0 us)
Async XLA Ops:
  0.6 10.9 %collective-permute-start.1 = (bf16[48,128,128]{2,1,0:T(8,128)(2,1)}, bf16[48,128,128]{2,1,0:T(8,128)(2,1)S(1)}, u32[]{:S(2)}, u32[]{:S(2)}) collective-permute-start(bf16[48,128,128]{2,1,0:T(8,128)(2,1)} %bitcast.7), channel_id=1, source_target_pairs={{0,1},{1,0},{2,3},{3,2},{4,5},{5,4},{6,7},{7,6},{8,9},{9,8},{10,11... | collective-permute-start | bytes 4718600 | tf_op jit(solution)/shard_map/ppermute | solution.py:418
  2.8 15.2 %collective-permute-start.2 = (bf16[1024,128]{1,0:T(8,128)(2,1)S(1)}, bf16[1024,128]{1,0:T(8,128)(2,1)S(1)}, u32[]{:S(2)}, u32[]{:S(2)}) collective-permute-start(bf16[1024,128]{1,0:T(8,128)(2,1)S(1)} %reorder.1.after_ref.own_ref), channel_id=1, source_target_pairs={{0,4},{4,0},{8,12},{12,8},{16,20},{20,16},{24,28},{28,24},{1,5},{5... | collective-permute-start | bytes 786440 | tf_op jit(solution)/shard_map/ppermute | solution.py:412
  5.4 12.6 %collective-permute-start.3 = (bf16[1024,128]{1,0:T(8,128)(2,1)S(1)}, bf16[1024,128]{1,0:T(8,128)(2,1)S(1)}, u32[]{:S(2)}, u32[]{:S(2)}) collective-permute-start(bf16[1024,128]{1,0:T(8,128)(2,1)S(1)} %reorder.1.after_ref.own_ref), channel_id=1, source_target_pairs={{0,28},{4,8},{8,4},{12,16},{16,12},{20,24},{24,20},{28,0},{1,29},{... | collective-permute-start | bytes 786440 | tf_op jit(solution)/shard_map/ppermute | solution.py:415
  10.3 1.2 %collective-permute-start = (s32[8,128]{1,0:T(8,128)S(1)}, s32[8,128]{1,0:T(8,128)S(1)}, u32[]{:S(2)}, u32[]{:S(2)}) collective-permute-start(s32[8,128]{1,0:T(8,128)S(1)} %index.1.mine), channel_id=1, source_target_pairs={{0,1},{1,0},{2,3},{3,2},{4,5},{5,4},{6,7},{7,6},{8,9},{9,8},{10,11... | collective-permute-start | bytes 12296 | tf_op jit(solution)/shard_map/ppermute | solution.py:418
  15.7 11.7 %copy-start.1 = (bf16[256,256]{1,0:T(8,128)(2,1)S(1)}, bf16[256,256]{1,0:T(8,128)(2,1)}, u32[]{:S(2)}) copy-start(bf16[256,256]{1,0:T(8,128)(2,1)} %wn_ref.1) | copy-start | bytes 393220
  19.7 5.9 %collective-permute-start.4 = (bf16[512,128]{1,0:T(8,128)(2,1)S(1)}, bf16[512,128]{1,0:T(8,128)(2,1)S(1)}, u32[]{:S(2)}, u32[]{:S(2)}) collective-permute-start(bf16[512,128]{1,0:T(8,128)(2,1)S(1)} %get-tuple-element.37.own_ref), channel_id=1, source_target_pairs={{0,2},{1,3},{2,0},{3,1},{4,6},{5,7},{6,4},{7,5},{8,10},{9,11},{10,... | collective-permute-start | bytes 393224 | tf_op jit(solution)/shard_map/ppermute | solution.py:421
  21.5 5.8 %collective-permute-start.5 = (bf16[512,128]{1,0:T(8,128)(2,1)S(1)}, bf16[512,128]{1,0:T(8,128)(2,1)S(1)}, u32[]{:S(2)}, u32[]{:S(2)}) collective-permute-start(bf16[512,128]{1,0:T(8,128)(2,1)S(1)} %get-tuple-element.38), channel_id=1, source_target_pairs={{0,3},{1,2},{2,1},{3,0},{4,7},{5,6},{6,5},{7,4},{8,11},{9,10},{10,... | collective-permute-start | bytes 393224 | tf_op jit(solution)/shard_map/ppermute | solution.py:424
  21.5 5.8 %collective-permute-start.6 = (bf16[512,128]{1,0:T(8,128)(2,1)S(1)}, bf16[512,128]{1,0:T(8,128)(2,1)S(1)}, u32[]{:S(2)}, u32[]{:S(2)}) collective-permute-start(bf16[512,128]{1,0:T(8,128)(2,1)S(1)} %get-tuple-element.38), channel_id=1, source_target_pairs={{0,1},{1,0},{2,3},{3,2},{4,5},{5,4},{6,7},{7,6},{8,9},{9,8},{10,11... | collective-permute-start | bytes 393224 | tf_op jit(solution)/shard_map/ppermute | solution.py:418
  28.0 2.7 %collective-permute-start.7 = (bf16[128,512]{1,0:T(8,128)(2,1)S(1)}, bf16[128,512]{1,0:T(8,128)(2,1)S(1)}, u32[]{:S(2)}, u32[]{:S(2)}) collective-permute-start(bf16[128,512]{1,0:T(8,128)(2,1)S(1)} %get-tuple-element.44), channel_id=1, source_target_pairs={{0,1},{1,0},{2,3},{3,2},{4,5},{5,4},{6,7},{7,6},{8,9},{9,8},{10,11... | collective-permute-start | bytes 393224 | tf_op jit(solution)/shard_map/ppermute | solution.py:418
  28.8 8.8 %collective-permute-start.10 = (bf16[64,256]{1,0:T(8,128)(2,1)S(1)}, bf16[64,256]{1,0:T(8,128)(2,1)S(1)}, u32[]{:S(2)}, u32[]{:S(2)}) collective-permute-start(bf16[64,256]{1,0:T(8,128)(2,1)S(1)} %get-tuple-element.51), channel_id=1, source_target_pairs={{0,1},{1,0},{2,3},{3,2},{4,5},{5,4},{6,7},{7,6},{8,9},{9,8},{10,11... | collective-permute-start | bytes 98312 | tf_op jit(solution)/shard_map/ppermute | solution.py:418
  29.0 8.6 %collective-permute-start.11 = (bf16[64,256]{1,0:T(8,128)(2,1)S(1)}, bf16[64,256]{1,0:T(8,128)(2,1)S(1)}, u32[]{:S(2)}, u32[]{:S(2)}) collective-permute-start(bf16[64,256]{1,0:T(8,128)(2,1)S(1)} %get-tuple-element.52), channel_id=1, source_target_pairs={{0,4},{1,5},{2,6},{3,7},{4,0},{5,1},{6,2},{7,3},{8,12},{9,13},{10,... | collective-permute-start | bytes 98312 | tf_op jit(solution)/shard_map/ppermute | solution.py:509
  30.4 7.1 %collective-permute-start.12 = (bf16[64,256]{1,0:T(8,128)(2,1)S(1)}, bf16[64,256]{1,0:T(8,128)(2,1)S(1)}, u32[]{:S(2)}, u32[]{:S(2)}) collective-permute-start(bf16[64,256]{1,0:T(8,128)(2,1)S(1)} %get-tuple-element.53), channel_id=1, source_target_pairs={{0,5},{1,4},{2,7},{3,6},{4,1},{5,0},{6,3},{7,2},{8,13},{9,12},{10,... | collective-permute-start | bytes 98312 | tf_op jit(solution)/shard_map/ppermute | solution.py:509
  32.4 14.3 %collective-permute-start.8 = (bf16[8,128,128]{2,1,0:T(8,128)(2,1)S(1)}, bf16[8,128,128]{2,1,0:T(8,128)(2,1)S(1)}, u32[]{:S(2)}, u32[]{:S(2)}) collective-permute-start(bf16[8,128,128]{2,1,0:T(8,128)(2,1)S(1)} %get-tuple-element.45.after_ref), channel_id=1, source_target_pairs={{0,4},{4,0},{8,12},{12,8},{16,20},{20,16},{24,28},{28,24},{1,5},{5... | collective-permute-start | bytes 786440 | tf_op jit(solution)/shard_map/ppermute | solution.py:412
  34.0 12.7 %collective-permute-start.9 = (bf16[8,128,128]{2,1,0:T(8,128)(2,1)S(1)}, bf16[8,128,128]{2,1,0:T(8,128)(2,1)S(1)}, u32[]{:S(2)}, u32[]{:S(2)}) collective-permute-start(bf16[8,128,128]{2,1,0:T(8,128)(2,1)S(1)} %get-tuple-element.46), channel_id=1, source_target_pairs={{0,28},{4,8},{8,4},{12,16},{16,12},{20,24},{24,20},{28,0},{1,29},{... | collective-permute-start | bytes 786440 | tf_op jit(solution)/shard_map/ppermute | solution.py:415
  37.6 10.8 %copy-start = (bf16[256,256]{1,0:T(8,128)(2,1)S(1)}, bf16[256,256]{1,0:T(8,128)(2,1)}, u32[]{:S(2)}) copy-start(bf16[256,256]{1,0:T(8,128)(2,1)} %ws_ref.1) | copy-start | bytes 393220
  37.6 7.2 %collective-permute-start.13 = (bf16[64,256]{1,0:T(8,128)(2,1)S(1)}, bf16[64,256]{1,0:T(8,128)(2,1)S(1)}, u32[]{:S(2)}, u32[]{:S(2)}) collective-permute-start(bf16[64,256]{1,0:T(8,128)(2,1)S(1)} %add_convert_fusion.g0_ref), channel_id=1, source_target_pairs={{0,8},{4,12},{8,0},{12,4},{16,24},{20,28},{24,16},{28,20},{1,9},{5... | collective-permute-start | bytes 98312 | tf_op jit(solution)/shard_map/ppermute | solution.py:544
  37.7 7.5 %collective-permute-start.14 = (bf16[64,256]{1,0:T(8,128)(2,1)S(1)}, bf16[64,256]{1,0:T(8,128)(2,1)S(1)}, u32[]{:S(2)}, u32[]{:S(2)}) collective-permute-start(bf16[64,256]{1,0:T(8,128)(2,1)S(1)} %add_convert_fusion.g0_ref), channel_id=1, source_target_pairs={{0,16},{4,20},{8,24},{12,28},{16,0},{20,4},{24,8},{28,12},{1,17},{... | collective-permute-start | bytes 98312 | tf_op jit(solution)/shard_map/ppermute | solution.py:544
  38.7 7.7 %collective-permute-start.15 = (bf16[64,256]{1,0:T(8,128)(2,1)S(1)}, bf16[64,256]{1,0:T(8,128)(2,1)S(1)}, u32[]{:S(2)}, u32[]{:S(2)}) collective-permute-start(bf16[64,256]{1,0:T(8,128)(2,1)S(1)} %add_convert_fusion.g0_ref), channel_id=1, source_target_pairs={{0,24},{4,28},{8,16},{12,20},{16,8},{20,12},{24,0},{28,4},{1,25},{... | collective-permute-start | bytes 98312 | tf_op jit(solution)/shard_map/ppermute | solution.py:544
  46.8 9.3 %collective-permute-start.16 = (bf16[9,128,128]{2,1,0:T(8,128)(2,1)S(1)}, bf16[9,128,128]{2,1,0:T(8,128)(2,1)S(1)}, u32[]{:S(2)}, u32[]{:S(2)}) collective-permute-start(bf16[9,128,128]{2,1,0:T(8,128)(2,1)S(1)} %get-tuple-element.56.mine_ref), channel_id=1, source_target_pairs={{0,2},{1,3},{2,0},{3,1},{4,6},{5,7},{6,4},{7,5},{8,10},{9,11},{10,... | collective-permute-start | bytes 884744 | tf_op jit(solution)/shard_map/ppermute | solution.py:421
  48.4 2.9 %collective-permute-start.17 = (bf16[512,256]{1,0:T(8,128)(2,1)S(1)}, bf16[512,256]{1,0:T(8,128)(2,1)S(1)}, u32[]{:S(2)}, u32[]{:S(2)}) collective-permute-start(bf16[512,256]{1,0:T(8,128)(2,1)S(1)} %get-tuple-element.57.own_ref), channel_id=1, source_target_pairs={{0,1},{1,0},{2,3},{3,2},{4,5},{5,4},{6,7},{7,6},{8,9},{9,8},{10,11... | collective-permute-start | bytes 786440 | tf_op jit(solution)/shard_map/ppermute | solution.py:418
  48.7 7.5 %collective-permute-start.18 = (f32[128,512]{1,0:T(8,128)S(1)}, f32[128,512]{1,0:T(8,128)S(1)}, u32[]{:S(2)}, u32[]{:S(2)}) collective-permute-start(f32[128,512]{1,0:T(8,128)S(1)} %get-tuple-element.61), channel_id=1, source_target_pairs={{0,1},{1,0},{2,3},{3,2},{4,5},{5,4},{6,7},{7,6},{8,9},{9,8},{10,11... | collective-permute-start | bytes 786440 | tf_op jit(solution)/shard_map/ppermute | solution.py:418
  49.2 6.9 %collective-permute-start.19 = (bf16[128,128]{1,0:T(8,128)(2,1)S(1)}, bf16[128,128]{1,0:T(8,128)(2,1)S(1)}, u32[]{:S(2)}, u32[]{:S(2)}) collective-permute-start(bf16[128,128]{1,0:T(8,128)(2,1)S(1)} %get-tuple-element.62), channel_id=1, source_target_pairs={{0,4},{1,5},{2,6},{3,7},{4,0},{5,1},{6,2},{7,3},{8,12},{9,13},{10,... | collective-permute-start | bytes 98312 | tf_op jit(solution)/shard_map/ppermute | solution.py:509
  50.7 5.4 %collective-permute-start.20 = (bf16[128,128]{1,0:T(8,128)(2,1)S(1)}, bf16[128,128]{1,0:T(8,128)(2,1)S(1)}, u32[]{:S(2)}, u32[]{:S(2)}) collective-permute-start(bf16[128,128]{1,0:T(8,128)(2,1)S(1)} %get-tuple-element.62), channel_id=1, source_target_pairs={{0,6},{1,7},{2,4},{3,5},{4,2},{5,3},{6,0},{7,1},{8,14},{9,15},{10,... | collective-permute-start | bytes 98312 | tf_op jit(solution)/shard_map/ppermute | solution.py:509
  56.3 1.8 %collective-permute-start.21 = (bf16[12,128,128]{2,1,0:T(8,128)(2,1)S(1)}, bf16[12,128,128]{2,1,0:T(8,128)(2,1)S(1)}, u32[]{:S(2)}, u32[]{:S(2)}) collective-permute-start(bf16[12,128,128]{2,1,0:T(8,128)(2,1)S(1)} %total.1.own_ref), channel_id=1, source_target_pairs={{0,1},{1,0},{2,3},{3,2},{4,5},{5,4},{6,7},{7,6},{8,9},{9,8},{10,11... | collective-permute-start | bytes 1179656 | tf_op jit(solution)/shard_map/ppermute | solution.py:418
  (1 other events, 7.8 us)

commit v9 on v8

--- a/solution.py
+++ b/solution.py
@@ -210,7 +210,7 @@
         return win[pl.ds(pl.multiple_of(col * T, T), T), :]
 
     most = (tiles_ref.shape[0] - 1 + tiles) // 2
-    for_pairs(pairs_ref, 0, most * 3 // 4, most, lambda p: gather_pair(pairs_ref, 0, p, tiles_ref, window, acc))
+    for_pairs(pairs_ref, 0, most * 5 // 6, most, lambda p: gather_pair(pairs_ref, 0, p, tiles_ref, window, acc))
     for i in range(tiles // 2):
         here_ref[i * T : (i + 1) * T, :] = acc[c * (tiles // 2) + i].astype(BF)
         other_ref[i * T : (i + 1) * T, :] = acc[(1 - c) * (tiles // 2) + i].astype(BF)
@@ -288,7 +288,7 @@
         acc[at(pairs_ref[base + 4, p])] += prod[:, T:]
 
     most = (tiles_ref.shape[0] - 1 + tiles) // 2
-    for_pairs(pairs_ref, base, most // 2 if base else most * 3 // 4, most, body)
+    for_pairs(pairs_ref, base, most // 2 if base else most * 5 // 6, most, body)
 
 
 def scatter_kernel(pairs_ref, mine_ref, theirs_ref, tiles_ref, near_ref, far_ref, src, acc):
@@ -541,7 +541,7 @@
     for at in range(1, bits, 2):
         g = four(*parts)
         parts = [g] + [
-            lax.ppermute(g, "blk", [(b, b ^ (k << at)) for b in range(blocks)]) for k in (1, 2, 3)
+            lax.ppermute(g, "blk", [(b, b ^ (k << at)) for b in range(blocks)]) for k in (3, 2, 1)
         ]
     chip, w_own = call(chip_kernel, [((tiles + 1, T, T), BF), ((T, T), BF)], [own, from_near, from_far] + parts, name="chip")
     chip, act = lax.optimization_barrier((chip, act))

time: 59.9 us -> 60 us (level)
    ppermute x2, waiting for transfers between devices: 2.56 us -> 3.22 us  [swap_near(): return lax.ppermute(x, 'blk', [(b, b ^ 1) for b in range(blocks)])]
    ppermute x3, waiting for transfers between devices: 2.94 us -> 2.3 us  [shards(): lax.ppermute(g, 'blk', [(b, b ^ k << at) for b in range(blocks)])]
  transfers between devices with their start and end apart: 22 -> 22, of which waited for: 10 -> 8; matrix products, arithmetic and copies ran while one was open for 0% -> 0% of each run, Pallas kernels for 20% -> 20%
where the time goes in v9:
time: 60 us; the launch traced here: 59.8 us
  starting transfers between devices  25.1 us (42%)
  waiting for transfers between devices  17.2 us (29%)
  Pallas kernels  16.1 us (27%)
  between operations  1.42 us (2%)
    pallas_call x14, Pallas kernels, call(): pl.pallas_call(kernel, out_shape=shapes[0] if single else shapes, in_spec...  16.1 us
    ppermute x2, starting transfers between devices, swap_far(): lax.ppermute(x, 'blk', [(b, (b + 2 * (b % 2) - 1) % blocks) for b in rang...  7.13 us
    ppermute x2, waiting for transfers between devices, swap_y(): return lax.ppermute(x, 'rep', [(r, r ^ 2) for r in range(reps)])  7.04 us
    ppermute x3, starting transfers between devices, shards(): lax.ppermute(g, 'blk', [(b, b ^ k << at) for b in range(blocks)])  4.45 us
    ppermute x2, starting transfers between devices, swap_near(): return lax.ppermute(x, 'blk', [(b, b ^ 1) for b in range(blocks)])  4.19 us
    ppermute x4, starting transfers between devices, swap_pair(): return lax.ppermute(x, ('blk', 'rep'), pairs_of)  3.71 us
    ppermute x2, starting transfers between devices, swap_y(): return lax.ppermute(x, 'rep', [(r, r ^ 2) for r in range(reps)])  3.38 us
    ppermute x2, waiting for transfers between devices, swap_near(): return lax.ppermute(x, 'blk', [(b, b ^ 1) for b in range(blocks)])  3.22 us
  transfers between devices with their start and end apart: 22, of which 8 were waited for; matrix products, arithmetic and copies ran while one was open for 0% of the time, Pallas kernels for 20%

profile of v9, /device:TPU:0, one launch (start us, length us, event | category | flops | bytes accessed | tf_op | source)
XLA Modules:
  0.0 59.8 jit_solution(5817714149993371782)
XLA Ops:
  1.1 1.7 %reorder.1.after_ref.own_ref = bf16[1024,128]{1,0:T(8,128)(2,1)S(1)} custom-call(s32[8,128]{1,0:T(8,128)} %bitcast.5, bf16[1024,256]{1,0:T(8,128)(2,1)} %x_ref.1), custom_call_target="tpu_custom_call" | custom-call | tf_op jit(solution)/shard_map/reorder/pallas_call | solution.py:388
  2.8 2.6 %collective-permute-start.2 = (bf16[1024,128]{1,0:T(8,128)(2,1)S(1)}, bf16[1024,128]{1,0:T(8,128)(2,1)S(1)}, u32[]{:S(2)}, u32[]{:S(2)}) collective-permute-start(bf16[1024,128]{1,0:T(8,128)(2,1)S(1)} %reorder.1.after_ref.own_ref), channel_id=1, source_target_pairs={{0,4},{4,0},{8,12},{12,8},{16,20},{20,16},{24,28},{28,24},{1,5},{5... | collective-permute-start | bytes 786440 | tf_op jit(solution)/shard_map/ppermute | solution.py:412
  5.4 3.6 %collective-permute-start.3 = (bf16[1024,128]{1,0:T(8,128)(2,1)S(1)}, bf16[1024,128]{1,0:T(8,128)(2,1)S(1)}, u32[]{:S(2)}, u32[]{:S(2)}) collective-permute-start(bf16[1024,128]{1,0:T(8,128)(2,1)S(1)} %reorder.1.after_ref.own_ref), channel_id=1, source_target_pairs={{0,28},{4,8},{8,4},{12,16},{16,12},{20,24},{24,20},{28,0},{1,29},{... | collective-permute-start | bytes 786440 | tf_op jit(solution)/shard_map/ppermute | solution.py:415
  10.3 1.2 %collective-permute-done.theirs = s32[8,128]{1,0:T(8,128)S(1)} collective-permute-done((s32[8,128]{1,0:T(8,128)S(1)}, s32[8,128]{1,0:T(8,128)S(1)}, u32[]{:S(2)}, u32[]{:S(2)}) %collective-permute-start) | collective-permute-done | bytes 4128 | tf_op jit(solution)/shard_map/ppermute | solution.py:418
  11.5 2.9 %prepare.1 = (bf16[512,256]{1,0:T(8,128)(2,1)S(1)}, bf16[512,256]{1,0:T(8,128)(2,1)S(1)}, f32[512,256]{1,0:T(8,128)S(1)}, f32[512,128]{1,0:T(8,128)S(1)}, f32[8,...) custom-call(s32[8,128]{1,0:T(8,128)S(1)} %index.1.mine, ...), custom_call_target="tpu_custom_call" | custom-call | tf_op jit(solution)/shard_map/prepare/pallas_call | solution.py:388
  14.4 1.3 %gather_own.1.start_ref = f32[9,128,128]{2,1,0:T(8,128)S(1)} custom-call(s32[16,128]{1,0:T(8,128)S(1)} %get-tuple-element.35.pairs_ref, bf16[1024,128]{1,0:T(8,128)(2,1)S(1)} %reorder.1.after_ref.own_ref, bf16[97,128,128]{2,1,0:T(8,128)(2,1)S(1)} %get-tuple-element.36.tiles_ref), custom_call_target="tpu_custom_call" | custom-call | tf_op jit(solution)/shard_map/gather_own/pallas_call | solution.py:388
  15.7 2.3 %collective-permute-done.2.near_ref = bf16[1024,128]{1,0:T(8,128)(2,1)S(1)} collective-permute-done((bf16[1024,128]{1,0:T(8,128)(2,1)S(1)}, bf16[1024,128]{1,0:T(8,128)(2,1)S(1)}, u32[]{:S(2)}, u32[]{:S(2)}) %collective-permute-start.2) | collective-permute-done | bytes 262176 | tf_op jit(solution)/shard_map/ppermute | solution.py:412
  18.0 1.8 %gather.1 = (bf16[512,128]{1,0:T(8,128)(2,1)S(1)}, bf16[512,128]{1,0:T(8,128)(2,1)S(1)}) custom-call(s32[16,128]{1,0:T(8,128)S(1)} %get-tuple-element.35.pairs_ref, bf16[1024,128]{1,0:T(8,128)(2,1)S(1)} %collective-permute-done.2.near_ref, f32[9,128,128]{2,1,0:T(8,128)S(1)} %gather_own.1.start_ref, bf16[1024,128]{1,0:T(8,128)(2,1)S(1)} %collective-permute-done.3.far_ref, ...), custom_call_target="tpu_custom_call" | custom-call | tf_op jit(solution)/shard_map/gather/pallas_call | solution.py:388
  19.8 1.8 %collective-permute-start.4 = (bf16[512,128]{1,0:T(8,128)(2,1)S(1)}, bf16[512,128]{1,0:T(8,128)(2,1)S(1)}, u32[]{:S(2)}, u32[]{:S(2)}) collective-permute-start(bf16[512,128]{1,0:T(8,128)(2,1)S(1)} %get-tuple-element.37.own_ref), channel_id=1, source_target_pairs={{0,2},{1,3},{2,0},{3,1},{4,6},{5,7},{6,4},{7,5},{8,10},{9,11},{10,... | collective-permute-start | bytes 393224 | tf_op jit(solution)/shard_map/ppermute | solution.py:421
  22.0 3.7 %collective-permute-done.4.y_ref = bf16[512,128]{1,0:T(8,128)(2,1)S(1)} collective-permute-done((bf16[512,128]{1,0:T(8,128)(2,1)S(1)}, bf16[512,128]{1,0:T(8,128)(2,1)S(1)}, u32[]{:S(2)}, u32[]{:S(2)}) %collective-permute-start.4) | collective-permute-done | bytes 131104 | tf_op jit(solution)/shard_map/ppermute | solution.py:421
  25.7 1.7 %collective-permute-done.5.diag_ref = bf16[512,128]{1,0:T(8,128)(2,1)S(1)} collective-permute-done((bf16[512,128]{1,0:T(8,128)(2,1)S(1)}, bf16[512,128]{1,0:T(8,128)(2,1)S(1)}, u32[]{:S(2)}, u32[]{:S(2)}) %collective-permute-start.5) | collective-permute-done | bytes 131104 | tf_op jit(solution)/shard_map/ppermute | solution.py:424
  29.1 1.5 %collective-permute-start.11 = (bf16[64,256]{1,0:T(8,128)(2,1)S(1)}, bf16[64,256]{1,0:T(8,128)(2,1)S(1)}, u32[]{:S(2)}, u32[]{:S(2)}) collective-permute-start(bf16[64,256]{1,0:T(8,128)(2,1)S(1)} %get-tuple-element.52), channel_id=1, source_target_pairs={{0,4},{1,5},{2,6},{3,7},{4,0},{5,1},{6,2},{7,3},{8,12},{9,13},{10,... | collective-permute-start | bytes 98312 | tf_op jit(solution)/shard_map/ppermute | solution.py:509
  30.8 1.8 %scatter.1 = (bf16[8,128,128]{2,1,0:T(8,128)(2,1)S(1)}, bf16[8,128,128]{2,1,0:T(8,128)(2,1)S(1)}) custom-call(s32[16,128]{1,0:T(8,128)S(1)} %get-tuple-element.35.pairs_ref, bf16[128,512]{1,0:T(8,128)(2,1)S(1)} %get-tuple-element.43.mine_ref, bf16[128,512]{1,0:T(8,128)(2,1)S(1)} %collective-permute-done.7.theirs_ref, ...), custom_call_target="tpu_custom_call" | custom-call | tf_op jit(solution)/shard_map/scatter/pallas_call | solution.py:388
  32.5 1.6 %collective-permute-start.8 = (bf16[8,128,128]{2,1,0:T(8,128)(2,1)S(1)}, bf16[8,128,128]{2,1,0:T(8,128)(2,1)S(1)}, u32[]{:S(2)}, u32[]{:S(2)}) collective-permute-start(bf16[8,128,128]{2,1,0:T(8,128)(2,1)S(1)} %get-tuple-element.45.after_ref), channel_id=1, source_target_pairs={{0,4},{4,0},{8,12},{12,8},{16,20},{20,16},{24,28},{28,24},{1,5},{5... | collective-permute-start | bytes 786440 | tf_op jit(solution)/shard_map/ppermute | solution.py:412
  34.2 3.6 %collective-permute-start.9 = (bf16[8,128,128]{2,1,0:T(8,128)(2,1)S(1)}, bf16[8,128,128]{2,1,0:T(8,128)(2,1)S(1)}, u32[]{:S(2)}, u32[]{:S(2)}) collective-permute-start(bf16[8,128,128]{2,1,0:T(8,128)(2,1)S(1)} %get-tuple-element.46), channel_id=1, source_target_pairs={{0,28},{4,8},{8,4},{12,16},{16,12},{20,24},{24,20},{28,0},{1,29},{... | collective-permute-start | bytes 786440 | tf_op jit(solution)/shard_map/ppermute | solution.py:415
  38.3 3.9 %collective-permute-start.15 = (bf16[64,256]{1,0:T(8,128)(2,1)S(1)}, bf16[64,256]{1,0:T(8,128)(2,1)S(1)}, u32[]{:S(2)}, u32[]{:S(2)}) collective-permute-start(bf16[64,256]{1,0:T(8,128)(2,1)S(1)} %add_convert_fusion.g0_ref), channel_id=1, source_target_pairs={{0,8},{4,12},{8,0},{12,4},{16,24},{20,28},{24,16},{28,20},{1,9},{5... | collective-permute-start | bytes 98312 | tf_op jit(solution)/shard_map/ppermute | solution.py:544
  42.2 1.4 %scatter_own.1.own_ref = f32[8,128,128]{2,1,0:T(8,128)S(1)} custom-call(s32[16,128]{1,0:T(8,128)S(1)} %get-tuple-element.35.pairs_ref, bf16[128,512]{1,0:T(8,128)(2,1)S(1)} %get-tuple-element.43.mine_ref, bf16[128,512]{1,0:T(8,128)(2,1)S(1)} %collective-permute-done.7.theirs_ref, bf16[97,128,128]{2,1,0:T(8,128)(2,1)S(1)} %get-tuple-element.36.tiles_ref, ...), custom_call_target="tpu_custom_call" | custom-call | tf_op jit(solution)/shard_map/scatter_own/pallas_call | solution.py:388
  43.6 2.3 %collective-permute-done.13.g1_ref = bf16[64,256]{1,0:T(8,128)(2,1)S(1)} collective-permute-done((bf16[64,256]{1,0:T(8,128)(2,1)S(1)}, bf16[64,256]{1,0:T(8,128)(2,1)S(1)}, u32[]{:S(2)}, u32[]{:S(2)}) %collective-permute-start.13) | collective-permute-done | bytes 32800 | tf_op jit(solution)/shard_map/ppermute | solution.py:544
  47.0 1.5 %collective-permute-start.16 = (bf16[9,128,128]{2,1,0:T(8,128)(2,1)S(1)}, bf16[9,128,128]{2,1,0:T(8,128)(2,1)S(1)}, u32[]{:S(2)}, u32[]{:S(2)}) collective-permute-start(bf16[9,128,128]{2,1,0:T(8,128)(2,1)S(1)} %get-tuple-element.56.mine_ref), channel_id=1, source_target_pairs={{0,2},{1,3},{2,0},{3,1},{4,6},{5,7},{6,4},{7,5},{8,10},{9,11},{10,... | collective-permute-start | bytes 884744 | tf_op jit(solution)/shard_map/ppermute | solution.py:421
  49.4 1.7 %collective-permute-start.19 = (bf16[128,128]{1,0:T(8,128)(2,1)S(1)}, bf16[128,128]{1,0:T(8,128)(2,1)S(1)}, u32[]{:S(2)}, u32[]{:S(2)}) collective-permute-start(bf16[128,128]{1,0:T(8,128)(2,1)S(1)} %get-tuple-element.62), channel_id=1, source_target_pairs={{0,4},{1,5},{2,6},{3,7},{4,0},{5,1},{6,2},{7,3},{8,12},{9,13},{10,... | collective-permute-start | bytes 98312 | tf_op jit(solution)/shard_map/ppermute | solution.py:509
  51.4 1.5 %output.1 = bf16[1024,256]{1,0:T(8,128)(2,1)} custom-call(s32[1,1024]{1,0:T(1,128)S(1)} %copy-done.2, bf16[512,256]{1,0:T(8,128)(2,1)S(1)} %get-tuple-element.57.own_ref, bf16[512,256]{1,0:T(8,128)(2,1)S(1)} %collective-permute-done.17.core_ref), custom_call_target="tpu_custom_call" | custom-call | tf_op jit(solution)/shard_map/output/pallas_call | solution.py:388
  53.0 3.3 %collective-permute-done.16.theirs_ref = bf16[9,128,128]{2,1,0:T(8,128)(2,1)S(1)} collective-permute-done((bf16[9,128,128]{2,1,0:T(8,128)(2,1)S(1)}, bf16[9,128,128]{2,1,0:T(8,128)(2,1)S(1)}, u32[]{:S(2)}, u32[]{:S(2)}) %collective-permute-start.16) | collective-permute-done | bytes 294944 | tf_op jit(solution)/shard_map/ppermute | solution.py:421
  56.5 1.7 %collective-permute-done.21.core_ref = bf16[12,128,128]{2,1,0:T(8,128)(2,1)S(1)} collective-permute-done((bf16[12,128,128]{2,1,0:T(8,128)(2,1)S(1)}, bf16[12,128,128]{2,1,0:T(8,128)(2,1)S(1)}, u32[]{:S(2)}, u32[]{:S(2)}) %collective-permute-start.21) | collective-permute-done | bytes 393248 | tf_op jit(solution)/shard_map/ppermute | solution.py:418
  58.2 1.6 %restore.1 = (bf16[1024,256]{1,0:T(8,128)(2,1)}, f32[256,256]{1,0:T(8,128)}, f32[256,256]{1,0:T(8,128)}) custom-call(s32[1,1024]{1,0:T(1,128)S(1)} %copy-done.2, bf16[12,128,128]{2,1,0:T(8,128)(2,1)S(1)} %total.1.own_ref, bf16[12,128,128]{2,1,0:T(8,128)(2,1)S(1)} %collective-permute-done.21.core_ref), custom_call_target="tpu_custom_call" | custom-call | tf_op jit(solution)/shard_map/restore/pallas_call | solution.py:388
  (41 shorter events, 6.4 us)
Async XLA Ops:
  0.6 10.9 %collective-permute-start.1 = (bf16[48,128,128]{2,1,0:T(8,128)(2,1)}, bf16[48,128,128]{2,1,0:T(8,128)(2,1)S(1)}, u32[]{:S(2)}, u32[]{:S(2)}) collective-permute-start(bf16[48,128,128]{2,1,0:T(8,128)(2,1)} %bitcast.7), channel_id=1, source_target_pairs={{0,1},{1,0},{2,3},{3,2},{4,5},{5,4},{6,7},{7,6},{8,9},{9,8},{10,11... | collective-permute-start | bytes 4718600 | tf_op jit(solution)/shard_map/ppermute | solution.py:418
  2.8 15.2 %collective-permute-start.2 = (bf16[1024,128]{1,0:T(8,128)(2,1)S(1)}, bf16[1024,128]{1,0:T(8,128)(2,1)S(1)}, u32[]{:S(2)}, u32[]{:S(2)}) collective-permute-start(bf16[1024,128]{1,0:T(8,128)(2,1)S(1)} %reorder.1.after_ref.own_ref), channel_id=1, source_target_pairs={{0,4},{4,0},{8,12},{12,8},{16,20},{20,16},{24,28},{28,24},{1,5},{5... | collective-permute-start | bytes 786440 | tf_op jit(solution)/shard_map/ppermute | solution.py:412
  5.4 12.6 %collective-permute-start.3 = (bf16[1024,128]{1,0:T(8,128)(2,1)S(1)}, bf16[1024,128]{1,0:T(8,128)(2,1)S(1)}, u32[]{:S(2)}, u32[]{:S(2)}) collective-permute-start(bf16[1024,128]{1,0:T(8,128)(2,1)S(1)} %reorder.1.after_ref.own_ref), channel_id=1, source_target_pairs={{0,28},{4,8},{8,4},{12,16},{16,12},{20,24},{24,20},{28,0},{1,29},{... | collective-permute-start | bytes 786440 | tf_op jit(solution)/shard_map/ppermute | solution.py:415
  10.3 1.2 %collective-permute-start = (s32[8,128]{1,0:T(8,128)S(1)}, s32[8,128]{1,0:T(8,128)S(1)}, u32[]{:S(2)}, u32[]{:S(2)}) collective-permute-start(s32[8,128]{1,0:T(8,128)S(1)} %index.1.mine), channel_id=1, source_target_pairs={{0,1},{1,0},{2,3},{3,2},{4,5},{5,4},{6,7},{7,6},{8,9},{9,8},{10,11... | collective-permute-start | bytes 12296 | tf_op jit(solution)/shard_map/ppermute | solution.py:418
  15.7 11.7 %copy-start.1 = (bf16[256,256]{1,0:T(8,128)(2,1)S(1)}, bf16[256,256]{1,0:T(8,128)(2,1)}, u32[]{:S(2)}) copy-start(bf16[256,256]{1,0:T(8,128)(2,1)} %wn_ref.1) | copy-start | bytes 393220
  19.8 5.9 %collective-permute-start.4 = (bf16[512,128]{1,0:T(8,128)(2,1)S(1)}, bf16[512,128]{1,0:T(8,128)(2,1)S(1)}, u32[]{:S(2)}, u32[]{:S(2)}) collective-permute-start(bf16[512,128]{1,0:T(8,128)(2,1)S(1)} %get-tuple-element.37.own_ref), channel_id=1, source_target_pairs={{0,2},{1,3},{2,0},{3,1},{4,6},{5,7},{6,4},{7,5},{8,10},{9,11},{10,... | collective-permute-start | bytes 393224 | tf_op jit(solution)/shard_map/ppermute | solution.py:421
  21.6 5.8 %collective-permute-start.5 = (bf16[512,128]{1,0:T(8,128)(2,1)S(1)}, bf16[512,128]{1,0:T(8,128)(2,1)S(1)}, u32[]{:S(2)}, u32[]{:S(2)}) collective-permute-start(bf16[512,128]{1,0:T(8,128)(2,1)S(1)} %get-tuple-element.38), channel_id=1, source_target_pairs={{0,3},{1,2},{2,1},{3,0},{4,7},{5,6},{6,5},{7,4},{8,11},{9,10},{10,... | collective-permute-start | bytes 393224 | tf_op jit(solution)/shard_map/ppermute | solution.py:424
  21.6 5.8 %collective-permute-start.6 = (bf16[512,128]{1,0:T(8,128)(2,1)S(1)}, bf16[512,128]{1,0:T(8,128)(2,1)S(1)}, u32[]{:S(2)}, u32[]{:S(2)}) collective-permute-start(bf16[512,128]{1,0:T(8,128)(2,1)S(1)} %get-tuple-element.38), channel_id=1, source_target_pairs={{0,1},{1,0},{2,3},{3,2},{4,5},{5,4},{6,7},{7,6},{8,9},{9,8},{10,11... | collective-permute-start | bytes 393224 | tf_op jit(solution)/shard_map/ppermute | solution.py:418
  28.1 2.7 %collective-permute-start.7 = (bf16[128,512]{1,0:T(8,128)(2,1)S(1)}, bf16[128,512]{1,0:T(8,128)(2,1)S(1)}, u32[]{:S(2)}, u32[]{:S(2)}) collective-permute-start(bf16[128,512]{1,0:T(8,128)(2,1)S(1)} %get-tuple-element.44), channel_id=1, source_target_pairs={{0,1},{1,0},{2,3},{3,2},{4,5},{5,4},{6,7},{7,6},{8,9},{9,8},{10,11... | collective-permute-start | bytes 393224 | tf_op jit(solution)/shard_map/ppermute | solution.py:418
  28.8 8.9 %collective-permute-start.10 = (bf16[64,256]{1,0:T(8,128)(2,1)S(1)}, bf16[64,256]{1,0:T(8,128)(2,1)S(1)}, u32[]{:S(2)}, u32[]{:S(2)}) collective-permute-start(bf16[64,256]{1,0:T(8,128)(2,1)S(1)} %get-tuple-element.51), channel_id=1, source_target_pairs={{0,1},{1,0},{2,3},{3,2},{4,5},{5,4},{6,7},{7,6},{8,9},{9,8},{10,11... | collective-permute-start | bytes 98312 | tf_op jit(solution)/shard_map/ppermute | solution.py:418
  29.1 8.7 %collective-permute-start.11 = (bf16[64,256]{1,0:T(8,128)(2,1)S(1)}, bf16[64,256]{1,0:T(8,128)(2,1)S(1)}, u32[]{:S(2)}, u32[]{:S(2)}) collective-permute-start(bf16[64,256]{1,0:T(8,128)(2,1)S(1)} %get-tuple-element.52), channel_id=1, source_target_pairs={{0,4},{1,5},{2,6},{3,7},{4,0},{5,1},{6,2},{7,3},{8,12},{9,13},{10,... | collective-permute-start | bytes 98312 | tf_op jit(solution)/shard_map/ppermute | solution.py:509
  30.5 7.2 %collective-permute-start.12 = (bf16[64,256]{1,0:T(8,128)(2,1)S(1)}, bf16[64,256]{1,0:T(8,128)(2,1)S(1)}, u32[]{:S(2)}, u32[]{:S(2)}) collective-permute-start(bf16[64,256]{1,0:T(8,128)(2,1)S(1)} %get-tuple-element.53), channel_id=1, source_target_pairs={{0,5},{1,4},{2,7},{3,6},{4,1},{5,0},{6,3},{7,2},{8,13},{9,12},{10,... | collective-permute-start | bytes 98312 | tf_op jit(solution)/shard_map/ppermute | solution.py:509
  32.5 14.3 %collective-permute-start.8 = (bf16[8,128,128]{2,1,0:T(8,128)(2,1)S(1)}, bf16[8,128,128]{2,1,0:T(8,128)(2,1)S(1)}, u32[]{:S(2)}, u32[]{:S(2)}) collective-permute-start(bf16[8,128,128]{2,1,0:T(8,128)(2,1)S(1)} %get-tuple-element.45.after_ref), channel_id=1, source_target_pairs={{0,4},{4,0},{8,12},{12,8},{16,20},{20,16},{24,28},{28,24},{1,5},{5... | collective-permute-start | bytes 786440 | tf_op jit(solution)/shard_map/ppermute | solution.py:412
  34.2 12.7 %collective-permute-start.9 = (bf16[8,128,128]{2,1,0:T(8,128)(2,1)S(1)}, bf16[8,128,128]{2,1,0:T(8,128)(2,1)S(1)}, u32[]{:S(2)}, u32[]{:S(2)}) collective-permute-start(bf16[8,128,128]{2,1,0:T(8,128)(2,1)S(1)} %get-tuple-element.46), channel_id=1, source_target_pairs={{0,28},{4,8},{8,4},{12,16},{16,12},{20,24},{24,20},{28,0},{1,29},{... | collective-permute-start | bytes 786440 | tf_op jit(solution)/shard_map/ppermute | solution.py:415
  37.8 10.8 %copy-start = (bf16[256,256]{1,0:T(8,128)(2,1)S(1)}, bf16[256,256]{1,0:T(8,128)(2,1)}, u32[]{:S(2)}) copy-start(bf16[256,256]{1,0:T(8,128)(2,1)} %ws_ref.1) | copy-start | bytes 393220
  37.8 8.2 %collective-permute-start.13 = (bf16[64,256]{1,0:T(8,128)(2,1)S(1)}, bf16[64,256]{1,0:T(8,128)(2,1)S(1)}, u32[]{:S(2)}, u32[]{:S(2)}) collective-permute-start(bf16[64,256]{1,0:T(8,128)(2,1)S(1)} %add_convert_fusion.g0_ref), channel_id=1, source_target_pairs={{0,24},{4,28},{8,16},{12,20},{16,8},{20,12},{24,0},{28,4},{1,25},{... | collective-permute-start | bytes 98312 | tf_op jit(solution)/shard_map/ppermute | solution.py:544
  38.3 7.6 %collective-permute-start.14 = (bf16[64,256]{1,0:T(8,128)(2,1)S(1)}, bf16[64,256]{1,0:T(8,128)(2,1)S(1)}, u32[]{:S(2)}, u32[]{:S(2)}) collective-permute-start(bf16[64,256]{1,0:T(8,128)(2,1)S(1)} %add_convert_fusion.g0_ref), channel_id=1, source_target_pairs={{0,16},{4,20},{8,24},{12,28},{16,0},{20,4},{24,8},{28,12},{1,17},{... | collective-permute-start | bytes 98312 | tf_op jit(solution)/shard_map/ppermute | solution.py:544
  38.3 7.6 %collective-permute-start.15 = (bf16[64,256]{1,0:T(8,128)(2,1)S(1)}, bf16[64,256]{1,0:T(8,128)(2,1)S(1)}, u32[]{:S(2)}, u32[]{:S(2)}) collective-permute-start(bf16[64,256]{1,0:T(8,128)(2,1)S(1)} %add_convert_fusion.g0_ref), channel_id=1, source_target_pairs={{0,8},{4,12},{8,0},{12,4},{16,24},{20,28},{24,16},{28,20},{1,9},{5... | collective-permute-start | bytes 98312 | tf_op jit(solution)/shard_map/ppermute | solution.py:544
  47.0 9.3 %collective-permute-start.16 = (bf16[9,128,128]{2,1,0:T(8,128)(2,1)S(1)}, bf16[9,128,128]{2,1,0:T(8,128)(2,1)S(1)}, u32[]{:S(2)}, u32[]{:S(2)}) collective-permute-start(bf16[9,128,128]{2,1,0:T(8,128)(2,1)S(1)} %get-tuple-element.56.mine_ref), channel_id=1, source_target_pairs={{0,2},{1,3},{2,0},{3,1},{4,6},{5,7},{6,4},{7,5},{8,10},{9,11},{10,... | collective-permute-start | bytes 884744 | tf_op jit(solution)/shard_map/ppermute | solution.py:421
  48.5 2.9 %collective-permute-start.17 = (bf16[512,256]{1,0:T(8,128)(2,1)S(1)}, bf16[512,256]{1,0:T(8,128)(2,1)S(1)}, u32[]{:S(2)}, u32[]{:S(2)}) collective-permute-start(bf16[512,256]{1,0:T(8,128)(2,1)S(1)} %get-tuple-element.57.own_ref), channel_id=1, source_target_pairs={{0,1},{1,0},{2,3},{3,2},{4,5},{5,4},{6,7},{7,6},{8,9},{9,8},{10,11... | collective-permute-start | bytes 786440 | tf_op jit(solution)/shard_map/ppermute | solution.py:418
  48.8 7.5 %collective-permute-start.18 = (f32[128,512]{1,0:T(8,128)S(1)}, f32[128,512]{1,0:T(8,128)S(1)}, u32[]{:S(2)}, u32[]{:S(2)}) collective-permute-start(f32[128,512]{1,0:T(8,128)S(1)} %get-tuple-element.61), channel_id=1, source_target_pairs={{0,1},{1,0},{2,3},{3,2},{4,5},{5,4},{6,7},{7,6},{8,9},{9,8},{10,11... | collective-permute-start | bytes 786440 | tf_op jit(solution)/shard_map/ppermute | solution.py:418
  49.4 6.9 %collective-permute-start.19 = (bf16[128,128]{1,0:T(8,128)(2,1)S(1)}, bf16[128,128]{1,0:T(8,128)(2,1)S(1)}, u32[]{:S(2)}, u32[]{:S(2)}) collective-permute-start(bf16[128,128]{1,0:T(8,128)(2,1)S(1)} %get-tuple-element.62), channel_id=1, source_target_pairs={{0,4},{1,5},{2,6},{3,7},{4,0},{5,1},{6,2},{7,3},{8,12},{9,13},{10,... | collective-permute-start | bytes 98312 | tf_op jit(solution)/shard_map/ppermute | solution.py:509
  51.1 5.2 %collective-permute-start.20 = (bf16[128,128]{1,0:T(8,128)(2,1)S(1)}, bf16[128,128]{1,0:T(8,128)(2,1)S(1)}, u32[]{:S(2)}, u32[]{:S(2)}) collective-permute-start(bf16[128,128]{1,0:T(8,128)(2,1)S(1)} %get-tuple-element.62), channel_id=1, source_target_pairs={{0,6},{1,7},{2,4},{3,5},{4,2},{5,3},{6,0},{7,1},{8,14},{9,15},{10,... | collective-permute-start | bytes 98312 | tf_op jit(solution)/shard_map/ppermute | solution.py:509
  56.4 1.8 %collective-permute-start.21 = (bf16[12,128,128]{2,1,0:T(8,128)(2,1)S(1)}, bf16[12,128,128]{2,1,0:T(8,128)(2,1)S(1)}, u32[]{:S(2)}, u32[]{:S(2)}) collective-permute-start(bf16[12,128,128]{2,1,0:T(8,128)(2,1)S(1)} %total.1.own_ref), channel_id=1, source_target_pairs={{0,1},{1,0},{2,3},{3,2},{4,5},{5,4},{6,7},{7,6},{8,9},{9,8},{10,11... | collective-permute-start | bytes 1179656 | tf_op jit(solution)/shard_map/ppermute | solution.py:418
  (1 other events, 7.8 us)
